TPU v7x, 128 devices: a whole 4x4x4 slice. The times are simulated.
128 devices in a mesh: wide: 16 (over x, z), narrow: 8 (over y, core).
Axes of the slice: x: 4, y: 4, z: 4, core: 2. Of those that a mesh axis runs over, the one named last changes fastest.
Arguments:
- tokens: bfloat16 [16384, 2048], P(('wide', 'narrow')), may hold values from -6 to 6
- lengths: int32 [16, 2], P('wide'), may hold values from 1 to 960, 1024 in all within a row
- picks: int32 [16384, 2], P(('wide', 'narrow')), may hold values from 0 to 3
- cotangent: bfloat16 [16384, 2048], P(('wide', 'narrow'))
- block_master: float32 [2048, 24576], P(('wide', 'narrow'))
- block_first: float32 [2048, 24576], P(('wide', 'narrow')), may hold values from -0.00024414062 to 0.00024414062
- block_second: float32 [2048, 24576], P(('wide', 'narrow')), may hold values from 5.111863e-10 to 8.257626e-09
- gains: float32 [2, 2048], replicated
- gains_first: float32 [2, 2048], replicated, may hold values from -0.00048828125 to 0.00048828125
- gains_second: float32 [2, 2048], replicated, may hold values from 4.915253e-09 to 1.9661012e-08
- router_in: float32 [2048, 256], replicated, may hold values from -0.125 to 0.125
- router_in_first: float32 [2048, 256], replicated, may hold values from -0.00024414062 to 0.00024414062
- router_in_second: float32 [2048, 256], replicated, may hold values from 5.111863e-10 to 8.257626e-09
- router_out: float32 [256, 8], replicated, may hold values from -0.27 to 0.27
- router_out_first: float32 [256, 8], replicated, may hold values from -0.00024414062 to 0.00024414062
- router_out_second: float32 [256, 8], replicated, may hold values from 5.111863e-10 to 8.257626e-09
Outputs:
- output: bfloat16 [16384, 2048], P(('wide', 'narrow'))
- input_grad: float32 [16384, 2048], P(('wide', 'narrow'))
- counts: float32 [2, 4], replicated
- grad_norm: float32 [], replicated
- new_block: float32 [2048, 24576], P(('wide', 'narrow'))
- new_block_first: float32 [2048, 24576], P(('wide', 'narrow'))
- new_block_second: float32 [2048, 24576], P(('wide', 'narrow'))
- block_copy: bfloat16 [2048, 24576], P(('wide', 'narrow'))
- new_gains: float32 [2, 2048], replicated
- new_gains_first: float32 [2, 2048], replicated
- new_gains_second: float32 [2, 2048], replicated
- new_router_in: float32 [2048, 256], replicated
- new_router_in_first: float32 [2048, 256], replicated
- new_router_in_second: float32 [2048, 256], replicated
- new_router_out: float32 [256, 8], replicated
- new_router_out_first: float32 [256, 8], replicated
- new_router_out_second: float32 [256, 8], replicated
Inputs may be any that keep to these rules, and one draw needn't show every extreme that they name: `lengths`: each row sums to 1024.
All inputs are finite; a program needn't handle non-finite values.
Results may differ from a plain program's by a relative error of at most 0.023.
Values may be sent and summed in bfloat16 or wider, within the bound.
A program may use at most 640 MiB of HBM per device.

v0:
```python
import jax
import jax.numpy as jnp
from jax import lax
from jax.sharding import PartitionSpec as P

D = 2048
HEADS = 16
FF = 8192
LEVELS = 4
STEP = 10


NORM_EPS = 1e-05
CLIP_NORM = 1.0
CONTRACT_COLS = (((1,), (1,)), ((), ()))
CONTRACT_ROWS = (((0,), (0,)), ((), ()))


def sent_together(arrays, axis, dim, along):
    ends, at = ([], 0)
    for a in arrays[:-1]:
        at += a.shape[along]
        ends.append(at)
    both = jnp.concatenate(arrays, axis=along)
    return tuple(jnp.split(lax.all_gather(both, axis, axis=dim, tiled=True), ends, axis=along))


def in_one(arrays, axis):
    ends = [0]
    for a in arrays:
        ends.append(ends[-1] + a.size)
    subtotal = lax.psum(jnp.concatenate([a.ravel() for a in arrays]), axis)
    return tuple((subtotal[b:e].reshape(a.shape) for a, b, e in zip(arrays, ends, ends[1:])))


def layer_norm(values, gain_row):
    average = jnp.mean(values, axis=-1, keepdims=True)
    centered = values - average
    spread = jnp.mean(centered * centered, axis=-1, keepdims=True)
    return centered * lax.rsqrt(spread + NORM_EPS) * gain_row


def rotate(values, position):
    halfway = values.shape[-1] // 2
    frequency = 10000.0 ** (-jnp.arange(halfway, dtype=jnp.float32) / halfway)
    angles = position.astype(jnp.float32)[:, None] * frequency[None, :]
    cosine = jnp.cos(angles)[:, None, :]
    sine_part = jnp.sin(angles)[:, None, :]
    first_part = values[..., :halfway]
    second_part = values[..., halfway:]
    return jnp.concatenate(
        [
            first_part * cosine - second_part * sine_part,
            first_part * sine_part + second_part * cosine,
        ],
        axis=-1,
    )


def segment_info(seg_lengths, token_index):
    seg_ends = jnp.cumsum(seg_lengths)
    segment = jnp.sum((token_index[:, None] >= seg_ends[None, :]).astype(jnp.int32), axis=1)
    starts = seg_ends - seg_lengths
    owners = segment[:, None] == jnp.arange(seg_lengths.shape[0], dtype=jnp.int32)[None, :]
    start_of = jnp.sum(jnp.where(owners, starts[None, :], 0), axis=1)
    return (segment, token_index - start_of)


def router_gates(normed, first_layer, second_layer, picks):
    hidden = jax.nn.gelu(jnp.dot(normed, first_layer))
    logits = jnp.dot(hidden, second_layer)
    levels = jnp.arange(LEVELS, dtype=jnp.int32)
    chosen_attn = (picks[:, 0:1] == levels[None, :]).astype(jnp.float32)
    chosen_ffn = (picks[:, 1:2] == levels[None, :]).astype(jnp.float32)
    gate_attn = float(LEVELS) * jnp.sum(
        jax.nn.softmax(logits[:, :LEVELS], axis=-1) * chosen_attn, axis=-1
    )
    gate_ffn = float(LEVELS) * jnp.sum(
        jax.nn.softmax(logits[:, LEVELS:], axis=-1) * chosen_ffn, axis=-1
    )
    return (gate_attn, gate_ffn)


def adamw(weight, moment_one, moment_two, gradient, step_rate):
    moment_one = 0.9 * moment_one + 0.1 * gradient
    moment_two = 0.95 * moment_two + 0.05 * gradient * gradient
    first_hat = moment_one / (1.0 - 0.9**STEP)
    second_hat = moment_two / (1.0 - 0.95**STEP)
    updated = weight - step_rate * (first_hat / (jnp.sqrt(second_hat) + 1e-08) + 0.1 * weight)
    return (updated, moment_one, moment_two)


def slab_columns(weight_rows, part_count):
    row_count = weight_rows.shape[0]
    pieces = []
    for group_number in range(4):
        pieces.append(
            weight_rows[:, group_number * D : (group_number + 1) * D].reshape(
                row_count, part_count, D // part_count
            )
        )
    for group_number in range(2):
        first_column = 4 * D + group_number * FF
        pieces.append(
            weight_rows[:, first_column : first_column + FF].reshape(
                row_count, part_count, FF // part_count
            )
        )
    return jnp.concatenate(pieces, axis=2)


def slab_restore(slab, part_count):
    row_count = slab.shape[0]
    widths_list = [D // part_count] * 4 + [FF // part_count] * 2
    pieces = []
    cursor = 0
    for column_count in widths_list:
        pieces.append(
            slab[:, :, cursor : cursor + column_count].reshape(row_count, part_count * column_count)
        )
        cursor = cursor + column_count
    return jnp.concatenate(pieces, axis=1)


def split_layout(tokens, lengths, picks, cotangent, weights_low, gains, router_in, router_out):
    local_rows, width = tokens.shape
    head_dim = width // HEADS
    score_scale = head_dim ** (-0.5)
    narrow_count = lax.axis_size("narrow")
    wide_count = lax.axis_size("wide")
    rank_number = lax.axis_index("narrow")
    group_rows = local_rows * narrow_count
    offset = rank_number * local_rows
    own_heads = HEADS // narrow_count
    head_part = width // narrow_count
    unit_part = FF // narrow_count
    shard_rows = weights_low.shape[0]
    spread = lax.all_to_all(
        slab_columns(weights_low, narrow_count), "narrow", split_axis=1, concat_axis=0, tiled=True
    )
    slab_width = spread.shape[2]
    slab = lax.all_gather(
        spread.reshape(narrow_count * shard_rows, slab_width), "wide", axis=0, tiled=True
    )
    w_qkv = slab[:, : 3 * head_part]
    w_out = slab[:, 3 * head_part : 4 * head_part]
    w_up = slab[:, 4 * head_part : 4 * head_part + unit_part]
    w_down = slab[:, 4 * head_part + unit_part :]
    group_tokens, group_cotangent, group_pick_low = sent_together(
        (tokens, cotangent, picks.astype(jnp.bfloat16)), "narrow", 0, 1
    )
    group_inputs = group_tokens.astype(jnp.float32)
    group_upstream = group_cotangent.astype(jnp.float32)
    group_picks = group_pick_low.astype(jnp.int32)

    def own_rows(values):
        return lax.dynamic_slice_in_dim(values, offset, local_rows, 0)

    key_index = jnp.arange(group_rows, dtype=jnp.int32)
    key_segment, key_position = segment_info(lengths[0], key_index)
    allowed = (key_segment[:, None] == key_segment[None, :]) & (
        key_index[None, :] <= key_index[:, None]
    )
    normed_low = layer_norm(group_inputs, gains[0]).astype(jnp.bfloat16)
    normed_round = normed_low.astype(jnp.float32)
    gate_attn, gate_ffn = router_gates(normed_round, router_in, router_out, group_picks)
    projected = jnp.dot(normed_low, w_qkv, preferred_element_type=jnp.float32)
    query_raw = projected[:, :head_part].reshape(group_rows, own_heads, head_dim)
    key_raw = projected[:, head_part : 2 * head_part].reshape(group_rows, own_heads, head_dim)
    rotated, rotate_back = jax.vjp(lambda values: rotate(values, key_position), query_raw)
    query_low = rotated.astype(jnp.bfloat16)
    key_low = rotate(key_raw, key_position).astype(jnp.bfloat16)
    value_low = (
        projected[:, 2 * head_part :].reshape(group_rows, own_heads, head_dim).astype(jnp.bfloat16)
    )
    scores = (
        jnp.einsum("qhd,khd->hqk", query_low, key_low, preferred_element_type=jnp.float32)
        * score_scale
    )
    scores = jnp.where(allowed[None], scores, -1e30)
    top_score = jnp.max(scores, axis=-1, keepdims=True)
    expo = jnp.exp(scores - top_score)
    probs = expo / jnp.sum(expo, axis=-1, keepdims=True)
    probs_low = probs.astype(jnp.bfloat16)
    attended = jnp.einsum("hqk,khd->qhd", probs_low, value_low, preferred_element_type=jnp.float32)
    head_number = rank_number * own_heads + jnp.arange(own_heads, dtype=jnp.int32)
    head_mask = (head_number[None, :] < HEADS * (group_picks[:, 0:1] + 1) // LEVELS).astype(
        jnp.float32
    )
    mixed_low = (
        (attended * head_mask[:, :, None]).reshape(group_rows, head_part).astype(jnp.bfloat16)
    )
    attn_part = lax.dot_general(mixed_low, w_out, CONTRACT_COLS, preferred_element_type=jnp.float32)
    attn_out = lax.psum(attn_part.astype(jnp.bfloat16), "narrow").astype(jnp.float32)
    after_attn = group_inputs + gate_attn[:, None] * attn_out
    norm_two, norm_two_back = jax.vjp(layer_norm, after_attn, gains[1])
    normed_two_low = norm_two.astype(jnp.bfloat16)
    up_proj = jnp.dot(normed_two_low, w_up, preferred_element_type=jnp.float32)
    unit_number = rank_number * unit_part + jnp.arange(unit_part, dtype=jnp.int32)
    unit_mask = (unit_number[None, :] < FF * (group_picks[:, 1:2] + 1) // LEVELS).astype(
        jnp.float32
    )
    positive = jnp.maximum(up_proj, 0.0)
    activity_low = (positive * positive * unit_mask).astype(jnp.bfloat16)
    ffn_part = lax.dot_general(
        activity_low, w_down, CONTRACT_COLS, preferred_element_type=jnp.float32
    )
    ffn_out = lax.psum(ffn_part.astype(jnp.bfloat16), "narrow").astype(jnp.float32)
    result = own_rows(after_attn + gate_ffn[:, None] * ffn_out).astype(jnp.bfloat16)
    d_gate_ffn = jnp.sum(group_upstream * ffn_out, axis=1)
    d_ffn_low = (group_upstream * gate_ffn[:, None]).astype(jnp.bfloat16)
    d_activity = jnp.dot(d_ffn_low, w_down, preferred_element_type=jnp.float32)
    grad_down = lax.dot_general(
        d_ffn_low, activity_low, CONTRACT_ROWS, preferred_element_type=jnp.float32
    )
    d_up_low = (d_activity * unit_mask * 2.0 * positive).astype(jnp.bfloat16)
    grad_up = lax.dot_general(
        normed_two_low, d_up_low, CONTRACT_ROWS, preferred_element_type=jnp.float32
    )
    d_norm_part = lax.dot_general(d_up_low, w_up, CONTRACT_COLS, preferred_element_type=jnp.float32)
    d_norm_two = lax.psum(d_norm_part.astype(jnp.bfloat16), "narrow").astype(jnp.float32)
    d_after, d_gain_two = norm_two_back(d_norm_two)
    d_after = d_after + group_upstream
    d_gain_two = d_gain_two * (1.0 / narrow_count)
    d_gate_attn = jnp.sum(d_after * attn_out, axis=1)
    d_attn_low = (d_after * gate_attn[:, None]).astype(jnp.bfloat16)
    grad_out = lax.dot_general(
        d_attn_low, mixed_low, CONTRACT_ROWS, preferred_element_type=jnp.float32
    )
    d_mixed = jnp.dot(d_attn_low, w_out, preferred_element_type=jnp.float32)
    d_attended = (d_mixed.reshape(group_rows, own_heads, head_dim) * head_mask[:, :, None]).astype(
        jnp.bfloat16
    )
    d_probs = jnp.einsum("qhd,khd->hqk", d_attended, value_low, preferred_element_type=jnp.float32)
    centre = jnp.sum(probs * d_probs, axis=-1, keepdims=True)
    d_scores = (probs * (d_probs - centre)).astype(jnp.bfloat16)
    d_query = (
        jnp.einsum("hqk,khd->qhd", d_scores, key_low, preferred_element_type=jnp.float32)
        * score_scale
    )
    d_key = (
        jnp.einsum("hqk,qhd->khd", d_scores, query_low, preferred_element_type=jnp.float32)
        * score_scale
    )
    d_value = jnp.einsum("hqk,qhd->khd", probs_low, d_attended, preferred_element_type=jnp.float32)
    d_query_raw = rotate_back(d_query)[0].reshape(group_rows, head_part)
    d_key_raw = rotate_back(d_key)[0].reshape(group_rows, head_part)
    d_proj_low = jnp.concatenate(
        [d_query_raw, d_key_raw, d_value.reshape(group_rows, head_part)], axis=1
    ).astype(jnp.bfloat16)
    grad_qkv = lax.dot_general(
        normed_low, d_proj_low, CONTRACT_ROWS, preferred_element_type=jnp.float32
    )
    d_normed_part = lax.dot_general(
        d_proj_low, w_qkv, CONTRACT_COLS, preferred_element_type=jnp.float32
    )
    d_normed = lax.psum_scatter(
        d_normed_part.astype(jnp.bfloat16), "narrow", scatter_dimension=0, tiled=True
    ).astype(jnp.float32)
    own_gates, router_back = jax.vjp(
        lambda normed, first_layer, second_layer: router_gates(
            normed, first_layer, second_layer, picks
        ),
        own_rows(normed_round),
        router_in,
        router_out,
    )
    d_normed_router, grad_router_in, grad_router_out = router_back(
        (own_rows(d_gate_attn), own_rows(d_gate_ffn))
    )
    inputs = tokens.astype(jnp.float32)
    norm_one_own, norm_one_back = jax.vjp(layer_norm, inputs, gains[0])
    d_inputs, d_gain_one = norm_one_back(d_normed + d_normed_router)
    d_inputs = d_inputs + own_rows(d_after)
    slab_grad = jnp.concatenate([grad_qkv, grad_out, grad_up, grad_down], axis=1)
    returned = lax.all_to_all(
        lax.all_to_all(
            slab_grad.reshape(wide_count, narrow_count, shard_rows, slab_width).astype(
                jnp.bfloat16
            ),
            "wide",
            split_axis=0,
            concat_axis=2,
            tiled=True,
        ),
        "narrow",
        split_axis=1,
        concat_axis=3,
        tiled=True,
    ).astype(jnp.float32)
    summed = jnp.sum(returned.reshape(wide_count, shard_rows, narrow_count * slab_width), axis=0)
    block_grad = slab_restore(summed.reshape(shard_rows, narrow_count, slab_width), narrow_count)
    return (
        result,
        d_inputs,
        block_grad,
        grad_router_in,
        grad_router_out,
        jnp.stack([d_gain_one, d_gain_two]),
    )


def on_device(
    tokens,
    lengths,
    picks,
    cotangent,
    block_master,
    block_first,
    block_second,
    gains,
    gains_first,
    gains_second,
    router_in,
    router_in_first,
    router_in_second,
    router_out,
    router_out_first,
    router_out_second,
):
    weights_low = block_master.astype(jnp.bfloat16)
    result, d_inputs, block_grad, grad_router_in, grad_router_out, gain_local = split_layout(
        tokens, lengths, picks, cotangent, weights_low, gains, router_in, router_out
    )
    levels = jnp.arange(LEVELS, dtype=jnp.int32)
    counts_local = jnp.stack(
        [
            jnp.sum((picks[:, 0:1] == levels[None, :]).astype(jnp.float32), axis=0),
            jnp.sum((picks[:, 1:2] == levels[None, :]).astype(jnp.float32), axis=0),
        ]
    )
    local_squares = jnp.sum(block_grad * block_grad)
    router_in_grad, router_out_grad, gain_grad, counts, squares = in_one(
        (grad_router_in, grad_router_out, gain_local, counts_local, local_squares),
        ("wide", "narrow"),
    )
    total = (
        squares
        + jnp.sum(gain_grad * gain_grad)
        + jnp.sum(router_in_grad * router_in_grad)
        + jnp.sum(router_out_grad * router_out_grad)
    )
    grad_norm = jnp.sqrt(total)
    clip_factor = jnp.minimum(1.0, CLIP_NORM / grad_norm)
    new_block, new_block_first, new_block_second = adamw(
        block_master, block_first, block_second, block_grad * clip_factor, 0.02
    )
    new_gains, new_gains_first, new_gains_second = adamw(
        gains, gains_first, gains_second, gain_grad * clip_factor, 0.6
    )
    new_router_in, new_router_in_first, new_router_in_second = adamw(
        router_in, router_in_first, router_in_second, router_in_grad * clip_factor, 0.02
    )
    new_router_out, new_router_out_first, new_router_out_second = adamw(
        router_out, router_out_first, router_out_second, router_out_grad * clip_factor, 0.02
    )
    return (
        result,
        d_inputs,
        counts,
        grad_norm,
        new_block,
        new_block_first,
        new_block_second,
        new_block.astype(jnp.bfloat16),
        new_gains,
        new_gains_first,
        new_gains_second,
        new_router_in,
        new_router_in_first,
        new_router_in_second,
        new_router_out,
        new_router_out_first,
        new_router_out_second,
    )


def solution(mesh):
    placed = (
        P(("wide", "narrow"), None),
        P("wide", None),
        P(("wide", "narrow"), None),
        P(("wide", "narrow"), None),
        P(("wide", "narrow"), None),
        P(("wide", "narrow"), None),
        P(("wide", "narrow"), None),
        P(),
        P(),
        P(),
        P(),
        P(),
        P(),
        P(),
        P(),
        P(),
    )
    return jax.shard_map(
        on_device,
        mesh=mesh,
        in_specs=placed,
        out_specs=(
            P(("wide", "narrow"), None),
            P(("wide", "narrow"), None),
            P(),
            P(),
            P(("wide", "narrow"), None),
            P(("wide", "narrow"), None),
            P(("wide", "narrow"), None),
            P(("wide", "narrow"), None),
            P(),
            P(),
            P(),
            P(),
            P(),
            P(),
            P(),
            P(),
            P(),
        ),
        check_vma=False,
    )
```

profile of v0, /device:TPU:1, one launch (start us, length us, event | category | flops | bytes accessed | tf_op | source)
XLA Modules:
  0.0 1102.2 jit_solution(18318400163526238643)
XLA Ops:
  8.2 2.3 pad_maximum_fusion.2
  11.7 19.4 %all_to_all.42 = bf16[16,8,3072]{2,0,1:T(8,128)(2,1)} all-to-all(bf16[16,8,3072]{2,0,1:T(8,128)(2,1)S(1)} %copy.190), channel_id=1, replica_groups=mesh['wide'=16,'narrow'=8] {'narrow'}, dimensions={1} | all-to-all | bytes 1572864 | tf_op jit(solution)/shard_map/all_to_all | solution.py:138
  31.6 1.9 multiply_cosine_fusion
  33.5 1.6 fusion.20
  35.1 31.6 %all-gather.3.cloned.1.call-done = bf16[1024,4098]{1,0:T(8,128)(2,1)} async-done(((bf16[128,4098]{1,0:T(8,128)(2,1)}), bf16[1024,4098]{1,0:T(8,128)(2,1)}) %all-gather.3.cloned.1.call-update) | async-done | bytes 8392720 | tf_op jit(solution)/shard_map/all_gather | solution.py:25
  66.7 2.8 convert_reduce_fusion
  69.5 3.3 fusion.5
  74.9 4.3 fusion.7
  79.2 79.9 %all-gather.5.cloned.1.call-done = bf16[2048,3072]{1,0:T(8,128)(2,1)} async-done(((bf16[128,3072]{1,0:T(8,128)(2,1)}), bf16[2048,3072]{1,0:T(8,128)(2,1)}) %all-gather.5.cloned.1.call-update) | async-done | bytes 12582928 | tf_op jit(solution)/shard_map/all_gather | solution.py:142
  159.2 6.2 fusion.29
  168.7 1.4 copy.228
  170.0 2.4 copy.227
  172.4 2.4 copy.229
  174.8 3.2 subtract_convert_fusion.1
  178.0 8.8 fusion.159
  186.8 4.2 fusion.54
  191.8 4.4 convolution_convert_fusion
  197.8 3.8 fusion.71
  201.8 65.0 %all-reduce.11.cloned.1.call-done = bf16[1024,2048]{1,0:T(8,128)(2,1)} async-done(((bf16[1024,2048]{1,0:T(8,128)(2,1)}), bf16[1024,2048]{1,0:T(8,128)(2,1)}) %all-reduce.11.cloned.1.call-update) | async-done | bytes 4194320 | tf_op jit(solution)/shard_map/psum | solution.py:194
  266.8 4.5 fusion.150
  272.3 3.2 copy-done
  277.1 4.5 fusion.26
  281.7 6.4 convolution_convert_fusion.5
  288.1 7.0 fusion.17
  295.1 6.5 convolution_convert_fusion.4
  301.7 8.5 convolution_convert_fusion.3
  310.2 6.9 convolution_convert_fusion.2
  317.1 90.3 %all-reduce.15.cloned.1.call-done = (bf16[1024,2048]{1,0:T(8,128)(2,1)}, bf16[1024,2048]{1,0:T(8,128)(2,1)}) async-done(((bf16[1024,2048]{1,0:T(8,128)(2,1)}, bf16[1024,2048]{1,0:T(8,128)(2,1)}), (bf16[1024,2048]{1,0:T(8,128)(2,1)}, bf16[1024,2048]{1,0:T(8,128)(2,1)})) %all-reduce.15.cloned.1.call-update) | async-done | bytes 8388624 | tf_op jit(solution)/shard_map/psum | solution.py:208
  407.3 5.7 fusion.8
  413.1 6.8 fusion.10
  420.0 9.3 fusion.9
  429.3 3.1 convolution_convert_fusion.7
  433.6 3.0 fusion.73
  436.6 1.5 fusion.51
  438.2 1.6 multiply_reduce_fusion
  439.8 2.9 multiply_convert_fusion
  444.1 2.0 fusion.46
  448.1 7.3 convolution_convert_fusion.6
  455.5 27.4 %pad_maximum_fusion = bf16[2048,3072]{0,1:T(8,128)(2,1)} fusion(bf16[2048,1024]{0,1:T(8,128)(2,1)S(1)} %copy-done.16, bf16[2048,1024]{0,1:T(8,128)(2,1)S(1)} %copy-done.15, bf16[2048,256]{0,1:T(8,128)(2,1)S(1)} %convolution_convert_fusion.7, bf16[2048,768]{0,1:T(8,128)(2,1)S(1)} %convolution_convert_fusion.6), kind=kLoop, calls=%fused_computation.2 | loop fusion | flops 50331648 | bytes 25165824 | tf_op jit(solution)/shard_map/concatenate | solution.py:275
  482.8 16.7 %copy.208 = bf16[2048,3072]{1,0:T(8,128)(2,1)} copy(bf16[2048,3072]{0,1:T(8,128)(2,1)} %pad_maximum_fusion) | data formatting | bytes 25165824 | tf_op jit(solution)/shard_map/concatenate | solution.py:275
  499.5 144.9 %all_to_all.43 = bf16[16,8,16,3072]{3,2,1,0:T(8,128)(2,1)S(1)} all-to-all(bf16[16,8,16,3072]{3,2,1,0:T(8,128)(2,1)} %bitcast.117), channel_id=1, replica_groups=mesh['wide'=16,'narrow'=8] {'wide'}, dimensions={0} | all-to-all | bytes 25165824 | tf_op jit(solution)/shard_map/all_to_all | solution.py:277
  644.4 5.3 copy.209
  649.7 8.7 all-to-all-start.2
  658.4 7.1 convolution_convert_fusion.1
  669.1 6.4 convert_element_type.158
  677.1 1.5 convolution_bitcast_fusion
  678.7 2.4 copy.236
  681.1 59.4 %reduce-scatter.2.cloned.1.call-done = bf16[128,2048]{1,0:T(8,128)(2,1)} async-done(((bf16[1024,2048]{1,0:T(8,128)(2,1)}), bf16[128,2048]{1,0:T(8,128)(2,1)}) %reduce-scatter.2.cloned.1.call-update) | async-done | bytes 524304 | tf_op jit(solution)/shard_map/reduce_scatter | solution.py:257
  740.5 1.7 fusion.59
  743.7 73.1 %all-to-all-done.2 = bf16[1,8,256,3072]{3,2,0,1:T(8,128)(2,1)} async-done(((bf16[1,8,256,3072]{3,2,0,1:T(8,128)(2,1)}), bf16[1,8,256,3072]{3,2,0,1:T(8,128)(2,1)}, u32[]{:S(2)}, u32[]{:S(2)}) %all-to-all-start.2) | async-done | bytes 12582944 | tf_op jit(solution)/shard_map/all_to_all | solution.py:276
  816.8 7.1 convert_bitcast_fusion
  824.0 30.0 %copy.211 = f32[1,1,256,8,3072]{4,3,2,1,0:T(8,128)} copy(f32[1,1,256,8,3072]{4,2,3,1,0:T(8,128)S(1)} %convert_bitcast_fusion) | data formatting | bytes 50331648 | tf_op jit(solution)/shard_map/convert_element_type | solution.py:290
  854.0 23.4 %reshape.433 = f32[16,16,24576]{2,1,0:T(8,128)} reshape(f32[1,1,256,8,3072]{4,3,2,1,0:T(8,128)} %copy.211) | data formatting | bytes 50331648 | tf_op jit(solution)/shard_map/convert_element_type | solution.py:290
  877.4 10.2 reduce_sum.357
  887.6 2.3 copy.238
  893.2 19.6 %concatenate.35 = f32[530441]{0:T(1024)} concatenate(f32[524288]{0:T(1024)} %bitcast.121, f32[2048]{0:T(1024)S(1)} %reshape.419, f32[4096]{0:T(1024)S(1)} %bitcast.172, f32[8]{0:T(128)S(1)} %reshape.422, f32[1]{0:T(128)} %bitcast.34), dimensions={0} | concatenate | bytes 4243528 | tf_op jit(solution)/shard_map/concatenate | solution.py:32
  912.8 2.5 fusion.70
  915.3 2.9 dynamic-slice_add_fusion.1
  918.2 146.2 %all-reduce.13.cloned.1.call-done = f32[530441]{0:T(1024)} async-done(((f32[530441]{0:T(1024)}), f32[530441]{0:T(1024)}) %all-reduce.13.cloned.1.call-update) | async-done | bytes 2121780 | tf_op jit(solution)/shard_map/psum | solution.py:32
  1068.3 2.7 multiply_reduce_fusion.2
  1075.0 3.0 slice_multiply_fusion
  1078.1 3.0 mul.867
  1082.8 6.2 fusion.148
  1090.3 3.7 multiply_subtract_fusion
  (230 shorter events, 35.6 us)
Async XLA Ops:
  7.2 3.3 copy-start.9
  7.2 59.5 %all-gather.3.cloned.1.call-start = ((), (), s32[]{:S(2)}) async-start(), calls=%async_computation.4 | async-start | bytes 9732096 | tf_op jit(solution)/shard_map/all_gather | solution.py:25
  10.5 148.7 %all-gather.5.cloned.1.call-start = ((), (), s32[]{:S(2)}) async-start(), calls=%async_computation.5 | async-start | bytes 13369344 | tf_op jit(solution)/shard_map/all_gather | solution.py:142
  10.6 20.6 %copy-start.42 = (s32[1,2]{1,0:T(1,128)S(1)}, s32[1,2]{1,0:T(1,128)}, u32[]{:S(2)}) copy-start(s32[1,2]{1,0:T(1,128)} %param.17) | copy-start | bytes 28
  11.0 24.0 %copy-start.28 = (f32[2,2048]{1,0:T(2,128)S(1)}, f32[2,2048]{1,0:T(2,128)}, u32[]{:S(2)}) copy-start(f32[2,2048]{1,0:T(2,128)} %param.23) | copy-start | bytes 49156
  31.1 235.6 %all-reduce.11.cloned.1.call-start = ((), (), s32[]{:S(2)}) async-start(), calls=%async_computation.6 | async-start | bytes 8388608 | tf_op jit(solution)/shard_map/psum | solution.py:194
  33.5 141.3 %copy-start.10 = (f32[1024,64]{1,0:T(8,128)}, f32[1024,64]{1,0:T(8,128)S(1)}, u32[]{:S(2)}) copy-start(f32[1024,64]{1,0:T(8,128)S(1)} %get-tuple-element.161) | copy-start | bytes 786436
  33.5 141.3 %copy-start.12 = (f32[1024,64]{1,0:T(8,128)}, f32[1024,64]{1,0:T(8,128)S(1)}, u32[]{:S(2)}) copy-start(f32[1024,64]{1,0:T(8,128)S(1)} %get-tuple-element.162) | copy-start | bytes 786436
  35.1 39.8 %copy-start.26 = (f32[1,2048]{1,0:T(1,128)}, f32[1,2048]{1,0:T(1,128)S(1)}, u32[]{:S(2)}) copy-start(f32[1,2048]{1,0:T(1,128)S(1)} %get-tuple-element.160) | copy-start | bytes 24580
  74.9 111.9 %copy-start.38 = (f32[1024,2]{0,1:T(2,128)}, f32[1024,2]{0,1:T(2,128)S(1)}, u32[]{:S(2)}) copy-start(f32[1024,2]{0,1:T(2,128)S(1)} %compare_convert_fusion) | copy-start | bytes 24580
  178.0 8.8 copy-start.24
  186.8 4.2 copy-start.32
  191.0 0.8 copy-start.17
  196.2 1.6 copy-start.3
  196.2 1.6 copy-start.34
  196.3 211.1 %all-reduce.15.cloned.1.call-start = ((), (), s32[]{:S(2)}) async-start(), calls=%async_computation.9 | async-start | bytes 16777216 | tf_op jit(solution)/shard_map/psum | solution.py:208
  201.7 108.4 %copy-start.40 = (f32[1024]{0:T(1024)}, f32[1024]{0:T(1024)S(1)}, u32[]{:S(2)}) copy-start(f32[1024]{0:T(1024)S(1)} %broadcast_multiply_fusion.1) | copy-start | bytes 12292
  266.8 10.2 slice-start.7
  266.8 10.2 slice-start.8
  271.3 4.3 copy-start
  272.3 4.8 slice-start.9
  277.1 4.5 copy-start.14
  281.7 6.4 copy-start.43
  301.6 8.5 slice-start.2
  301.6 8.5 slice-start.3
  301.6 8.5 slice-start.4
  301.7 8.5 copy-start.44
  407.3 5.8 copy-start.2
  407.3 12.6 %slice-start = ((s8[8388608]{0:T(1024)(128)(4,1)}), s8[4194304]{0:T(1024)(128)(4,1)S(1)}, s32[]{:S(2)}) async-start(s8[8388608]{0:T(1024)(128)(4,1)} %bitcast.112), calls=%async_computation.10 | async-start | bytes 8388608
  413.1 6.8 slice-start.1
  429.3 4.3 copy-start.1
  429.3 7.3 slice-start.5
  433.6 3.0 slice-start.6
  433.6 3.1 copy-start.33
  433.6 3.1 copy-start.39
  436.6 1.5 copy-start.25
  439.8 2.9 copy-start.20
  439.8 2.9 copy-start.21
  442.7 1.4 copy-start.18
  442.7 1.4 copy-start.19
  444.1 2.0 copy-start.11
  444.1 2.0 copy-start.13
  448.1 7.4 copy-start.15
  448.1 7.4 copy-start.16
  649.7 167.2 %all-to-all-start.2 = ((bf16[1,8,256,3072]{3,2,0,1:T(8,128)(2,1)}), bf16[1,8,256,3072]{3,2,0,1:T(8,128)(2,1)}, u32[]{:S(2)}, u32[]{:S(2)}) async-start(bf16[1,8,256,3072]{3,2,0,1:T(8,128)(2,1)} %bitcast.116), calls=%async_computation.3 | async-start | bytes 25165824 | tf_op jit(solution)/shard_map/all_to_all | solution.py:276
  658.4 82.1 %reduce-scatter.2.cloned.1.call-start = ((), (), s32[]{:S(2)}) async-start(), calls=%async_computation.7 | async-start | bytes 4718592 | tf_op jit(solution)/shard_map/reduce_scatter | solution.py:257
  665.5 1.0 copy-start.5
  665.5 1.2 copy-start.41
  665.5 2.0 copy-start.4
  665.5 3.3 copy-start.35
  665.5 398.8 %all-reduce.13.cloned.1.call-start = ((), (), s32[]{:S(2)}) async-start(), calls=%async_computation.8 | async-start | bytes 4251648 | tf_op jit(solution)/shard_map/psum | solution.py:32
  675.5 65.0 %copy-start.27 = (f32[1,2048]{1,0:T(1,128)S(1)}, f32[1,2048]{1,0:T(1,128)}, u32[]{:S(2)}) copy-start(f32[1,2048]{1,0:T(1,128)} %copy-done.26) | copy-start | bytes 24580
  742.2 1.0 copy-start.6
  891.0 1.1 copy-start.8
  1082.7 6.3 copy-start.29
  1082.7 6.3 copy-start.30
  1082.7 6.3 copy-start.31
  1082.7 7.0 copy-start.36
  1082.7 6.9 copy-start.37
  1082.8 7.6 copy-start.7
  1082.8 7.6 copy-start.22
  1082.8 7.5 copy-start.23
Sparse Core Ops, SparseCore 0:
  10.6 56.0 all-gather.2
  68.9 90.2 all-gather.4
  196.4 70.3 all-reduce.10
  301.8 105.5 all-reduce.14
  665.7 74.8 reduce-scatter.1
  912.9 151.4 all-reduce.12
where the time goes:
time: 1110 us; the launch traced here: 1100 us
  waiting for transfers between devices  546 us (49%)
  blocking collectives  164 us (15%)
  other arithmetic  136 us (12%)
  local copies, waits for them, and re-layouts  128 us (12%)
  matrix products  99.4 us (9%)
  between operations  19.3 us (2%)
    psum x1, waiting for transfers between devices, in_one(): subtotal = lax.psum(jnp.concatenate([a.ravel() for a in arrays]), axis)  146 us
    all_to_all x1, blocking collectives, split_layout(): lax.all_to_all(slab_grad.reshape(wide_count, narrow_count, shard_rows, sl...  145 us
    psum x1, waiting for transfers between devices, split_layout(): lax.psum(ffn_part.astype(jnp.bfloat16), 'narrow').astype(jnp.float32)  90.3 us
    all_gather x1, waiting for transfers between devices, split_layout(): lax.all_gather(spread.reshape(narrow_count * shard_rows, slab_width), 'wi...  79.9 us
    all_to_all x1, waiting for transfers between devices, split_layout(): lax.all_to_all(lax.all_to_all(slab_grad.reshape(wide_count, narrow_count,...  73.1 us
    psum x1, waiting for transfers between devices, split_layout(): lax.psum(attn_part.astype(jnp.bfloat16), 'narrow').astype(jnp.float32)  65 us
    reduce_scatter x1, waiting for transfers between devices, split_layout(): lax.psum_scatter(d_normed_part.astype(jnp.bfloat16), 'narrow', scatter_di...  59.4 us
    convert_element_type x2, local copies, waits for them, and re-layouts, split_layout(): returned = lax.all_to_all(lax.all_to_all(slab_grad.reshape(wide_count, na...  53.4 us
  transfers between devices with their start and end apart: 7, of which 7 were waited for; matrix products, arithmetic and copies ran while one was open for 6% of the time, Pallas kernels for 0%

commit v1 on v0

v1 whole, which is shorter than its diff:
```python
import functools

import jax
import jax.numpy as jnp
from jax import lax
from jax.experimental import pallas as pl
from jax.experimental.pallas import tpu as pltpu
from jax.sharding import PartitionSpec as P

D = 2048
HEADS = 16
HEAD_DIM = 128
FF = 8192
RH = 256
LEVELS = 4
STEP = 10
TOK = 128
GROUP = 1024
SIDE = 4
WIDE = 16
NARROW = 8
ROWS = 16

NORM_EPS = 1e-05
CLIP_NORM = 1.0
CONTRACT_COLS = (((1,), (1,)), ((), ()))
CONTRACT_ROWS = (((0,), (0,)), ((), ()))
MESH = pl.DeviceIdType.MESH
BF = jnp.bfloat16
F32 = jnp.float32


def here():
    w = lax.axis_index("wide")
    n = lax.axis_index("narrow")
    return lax.div(w, SIDE), lax.rem(w, SIDE), lax.div(n, 2), lax.rem(n, 2)


def wrap(i):
    return lax.rem(i + 2 * SIDE, SIDE)


def moved(dx=0, dz=0, dy=0, dc=0):
    x, z, y, c = here()
    return (wrap(x + dx) * SIDE + wrap(z + dz), wrap(y + dy) * 2 + lax.rem(c + dc, 2))


NEAR_Y = [dict(dy=1), dict(dy=-1), dict(dc=1)]
NARROW_ALL = [dict(dy=a, dc=b) for a in range(SIDE) for b in range(2) if a or b]
NEAR_XZ = [dict(dx=1), dict(dx=-1), dict(dz=1), dict(dz=-1)]
LINES_XZ = [dict(dx=a) for a in (1, 2, 3)] + [dict(dz=a) for a in (1, 2, 3)]
WIDE_ALL = [dict(dx=a, dz=b) for a in range(SIDE) for b in range(SIDE) if a or b]


def greet(partners):
    barrier = pltpu.get_barrier_semaphore()
    for p in partners:
        pl.semaphore_signal(barrier, inc=1, device_id=moved(**p), device_id_type=MESH)
    pl.semaphore_wait(barrier, len(partners))


def span(start, size):
    if not isinstance(start, int):
        start = pl.multiple_of(start, ROWS)
    return pl.ds(start, size)


class Net:
    def __init__(self, send, recv, local):
        self.send, self.recv, self.local = send, recv, local
        self.used, self.used_local = 0, 0
        self.sent, self.kept = [], []

    def put(self, src, dst, target):
        i = self.used
        self.used += 1
        copy = pltpu.make_async_remote_copy(
            src_ref=src,
            dst_ref=dst,
            send_sem=self.send.at[i],
            recv_sem=self.recv.at[i],
            device_id=target,
            device_id_type=MESH,
        )
        copy.start()
        self.sent.append(copy)
        return copy

    def keep(self, src, dst):
        i = self.used_local
        self.used_local += 1
        copy = pltpu.make_async_copy(src, dst, self.local.at[i])
        copy.start()
        return copy

    def finish(self):
        for copy in self.sent:
            copy.wait_send()


def take_turns(*parts):
    live = list(parts)
    while live:
        still = []
        for part in live:
            try:
                next(part)
                still.append(part)
            except StopIteration:
                pass
        live = still


def comm_call(body, ins, outs, scratch, cid, copies, locals_, name, flops=0):
    n_in, n_out, n_scr = len(ins), len(outs), len(scratch)

    def kernel(*refs):
        in_refs = refs[:n_in]
        out_refs = refs[n_in : n_in + n_out]
        scr = refs[n_in + n_out : n_in + n_out + n_scr]
        send, recv, local = refs[n_in + n_out + n_scr :]
        net = Net(send, recv, local)
        body(net, in_refs, out_refs, scr)
        net.finish()
        assert net.used <= copies and net.used_local <= locals_, (net.used, net.used_local)

    return pl.pallas_call(
        kernel,
        out_shape=outs,
        in_specs=[pl.BlockSpec(memory_space=pl.ANY)] * n_in,
        out_specs=[pl.BlockSpec(memory_space=pl.ANY)] * n_out,
        scratch_shapes=list(scratch)
        + [
            pltpu.SemaphoreType.DMA((copies,)),
            pltpu.SemaphoreType.DMA((copies,)),
            pltpu.SemaphoreType.DMA((max(locals_, 1),)),
        ],
        compiler_params=pltpu.CompilerParams(
            collective_id=cid, has_side_effects=True, vmem_limit_bytes=56 * 2**20
        ),
        name=name,
    )(*ins)


def gather_narrow(net, own, out):
    x, z, y, c = here()
    rows = own.shape[0]
    half = rows // 2

    def block(dy, lo=0, size=rows):
        return out.at[span((wrap(y + dy) * 2 + c) * rows + lo, size)]

    mine = net.keep(own, block(0))
    up = net.put(own, block(0), moved(dy=1))
    down = net.put(own, block(0), moved(dy=-1))
    across = [net.put(own, block(0), moved(dc=1))]
    yield
    up.wait_recv()
    on = net.put(block(-1, 0, half), block(-1, 0, half), moved(dy=1))
    across.append(net.put(block(-1), block(-1), moved(dc=1)))
    yield
    down.wait_recv()
    back = net.put(block(1, half, half), block(1, half, half), moved(dy=-1))
    across.append(net.put(block(1), block(1), moved(dc=1)))
    yield
    on.wait_recv()
    across.append(net.put(block(2, 0, half), block(2, 0, half), moved(dc=1)))
    yield
    back.wait_recv()
    across.append(net.put(block(2, half, half), block(2, half, half), moved(dc=1)))
    yield
    mine.wait()
    for copy in across:
        copy.wait_recv()


GATHER_COPIES = 10


def gather_call(own, cid, name):
    rows, cols = own.shape

    def body(net, ins, outs, scr):
        greet(NEAR_Y)
        take_turns(gather_narrow(net, ins[0], outs[0]))

    return comm_call(
        body,
        [own],
        [jax.ShapeDtypeStruct((NARROW * rows, cols), own.dtype)],
        [],
        cid,
        GATHER_COPIES,
        1,
        name,
    )[0]


def reduce_scratch(rows, cols):
    return [
        pltpu.VMEM((SIDE, rows, cols), BF),
        pltpu.VMEM((SIDE, rows, cols), BF),
        pltpu.VMEM((2, rows // 2, cols), BF),
        pltpu.VMEM((2, rows, cols), BF),
        pltpu.VMEM((3, rows, cols), BF),
        pltpu.VMEM((rows, cols), F32),
    ]


REDUCE_COPIES = 10
REDUCE_LOCALS = 5


def reduce_narrow(net, part, out, scr):
    own, other, through, landed, ready, total = scr
    x, z, y, c = here()
    rows, cols = out.shape
    half = rows // 2

    def block(dy, core):
        return part.at[span((wrap(y + dy) * 2 + core) * rows, rows)]

    order = (2, 1, 3, 0)
    local, cross = {}, {}
    for dy in order:
        cross[dy] = net.put(block(dy, 1 - c), other.at[dy], moved(dc=1))
        local[dy] = net.keep(block(dy, c), own.at[dy])

    def pair(dy, lo, size):
        s = span(lo, size)
        return own[dy, s, :].astype(F32) + other[dy, s, :].astype(F32)

    yield
    local[2].wait()
    cross[2].wait_recv()
    ready[0] = pair(2, 0, rows).astype(BF)
    first, last = span(0, half), span(half, half)
    via_up = net.put(ready.at[0, first], through.at[0], moved(dy=1))
    via_down = net.put(ready.at[0, last], through.at[1], moved(dy=-1))
    yield
    local[1].wait()
    cross[1].wait_recv()
    ready[1, last, :] = pair(1, half, half).astype(BF)
    up_late = net.put(ready.at[1, last], landed.at[0, last], moved(dy=1))
    local[3].wait()
    cross[3].wait_recv()
    ready[2, first, :] = pair(3, 0, half).astype(BF)
    down_first = net.put(ready.at[2, first], landed.at[1, first], moved(dy=-1))
    yield
    via_up.wait_recv()
    ready[1, first, :] = (pair(1, 0, half) + through[0].astype(F32)).astype(BF)
    up_first = net.put(ready.at[1, first], landed.at[0, first], moved(dy=1))
    via_down.wait_recv()
    ready[2, last, :] = (pair(3, half, half) + through[1].astype(F32)).astype(BF)
    down_late = net.put(ready.at[2, last], landed.at[1, last], moved(dy=-1))
    yield
    local[0].wait()
    cross[0].wait_recv()
    total[...] = pair(0, 0, rows)
    yield
    for copy in (up_late, down_first, up_first, down_late):
        copy.wait_recv()
    total[...] += landed[0].astype(F32) + landed[1].astype(F32)
    done = net.keep(total, out)
    yield
    done.wait()


def reduce_call(parts, cid, name):
    n = len(parts)
    shapes = [(p.shape[0] // NARROW, p.shape[1]) for p in parts]
    scratch = [s for shape in shapes for s in reduce_scratch(*shape)]

    def body(net, ins, outs, scr):
        greet(NEAR_Y)
        take_turns(
            *[reduce_narrow(net, ins[i], outs[i], scr[6 * i : 6 * i + 6]) for i in range(n)]
        )

    return comm_call(
        body,
        list(parts),
        [jax.ShapeDtypeStruct(s, F32) for s in shapes],
        scratch,
        cid,
        REDUCE_COPIES * n,
        REDUCE_LOCALS * n,
        name,
    )


def spread_narrow(net, src, slab):
    w = lax.axis_index("wide")
    n = lax.axis_index("narrow")
    base = w * TOK + n * ROWS
    mine = net.keep(src.at[n], slab.at[span(base, ROWS)])
    copies = []
    for p in NARROW_ALL:
        target = moved(**p)
        copies.append(net.put(src.at[target[1]], slab.at[span(base, ROWS)], target))
    yield
    mine.wait()
    for copy in copies:
        copy.wait_recv()


SPREAD_COPIES = 7


def gather_wide(net, slab, lead):
    x, z, y, c = here()
    rows = TOK // 2
    half = rows // 2
    low = 0 if lead == "x" else rows

    def block(a, b, lo=0, size=rows):
        px, pz = (a, b) if lead == "x" else (b, a)
        return slab.at[span((wrap(x + px) * SIDE + wrap(z + pz)) * TOK + low + lo, size)]

    def lead_to(d):
        return moved(dx=d) if lead == "x" else moved(dz=d)

    def then_to(d):
        return moved(dz=d) if lead == "x" else moved(dx=d)

    def both(src, to):
        return net.put(src, src, to(1)), net.put(src, src, to(-1))

    fore, aft = both(block(0, 0), lead_to)
    second = {0: both(block(0, 0), then_to)}
    yield
    fore.wait_recv()
    on = net.put(block(-1, 0, 0, half), block(-1, 0, 0, half), lead_to(1))
    second[-1] = both(block(-1, 0), then_to)
    aft.wait_recv()
    back = net.put(block(1, 0, half, half), block(1, 0, half, half), lead_to(-1))
    second[1] = both(block(1, 0), then_to)
    yield
    last = []

    def relay(a):
        f, b = second[a]
        f.wait_recv()
        last.append(net.put(block(a, -1, 0, half), block(a, -1, 0, half), then_to(1)))
        b.wait_recv()
        last.append(net.put(block(a, 1, half, half), block(a, 1, half, half), then_to(-1)))

    relay(0)
    yield
    on.wait_recv()
    back.wait_recv()
    second[2] = both(block(2, 0), then_to)
    yield
    relay(-1)
    relay(1)
    yield
    relay(2)
    yield
    for copy in last:
        copy.wait_recv()


WIDE_COPIES = 20


def chain(*parts):
    for part in parts:
        yield from part


def first_gather(owns, sources, cid):
    k, m = len(owns), len(sources)

    def body(net, ins, outs, scr):
        greet(NARROW_ALL + NEAR_XZ)

        def weights(i):
            yield from spread_narrow(net, ins[k + i], outs[k + i])
            a = gather_wide(net, outs[k + i], "x")
            b = gather_wide(net, outs[k + i], "z")
            live = [a, b]
            while live:
                for g in list(live):
                    try:
                        next(g)
                    except StopIteration:
                        live.remove(g)
                yield

        take_turns(
            weights(0),
            gather_narrow(net, ins[0], outs[0]),
            *[weights(i) for i in range(1, m)],
            *[gather_narrow(net, ins[i], outs[i]) for i in range(1, k)],
        )

    shapes = [jax.ShapeDtypeStruct((NARROW * o.shape[0], o.shape[1]), o.dtype) for o in owns] + [
        jax.ShapeDtypeStruct((D, s.shape[2]), s.dtype) for s in sources
    ]
    return comm_call(
        body,
        list(owns) + list(sources),
        shapes,
        [],
        cid,
        k * GATHER_COPIES + m * (SPREAD_COPIES + 2 * WIDE_COPIES),
        k + m,
        "first_gather",
    )


def grad_scratch(cols):
    part = TOK // 2
    return [
        pltpu.VMEM((2, SIDE, part, cols), BF),
        pltpu.VMEM((2, 3, SIDE, part, cols), BF),
        pltpu.VMEM((2, SIDE, part, cols), BF),
        pltpu.VMEM((2, 3, part, cols), BF),
        pltpu.VMEM((TOK, cols), BF),
    ]


GRAD_COPIES = 2 * 6 + 7
GRAD_LOCALS = 3


def reduce_wide(net, grad, out, scr, lead):
    own, landed, sums, late, total = scr
    x, z, y, c = here()
    part = TOK // 2
    half = 0 if lead == "x" else 1
    low = half * part
    blocks = grad.reshape(SIDE, SIDE, TOK, grad.shape[1])

    def line(d):
        if lead == "x":
            return blocks.at[wrap(x + d), :, span(low, part), :]
        return blocks.at[:, wrap(z + d), span(low, part), :]

    def lead_to(d):
        return moved(dx=d) if lead == "x" else moved(dz=d)

    def then_to(d):
        return moved(dz=d) if lead == "x" else moved(dx=d)

    mine = net.keep(line(0), own.at[half])
    copies = [net.put(line(d), landed.at[half, d - 1], lead_to(d)) for d in (2, 1, 3)]
    yield
    mine.wait()
    for copy in copies:
        copy.wait_recv()

    @pl.loop(0, SIDE)
    def _(i):
        s = own[half, i].astype(F32)
        for d in range(3):
            s = s + landed[half, d, i].astype(F32)
        sums[half, i] = s.astype(BF)

    me = z if lead == "x" else x
    copies = [net.put(sums.at[half, wrap(me + d)], late.at[half, d - 1], then_to(d)) for d in (2, 1, 3)]
    yield
    for copy in copies:
        copy.wait_recv()
    s = sums[half, me].astype(F32)
    for d in range(3):
        s = s + late[half, d].astype(F32)
    total[span(low, part), :] = s.astype(BF)


def return_narrow(net, total, out):
    n = lax.axis_index("narrow")

    def rows(i):
        return total.at[span(i * ROWS, ROWS)]

    mine = net.keep(rows(n), out.at[n])
    copies = []
    for p in NARROW_ALL:
        target = moved(**p)
        copies.append(net.put(rows(target[1]), out.at[n], target))
    yield
    mine.wait()
    for copy in copies:
        copy.wait_recv()


def reduce_grads(grads, small, cid):
    m = len(grads)
    scratch = [s for g in grads for s in grad_scratch(g.shape[1])]
    scratch += [pltpu.VMEM((WIDE, ROWS, RH), BF), pltpu.VMEM((ROWS, RH), F32)]

    def body(net, ins, outs, scr):
        greet(NARROW_ALL + WIDE_ALL)
        w = lax.axis_index("wide")

        def one(i):
            s = scr[5 * i : 5 * i + 5]
            a = reduce_wide(net, ins[i], outs[i], s, "x")
            b = reduce_wide(net, ins[i], outs[i], s, "z")
            live = [a, b]
            while live:
                for g in list(live):
                    try:
                        next(g)
                    except StopIteration:
                        live.remove(g)
                if live:
                    yield
            yield from return_narrow(net, s[4], outs[i])

        def little():
            landed, total = scr[5 * m :]

            def rows(i):
                return ins[m].at[span(i * ROWS, ROWS)]

            mine = net.keep(rows(w), landed.at[w])
            copies = []
            for p in WIDE_ALL:
                target = moved(**p)
                copies.append(net.put(rows(target[0]), landed.at[w], target))
            yield
            yield
            mine.wait()
            for copy in copies:
                copy.wait_recv()
            s = landed[0].astype(F32)
            for i in range(1, WIDE):
                s = s + landed[i].astype(F32)
            total[...] = s
            done = net.keep(total, outs[m])
            yield
            done.wait()

        take_turns(*[one(i) for i in range(m)], little())

    shapes = [jax.ShapeDtypeStruct((NARROW, ROWS, g.shape[1]), BF) for g in grads]
    shapes.append(jax.ShapeDtypeStruct((ROWS, RH), F32))
    return comm_call(
        body,
        list(grads) + [small],
        shapes,
        scratch,
        cid,
        m * GRAD_COPIES + 15,
        m * GRAD_LOCALS + 2,
        "reduce_grads",
    )


def last_sums(vector, shard, cid):
    rows = vector.shape[0]

    def body(net, ins, outs, scr):
        vec, own = ins
        vec_out, full = outs
        first, mid, second, total = scr
        w = lax.axis_index("wide")
        n = lax.axis_index("narrow")
        greet(NARROW_ALL + WIDE_ALL)

        def sums():
            mine = net.keep(vec, first.at[n])
            copies = [net.put(vec, first.at[n], moved(**p)) for p in NARROW_ALL]
            yield
            mine.wait()
            for copy in copies:
                copy.wait_recv()
            s = first[0]
            for i in range(1, NARROW):
                s = s + first[i]
            mid[...] = s
            mine = net.keep(mid, second.at[w])
            copies = [net.put(mid, second.at[w], moved(**p)) for p in WIDE_ALL]
            yield
            mine.wait()
            for copy in copies:
                copy.wait_recv()
            s = second[0]
            for i in range(1, WIDE):
                s = s + second[i]
            total[...] = s
            done = net.keep(total, vec_out)
            yield
            done.wait()

        def table():
            spot = full.at[span(n * GROUP // 4 + w * ROWS, ROWS)]
            mine = net.keep(own, spot)
            copies = [net.put(own, spot, moved(**p)) for p in WIDE_ALL]
            yield
            mine.wait()
            for copy in copies:
                copy.wait_recv()
            x, z, y, c = here()

            def block(dy):
                return full.at[span((wrap(y + dy) * 2 + c) * RH, RH)]

            along = [net.put(block(0), block(0), moved(dy=d)) for d in (1, 3, 2)]
            across = [net.put(block(0), block(0), moved(dc=1))]
            yield
            for copy, d in zip(along, (1, 3, 2)):
                copy.wait_recv()
                across.append(net.put(block(-d), block(-d), moved(dc=1)))
            yield
            for copy in across:
                copy.wait_recv()

        take_turns(sums(), table())

    return comm_call(
        body,
        [vector, shard],
        [jax.ShapeDtypeStruct((rows, 128), F32), jax.ShapeDtypeStruct((D, RH), F32)],
        [
            pltpu.VMEM((NARROW, rows, 128), F32),
            pltpu.VMEM((rows, 128), F32),
            pltpu.VMEM((WIDE, rows, 128), F32),
            pltpu.VMEM((rows, 128), F32),
        ],
        cid,
        7 + 15 + 15 + 7,
        4,
        "last_sums",
    )


def layer_norm(values, gain_row):
    average = jnp.mean(values, axis=-1, keepdims=True)
    centered = values - average
    spread = jnp.mean(centered * centered, axis=-1, keepdims=True)
    return centered * lax.rsqrt(spread + NORM_EPS) * gain_row


def rotate(values, position):
    halfway = values.shape[-1] // 2
    frequency = 10000.0 ** (-jnp.arange(halfway, dtype=jnp.float32) / halfway)
    angles = position.astype(jnp.float32)[:, None] * frequency[None, :]
    cosine = jnp.cos(angles)[:, None, :]
    sine_part = jnp.sin(angles)[:, None, :]
    first_part = values[..., :halfway]
    second_part = values[..., halfway:]
    return jnp.concatenate(
        [
            first_part * cosine - second_part * sine_part,
            first_part * sine_part + second_part * cosine,
        ],
        axis=-1,
    )


def segment_info(seg_lengths, token_index):
    seg_ends = jnp.cumsum(seg_lengths)
    segment = jnp.sum((token_index[:, None] >= seg_ends[None, :]).astype(jnp.int32), axis=1)
    starts = seg_ends - seg_lengths
    owners = segment[:, None] == jnp.arange(seg_lengths.shape[0], dtype=jnp.int32)[None, :]
    start_of = jnp.sum(jnp.where(owners, starts[None, :], 0), axis=1)
    return (segment, token_index - start_of)


def router_gates(normed, first_layer, second_layer, picks):
    hidden = jax.nn.gelu(jnp.dot(normed, first_layer))
    logits = jnp.dot(hidden, second_layer)
    levels = jnp.arange(LEVELS, dtype=jnp.int32)
    chosen_attn = (picks[:, 0:1] == levels[None, :]).astype(jnp.float32)
    chosen_ffn = (picks[:, 1:2] == levels[None, :]).astype(jnp.float32)
    gate_attn = float(LEVELS) * jnp.sum(
        jax.nn.softmax(logits[:, :LEVELS], axis=-1) * chosen_attn, axis=-1
    )
    gate_ffn = float(LEVELS) * jnp.sum(
        jax.nn.softmax(logits[:, LEVELS:], axis=-1) * chosen_ffn, axis=-1
    )
    return (gate_attn, gate_ffn)


def adamw(weight, moment_one, moment_two, gradient, step_rate):
    moment_one = 0.9 * moment_one + 0.1 * gradient
    moment_two = 0.95 * moment_two + 0.05 * gradient * gradient
    first_hat = moment_one / (1.0 - 0.9**STEP)
    second_hat = moment_two / (1.0 - 0.95**STEP)
    updated = weight - step_rate * (first_hat / (jnp.sqrt(second_hat) + 1e-08) + 0.1 * weight)
    return (updated, moment_one, moment_two)


def cut(rows, start, width, pieces):
    part = rows[:, start : start + width].reshape(rows.shape[0], pieces, width // pieces)
    return part.transpose(1, 0, 2)


def joined(part):
    return part.transpose(1, 0, 2).reshape(ROWS, -1)


def on_device(
    tokens,
    lengths,
    picks,
    cotangent,
    block_master,
    block_first,
    block_second,
    gains,
    gains_first,
    gains_second,
    router_in,
    router_in_first,
    router_in_second,
    router_out,
    router_out_first,
    router_out_second,
):
    score_scale = HEAD_DIM ** (-0.5)
    rank_number = lax.axis_index("narrow")
    own_heads = HEADS // NARROW
    head_part = D // NARROW
    unit_part = FF // NARROW

    low = block_master.astype(BF)
    source_a = jnp.concatenate([cut(low, i * D, D, NARROW) for i in range(4)], axis=2)
    source_b = jnp.concatenate([cut(low, 4 * D + i * FF, FF, NARROW) for i in range(2)], axis=2)
    inputs = tokens.astype(F32)
    norm_one, norm_one_back = jax.vjp(layer_norm, inputs, gains[0])
    normed_own = norm_one.astype(BF)
    (gate_attn, gate_ffn), router_back = jax.vjp(
        lambda normed, first_layer, second_layer: router_gates(
            normed, first_layer, second_layer, picks
        ),
        normed_own.astype(F32),
        router_in,
        router_out,
    )
    upstream = cotangent.astype(F32)
    d_ffn_own = (upstream * gate_ffn[:, None]).astype(BF)
    marks = jnp.where(jnp.arange(128)[None, :] < 64, picks[:, 0:1], picks[:, 1:2]).astype(BF)

    normed_low, d_ffn_low, group_marks, slab_a, slab_b = first_gather(
        [normed_own, d_ffn_own, marks], [source_a, source_b], 0
    )
    w_qkv, w_out = slab_a[:, : 3 * head_part], slab_a[:, 3 * head_part :]
    w_up, w_down = slab_b[:, :unit_part], slab_b[:, unit_part:]
    picks_attn = group_marks[:, 0:1].astype(jnp.int32)
    picks_ffn = group_marks[:, 64:65].astype(jnp.int32)

    key_index = jnp.arange(GROUP, dtype=jnp.int32)
    key_segment, key_position = segment_info(lengths[0], key_index)
    allowed = (key_segment[:, None] == key_segment[None, :]) & (
        key_index[None, :] <= key_index[:, None]
    )
    projected = jnp.dot(normed_low, w_qkv, preferred_element_type=F32)
    query_raw = projected[:, :head_part].reshape(GROUP, own_heads, HEAD_DIM)
    key_raw = projected[:, head_part : 2 * head_part].reshape(GROUP, own_heads, HEAD_DIM)
    rotated, rotate_back = jax.vjp(lambda values: rotate(values, key_position), query_raw)
    query_low = rotated.astype(BF)
    key_low = rotate(key_raw, key_position).astype(BF)
    value_low = projected[:, 2 * head_part :].reshape(GROUP, own_heads, HEAD_DIM).astype(BF)
    scores = (
        jnp.einsum("qhd,khd->hqk", query_low, key_low, preferred_element_type=F32) * score_scale
    )
    scores = jnp.where(allowed[None], scores, -1e30)
    top_score = jnp.max(scores, axis=-1, keepdims=True)
    expo = jnp.exp(scores - top_score)
    probs = expo / jnp.sum(expo, axis=-1, keepdims=True)
    probs_low = probs.astype(BF)
    attended = jnp.einsum("hqk,khd->qhd", probs_low, value_low, preferred_element_type=F32)
    head_number = rank_number * own_heads + jnp.arange(own_heads, dtype=jnp.int32)
    head_mask = (head_number[None, :] < HEADS * (picks_attn + 1) // LEVELS).astype(F32)
    mixed_low = (attended * head_mask[:, :, None]).reshape(GROUP, head_part).astype(BF)
    attn_part = lax.dot_general(mixed_low, w_out, CONTRACT_COLS, preferred_element_type=F32)
    (attn_out,) = reduce_call([attn_part.astype(BF)], 1, "sum_attention")

    after_attn = inputs + gate_attn[:, None] * attn_out
    norm_two, norm_two_back = jax.vjp(layer_norm, after_attn, gains[1])
    normed_two_low = gather_call(norm_two.astype(BF), 2, "gather_normed")

    up_proj = jnp.dot(normed_two_low, w_up, preferred_element_type=F32)
    unit_number = rank_number * unit_part + jnp.arange(unit_part, dtype=jnp.int32)
    unit_mask = (unit_number[None, :] < FF * (picks_ffn + 1) // LEVELS).astype(F32)
    positive = jnp.maximum(up_proj, 0.0)
    activity_low = (positive * positive * unit_mask).astype(BF)
    ffn_part = lax.dot_general(activity_low, w_down, CONTRACT_COLS, preferred_element_type=F32)
    d_activity = jnp.dot(d_ffn_low, w_down, preferred_element_type=F32)
    d_up_low = (d_activity * unit_mask * 2.0 * positive).astype(BF)
    d_norm_part = lax.dot_general(d_up_low, w_up, CONTRACT_COLS, preferred_element_type=F32)
    grad_down = lax.dot_general(
        d_ffn_low, activity_low, CONTRACT_ROWS, preferred_element_type=F32
    ).astype(BF)
    grad_up = lax.dot_general(
        normed_two_low, d_up_low, CONTRACT_ROWS, preferred_element_type=F32
    ).astype(BF)
    d_norm_two, ffn_out = reduce_call(
        [d_norm_part.astype(BF), ffn_part.astype(BF)], 3, "sum_ffn"
    )

    result = (after_attn + gate_ffn[:, None] * ffn_out).astype(BF)
    d_gate_ffn = jnp.sum(upstream * ffn_out, axis=1)
    d_after, d_gain_two = norm_two_back(d_norm_two)
    d_after = d_after + upstream
    d_gate_attn = jnp.sum(d_after * attn_out, axis=1)
    d_attn_low = gather_call((d_after * gate_attn[:, None]).astype(BF), 4, "gather_dattn")

    grad_out = lax.dot_general(
        d_attn_low, mixed_low, CONTRACT_ROWS, preferred_element_type=F32
    ).astype(BF)
    d_mixed = jnp.dot(d_attn_low, w_out, preferred_element_type=F32)
    d_attended = (d_mixed.reshape(GROUP, own_heads, HEAD_DIM) * head_mask[:, :, None]).astype(BF)
    d_probs = jnp.einsum("qhd,khd->hqk", d_attended, value_low, preferred_element_type=F32)
    centre = jnp.sum(probs * d_probs, axis=-1, keepdims=True)
    d_scores = (probs * (d_probs - centre)).astype(BF)
    d_query = (
        jnp.einsum("hqk,khd->qhd", d_scores, key_low, preferred_element_type=F32) * score_scale
    )
    d_key = (
        jnp.einsum("hqk,qhd->khd", d_scores, query_low, preferred_element_type=F32) * score_scale
    )
    d_value = jnp.einsum("hqk,qhd->khd", probs_low, d_attended, preferred_element_type=F32)
    d_query_raw = rotate_back(d_query)[0].reshape(GROUP, head_part)
    d_key_raw = rotate_back(d_key)[0].reshape(GROUP, head_part)
    d_proj_low = jnp.concatenate(
        [d_query_raw, d_key_raw, d_value.reshape(GROUP, head_part)], axis=1
    ).astype(BF)
    grad_qkv = lax.dot_general(
        normed_low, d_proj_low, CONTRACT_ROWS, preferred_element_type=F32
    ).astype(BF)
    d_normed_part = lax.dot_general(d_proj_low, w_qkv, CONTRACT_COLS, preferred_element_type=F32)
    d_normed_router, grad_router_in, grad_router_out = router_back((d_gate_attn, d_gate_ffn))
    d_normed, router_in_part = reduce_call(
        [d_normed_part.astype(BF), grad_router_in.astype(BF)], 5, "sum_dnormed"
    )
    d_inputs, d_gain_one = norm_one_back(d_normed + d_normed_router)
    d_inputs = d_inputs + d_after

    sum_qkv, sum_out, sum_up, sum_down, router_in_shard = reduce_grads(
        [grad_qkv, grad_out, grad_up, grad_down], router_in_part.astype(BF), 6
    )
    block_grad = jnp.concatenate(
        [joined(sum_qkv[:, :, i * head_part : (i + 1) * head_part]) for i in range(3)]
        + [joined(sum_out), joined(sum_up), joined(sum_down)],
        axis=1,
    ).astype(F32)

    levels = jnp.arange(LEVELS, dtype=jnp.int32)
    counts_local = jnp.concatenate(
        [
            jnp.sum((picks[:, 0:1] == levels[None, :]).astype(F32), axis=0),
            jnp.sum((picks[:, 1:2] == levels[None, :]).astype(F32), axis=0),
        ]
    )
    local_squares = jnp.sum(block_grad * block_grad) + jnp.sum(router_in_shard * router_in_shard)
    pieces = [
        d_gain_one,
        d_gain_two,
        grad_router_out.ravel(),
        counts_local,
        local_squares[None],
    ]
    size = sum(p.shape[0] for p in pieces)
    padded = -(-size // 1024) * 1024
    vector = jnp.concatenate(pieces + [jnp.zeros((padded - size,), F32)]).reshape(-1, 128)
    vector, router_in_grad = last_sums(vector, router_in_shard, 7)
    flat = vector.ravel()
    gain_grad = flat[: 2 * D].reshape(2, D)
    router_out_grad = flat[2 * D : 2 * D + RH * 8].reshape(RH, 8)
    at = 2 * D + RH * 8
    counts = flat[at : at + 8].reshape(2, LEVELS)
    squares = flat[at + 8]

    total = squares + jnp.sum(gain_grad * gain_grad) + jnp.sum(router_out_grad * router_out_grad)
    grad_norm = jnp.sqrt(total)
    clip_factor = jnp.minimum(1.0, CLIP_NORM / grad_norm)
    new_block, new_block_first, new_block_second = adamw(
        block_master, block_first, block_second, block_grad * clip_factor, 0.02
    )
    new_gains, new_gains_first, new_gains_second = adamw(
        gains, gains_first, gains_second, gain_grad * clip_factor, 0.6
    )
    new_router_in, new_router_in_first, new_router_in_second = adamw(
        router_in, router_in_first, router_in_second, router_in_grad * clip_factor, 0.02
    )
    new_router_out, new_router_out_first, new_router_out_second = adamw(
        router_out, router_out_first, router_out_second, router_out_grad * clip_factor, 0.02
    )
    return (
        result,
        d_inputs,
        counts,
        grad_norm,
        new_block,
        new_block_first,
        new_block_second,
        new_block.astype(BF),
        new_gains,
        new_gains_first,
        new_gains_second,
        new_router_in,
        new_router_in_first,
        new_router_in_second,
        new_router_out,
        new_router_out_first,
        new_router_out_second,
    )


def solution(mesh):
    both = P(("wide", "narrow"), None)
    return jax.shard_map(
        on_device,
        mesh=mesh,
        in_specs=(both, P("wide", None)) + (both,) * 5 + (P(),) * 9,
        out_specs=(both, both, P(), P()) + (both,) * 4 + (P(),) * 9,
        check_vma=False,
    )
```

time: 1110 us -> 557 us (0.50)
  waiting for transfers between devices: 546 us -> 0 us
  Pallas kernels: 0 us -> 360 us
  blocking collectives: 164 us -> 0 us
  local copies, waits for them, and re-layouts: 128 us -> 27.2 us
  other arithmetic: 136 us -> 54 us
  between operations: 19.3 us -> 6.81 us
    pallas_call x0 -> x8, Pallas kernels: none -> 360 us  [comm_call(): pl.pallas_call(kernel, out_shape=outs, in_specs=[pl.BlockSpec(memory_spac...]
    psum x3 -> x0, waiting for transfers between devices: 301 us -> none  [the longest x1 146 us: in_one(): subtotal = lax.psum(jnp.concatenate([a.ravel() for a in arrays]), axis)]
    all_to_all x2 -> x0, blocking collectives: 164 us -> none  [the longest x1 145 us: split_layout(): lax.all_to_all(slab_grad.reshape(wide_count, narrow_count, shard_rows, sl...]
    all_gather x2 -> x0, waiting for transfers between devices: 112 us -> none  [the longest x1 79.9 us: split_layout(): lax.all_gather(spread.reshape(narrow_count * shard_rows, slab_width), 'wi...]
    all_to_all x1 -> x0, waiting for transfers between devices: 73.1 us -> none  [split_layout(): lax.all_to_all(lax.all_to_all(slab_grad.reshape(wide_count, narrow_count,...]
    reduce_scatter x1 -> x0, waiting for transfers between devices: 59.4 us -> none  [split_layout(): lax.psum_scatter(d_normed_part.astype(jnp.bfloat16), 'narrow', scatter_di...]
    convert_element_type x3 -> x0, local copies, waits for them, and re-layouts: 53.5 us -> none  [the longest x2 53.4 us: split_layout(): returned = lax.all_to_all(lax.all_to_all(slab_grad.reshape(wide_count, na...]
    concatenate x5 -> x2, local copies, waits for them, and re-layouts: 36.8 us -> 0.71 us  [the longest x1 0.69 us: on_device(): jnp.concatenate(pieces + [jnp.zeros((padded - size,), F32)])]
  transfers between devices with their start and end apart: 7 -> 0, of which waited for: 7 -> 0; matrix products, arithmetic and copies ran while one was open for 6% -> 0% of each run, Pallas kernels for 0% -> 0%
where the time goes in v1:
time: 557 us; the launch traced here: 552 us
  Pallas kernels  360 us (65%)
  matrix products  104 us (19%)
  other arithmetic  54 us (10%)
  local copies, waits for them, and re-layouts  27.2 us (5%)
  between operations  6.81 us (1%)
    pallas_call x8, Pallas kernels, comm_call(): pl.pallas_call(kernel, out_shape=outs, in_specs=[pl.BlockSpec(memory_spac...  360 us
    unnamed x152, local copies, waits for them, and re-layouts  11.5 us

profile of v1, /device:TPU:1, one launch (start us, length us, event | category | flops | bytes accessed | tf_op | source)
XLA Modules:
  0.0 551.8 jit_solution(15288692180198430218)
XLA Ops:
  0.7 1.3 convert_reduce_fusion
  2.1 1.3 fusion.52
  4.2 1.4 fusion.50.refs_0_
  5.7 2.1 fusion.129
  13.2 91.4 %first_gather.1 = (bf16[1024,2048]{1,0:T(8,128)(2,1)}, bf16[1024,2048]{1,0:T(8,128)(2,1)}, bf16[1024,128]{1,0:T(8,128)(2,1)}, bf16[2048,1024]{1,0:T(8,128)(2,1)}, bf16[2048,2048]{1,0:T(8,128)(2,1)}) custom-call(bf16[128,2048]{1,0:T(8,128)(2,1)} %copy-done.7, bf16[128,2048]{1,0:T(8,128)(2,1)} %fusion.54.refs_1_, bf16[128,128]{1,0:T(8,128)(2,1)} %select_convert_fusion.refs_2_, ...), custom_call_target="tpu_custom_call" | custom-call | tf_op jit(solution)/shard_map/first_gather/pallas_call | solution.py:127
  104.6 6.4 %fusion.17 = f32[1024,768]{0,1:T(8,128)S(1)} fusion(bf16[1024,2048]{1,0:T(8,128)(2,1)} %get-tuple-element.33, bf16[2048,1024]{1,0:T(8,128)(2,1)} %get-tuple-element.34), kind=kOutput, calls=%fused_computation.33 | convolution fusion | flops 3221225472 | bytes 10485760 | tf_op jit(solution)/shard_map/dot_general | solution.py:751
  111.2 1.0 fusion.123
  112.9 1.4 copy.177
  114.3 1.3 copy.178
  116.5 2.4 copy.179
  118.8 1.3 copy.180
  120.5 1.9 multiply_cosine_fusion
  122.4 3.4 subtract_convert_fusion.1
  126.4 8.8 %fusion.128 = (f32[2,1024]{1,0:T(2,128)}, f32[2,1024,1024]{1,2,0:T(8,128)}) fusion(pred[1024,1024]{0,1:T(8,128)(4,1)S(1)} %fusion.8, bf16[1024,2,64]{2,0,1:T(8,128)(2,1)S(1)} %get-tuple-element.132, bf16[1024,2,64]{2,0,1:T(8,128)(2,1)} %get-tuple-element.133, bf16[1024,2,64]{2,0,1:T(8,128)(2,1)} %get-tuple-element.119, ...), kind=kOutput, calls=%fused_computation.254 | convolution fusion | flops 547357696 | bytes 10493952 | tf_op jit(solution)/shard_map/sub | solution.py:763
  135.2 1.3 slice.204
  136.6 1.4 fusion.64
  138.0 4.2 fusion.45
  143.0 4.5 convolution_convert_fusion.refs_0_
  147.5 25.7 %sum_attention.1 = f32[128,2048]{1,0:T(8,128)} custom-call(bf16[1024,2048]{1,0:T(8,128)(2,1)} %convolution_convert_fusion.refs_0_), custom_call_target="tpu_custom_call" | custom-call | tf_op jit(solution)/shard_map/sum_attention/pallas_call | solution.py:127
  173.2 1.9 fusion.121
  175.3 1.0 multiply_convert_fusion.3.refs_0_
  176.4 24.0 %gather_normed.1 = bf16[1024,2048]{1,0:T(8,128)(2,1)} custom-call(bf16[128,2048]{1,0:T(8,128)(2,1)} %multiply_convert_fusion.3.refs_0_), custom_call_target="tpu_custom_call" | custom-call | tf_op jit(solution)/shard_map/gather_normed/pallas_call | solution.py:127
  200.4 10.0 %fusion.11 = f32[1024,1024]{1,0:T(8,128)} fusion(bf16[1024,2048]{1,0:T(8,128)(2,1)} %gather_normed.1, bf16[2048,2048]{1,0:T(8,128)(2,1)} %get-tuple-element.37), kind=kOutput, calls=%fused_computation.25 | convolution fusion | flops 4294967296 | bytes 12582912 | tf_op jit(solution)/shard_map/dot_general | solution.py:777
  210.5 9.5 %fusion.4 = bf16[1024,1024]{1,0:T(8,128)(2,1)S(1)} fusion(f32[1024,1024]{1,0:T(8,128)} %fusion.11, bf16[1024,2048]{1,0:T(8,128)(2,1)} %get-tuple-element.36, bf16[2048,2048]{1,0:T(8,128)(2,1)} %get-tuple-element.37, s32[1024]{0:T(1024)S(1)} %iota_add_fusion, s32[1024]{0:T(1024)S(1)} %copy-done.55), kind=kOutput, calls=%fused_computation.10 | convolution fusion | flops 4301258752 | bytes 14688256 | tf_op jit(solution)/shard_map/dot_general | solution.py:783
  220.0 6.3 %convolution_convert_fusion.3.refs_2_ = bf16[2048,1024]{1,0:T(8,128)(2,1)} fusion(bf16[1024,2048]{1,0:T(8,128)(2,1)S(1)} %copy-done.12, bf16[1024,1024]{1,0:T(8,128)(2,1)S(1)} %fusion.4), kind=kOutput, calls=%fused_computation.21 | convolution fusion | flops 4297064448 | bytes 10485760 | tf_op jit(solution)/shard_map/dot_general | solution.py:789
  226.3 6.4 %convolution_convert_fusion.2.refs_3_ = bf16[2048,1024]{1,0:T(8,128)(2,1)} fusion(bf16[1024,2048]{1,0:T(8,128)(2,1)S(1)} %copy-done.63, f32[1024,1024]{1,0:T(8,128)S(1)} %copy-done.66, s32[1024]{0:T(1024)S(1)} %iota_add_fusion, s32[1024]{0:T(1024)S(1)} %copy-done.55), kind=kOutput, calls=%fused_computation.20 | convolution fusion | flops 4302307328 | bytes 12591104 | tf_op jit(solution)/shard_map/dot_general | solution.py:786
  232.7 6.5 %convolution_convert_fusion.4.refs_1_ = bf16[1024,2048]{1,0:T(8,128)(2,1)} fusion(bf16[2048,2048]{1,0:T(8,128)(2,1)S(1)} %bitcast.151, f32[1024,1024]{1,0:T(8,128)S(1)} %copy-done.66, s32[1024]{0:T(1024)S(1)} %iota_add_fusion, s32[1024]{0:T(1024)S(1)} %copy-done.55), kind=kOutput, calls=%fused_computation.22 | convolution fusion | flops 4302307328 | bytes 12591104 | tf_op jit(solution)/shard_map/dot_general | solution.py:782
  239.2 6.2 %convolution_convert_fusion.5.refs_0_ = bf16[1024,2048]{1,0:T(8,128)(2,1)} fusion(bf16[1024,1024]{1,0:T(8,128)(2,1)S(1)} %fusion.4, bf16[2048,2048]{1,0:T(8,128)(2,1)S(1)} %bitcast.151), kind=kOutput, calls=%fused_computation.23 | convolution fusion | flops 4297064448 | bytes 10485760 | tf_op jit(solution)/shard_map/dot_general | solution.py:785
  245.4 41.1 %sum_ffn.1 = (f32[128,2048]{1,0:T(8,128)}, f32[128,2048]{1,0:T(8,128)}) custom-call(bf16[1024,2048]{1,0:T(8,128)(2,1)} %convolution_convert_fusion.5.refs_0_, bf16[1024,2048]{1,0:T(8,128)(2,1)} %convolution_convert_fusion.4.refs_1_), custom_call_target="tpu_custom_call" | custom-call | tf_op jit(solution)/shard_map/sum_ffn/pallas_call | solution.py:127
  286.6 1.7 multiply_reduce_fusion.1
  288.3 1.6 fusion.120
  290.0 1.4 fusion.55
  291.4 25.1 %gather_dattn.1 = bf16[1024,2048]{1,0:T(8,128)(2,1)} custom-call(bf16[128,2048]{1,0:T(8,128)(2,1)} %get-tuple-element.128.refs_0_), custom_call_target="tpu_custom_call" | custom-call | tf_op jit(solution)/shard_map/gather_dattn/pallas_call | solution.py:127
  316.5 4.7 convolution_convert_fusion.7.refs_1_
  321.1 3.9 fusion.56
  325.1 1.6 multiply_reduce_fusion
  326.8 2.7 multiply_convert_fusion
  329.5 1.3 fusion.40
  330.9 2.0 fusion.41
  332.9 1.6 multiply_add_fusion.4
  334.5 1.1 add_convert_fusion.1
  335.6 2.0 copy.150
  337.6 1.1 add_convert_fusion
  338.8 1.2 copy.154
  340.0 5.4 fusion.42
  345.5 5.0 convolution_convert_fusion.6.refs_0_
  351.0 1.4 fusion.130.refs_1_
  352.4 5.3 convolution_convert_fusion.1.refs_0_
  357.7 28.2 %sum_dnormed.1 = (f32[128,2048]{1,0:T(8,128)}, f32[256,256]{1,0:T(8,128)}) custom-call(bf16[1024,2048]{1,0:T(8,128)(2,1)} %convolution_convert_fusion.1.refs_0_, bf16[2048,256]{1,0:T(8,128)(2,1)} %fusion.130.refs_1_), custom_call_target="tpu_custom_call" | custom-call | tf_op jit(solution)/shard_map/sum_dnormed/pallas_call | solution.py:127
  386.0 1.6 convert_element_type.158.refs_4_
  387.6 98.7 %reduce_grads.1 = (bf16[8,16,768]{2,1,0:T(8,128)(2,1)}, bf16[8,16,256]{2,1,0:T(8,128)(2,1)}, bf16[8,16,1024]{2,1,0:T(8,128)(2,1)}, bf16[8,16,1024]{2,1,0:T(8,128)(2,1)}, f32[16,256]{1,0:T(8,128)}) custom-call(bf16[2048,768]{1,0:T(8,128)(2,1)} %convolution_convert_fusion.6.refs_0_, bf16[2048,256]{1,0:T(8,128)(2,1)} %convolution_convert_fusion.7.refs_1_, ...), custom_call_target="tpu_custom_call" | custom-call | tf_op jit(solution)/shard_map/reduce_grads/pallas_call | solution.py:127
  486.3 1.1 slice_bitcast_fusion
  491.2 1.0 fusion.28
  494.5 1.8 fusion.53
  498.5 25.6 %last_sums.1 = (f32[56,128]{1,0:T(8,128)}, f32[2048,256]{1,0:T(8,128)}) custom-call(f32[56,128]{1,0:T(8,128)} %bitcast.147, f32[16,256]{1,0:T(8,128)} %get-tuple-element.46.refs_1_), custom_call_target="tpu_custom_call" | custom-call | tf_op jit(solution)/shard_map/last_sums/pallas_call | solution.py:127
  524.2 1.3 slice.153
  525.4 1.3 multiply_reduce_fusion.5
  528.1 1.3 multiply_reduce_fusion.7
  531.0 1.4 multiply_subtract_fusion.3
  532.3 6.6 %multiply_subtract_fusion = (f32[2048,256]{1,0:T(8,128)}, f32[2048,256]{1,0:T(8,128)}, f32[2048,256]{1,0:T(8,128)}) fusion(f32[2048,256]{1,0:T(8,128)S(1)} %copy-done.1, f32[2048,256]{1,0:T(8,128)} %get-tuple-element.48, f32[]{:T(128)S(6)} %min.3, f32[2048,256]{1,0:T(8,128)} %param.27, f32[2048,256]{1,0:T(8,128)} %param.28), kind=kLoop, calls=%fused_computation.40 | loop fusion | flops 8388608 | bytes 14680068 | tf_op jit(solution)/shard_map/sub | solution.py:683
  539.7 6.0 %fusion.117 = (bf16[16,24576]{1,0:T(8,128)(2,1)}, f32[16,24576]{1,0:T(8,128)}, f32[16,24576]{1,0:T(8,128)}, f32[16,24576]{1,0:T(8,128)}) fusion(f32[16,24576]{1,0:T(8,128)} %param.20, f32[]{:T(128)S(6)} %min.3, bf16[16,24576]{1,0:T(8,128)(2,1)} %copy-done.13, f32[16,24576]{1,0:T(8,128)} %param.21, f32[16,24576]{1,0:T(8,128)} %param.22), kind=kLoop, calls=%fused_computation.245 | loop fusion | flops 7077888 | bytes 11010052 | tf_op jit(solution)/shard_map/convert_element_type | solution.py:892
  545.7 1.9 slice.134
  547.5 1.2 slice.152
  548.8 1.5 add_add_fusion.2
  (215 shorter events, 18.9 us)
Async XLA Ops:
  0.7 7.1 %copy-start.44 = (f32[256,8]{0,1:T(8,128)S(1)}, f32[256,8]{0,1:T(8,128)}, u32[]{:S(2)}) copy-start(f32[256,8]{0,1:T(8,128)} %param.29) | copy-start | bytes 24580
  0.7 7.4 %copy-start.59 = (s32[128,2]{0,1:T(2,128)S(1)}, s32[128,2]{0,1:T(2,128)}, u32[]{:S(2)}) copy-start(s32[128,2]{0,1:T(2,128)} %param.18) | copy-start | bytes 3076
  0.7 9.0 %copy-start.10 = (bf16[128,2048]{1,0:T(8,128)(2,1)S(1)}, bf16[128,2048]{1,0:T(8,128)(2,1)}, u32[]{:S(2)}) copy-start(bf16[128,2048]{1,0:T(8,128)(2,1)} %param.19) | copy-start | bytes 1572868
  0.7 10.0 %copy-start.9 = (f32[16,24576]{1,0:T(8,128)S(1)}, f32[16,24576]{1,0:T(8,128)}, u32[]{:S(2)}) copy-start(f32[16,24576]{1,0:T(8,128)} %param.20) | copy-start | bytes 4718596
  2.0 7.2 %copy-start.41 = (f32[128]{0:T(128)}, f32[128]{0:T(128)S(1)}, u32[]{:S(2)}) copy-start(f32[128]{0:T(128)S(1)} %broadcast_multiply_fusion.5) | copy-start | bytes 1540
  3.4 4.4 copy-start.60
  3.4 5.8 %copy-start.50 = (f32[128]{0:T(128)}, f32[128]{0:T(128)S(1)}, u32[]{:S(2)}) copy-start(f32[128]{0:T(128)S(1)} %fusion.93) | copy-start | bytes 1540
  4.2 5.0 copy-start.29
  5.7 5.9 %copy-start.7 = (bf16[128,2048]{1,0:T(8,128)(2,1)}, bf16[128,2048]{1,0:T(8,128)(2,1)S(1)}, u32[]{:S(2)}) copy-start(bf16[128,2048]{1,0:T(8,128)(2,1)S(1)} %fusion.50.refs_0_) | copy-start | bytes 1572868
  8.0 1.3 copy-start.39
  8.1 4.4 copy-start.35
  111.1 1.8 copy-start.14
  112.9 7.2 %copy-start.64 = (s32[1,2]{1,0:T(1,128)S(1)}, s32[1,2]{1,0:T(1,128)}, u32[]{:S(2)}) copy-start(s32[1,2]{1,0:T(1,128)} %param.17) | copy-start | bytes 28
  125.8 9.4 %copy-start.15 = (bf16[1024,2,64]{2,0,1:T(8,128)(2,1)}, bf16[1024,2,64]{2,0,1:T(8,128)(2,1)S(1)}, u32[]{:S(2)}) copy-start(bf16[1024,2,64]{2,0,1:T(8,128)(2,1)S(1)} %get-tuple-element.132) | copy-start | bytes 786436
  126.4 10.2 %copy-start.22 = (bf16[1024,128]{1,0:T(8,128)(2,1)S(1)}, bf16[1024,128]{1,0:T(8,128)(2,1)}, u32[]{:S(2)}) copy-start(bf16[1024,128]{1,0:T(8,128)(2,1)} %get-tuple-element.35) | copy-start | bytes 786436
  136.5 5.6 %copy-start.24 = (bf16[1024,256]{0,1:T(8,128)(2,1)}, bf16[1024,256]{0,1:T(8,128)(2,1)S(1)}, u32[]{:S(2)}) copy-start(bf16[1024,256]{0,1:T(8,128)(2,1)S(1)} %slice.204) | copy-start | bytes 1572868
  147.5 25.7 %copy-start = (bf16[128,2048]{1,0:T(8,128)(2,1)S(1)}, bf16[128,2048]{1,0:T(8,128)(2,1)}, u32[]{:S(2)}) copy-start(bf16[128,2048]{1,0:T(8,128)(2,1)} %param.16) | copy-start | bytes 1572868
  147.5 25.7 %copy-start.54 = (f32[128]{0:T(128)S(1)}, f32[128]{0:T(128)}, u32[]{:S(2)}) copy-start(f32[128]{0:T(128)} %get-tuple-element.164) | copy-start | bytes 1540
  200.4 10.0 %copy-start.55 = (s32[1024]{0:T(1024)S(1)}, s32[1024]{0:T(1024)}, u32[]{:S(2)}) copy-start(s32[1024]{0:T(1024)} %get-tuple-element.89) | copy-start | bytes 12292
  210.4 9.5 %copy-start.12 = (bf16[1024,2048]{1,0:T(8,128)(2,1)S(1)}, bf16[1024,2048]{1,0:T(8,128)(2,1)}, u32[]{:S(2)}) copy-start(bf16[1024,2048]{1,0:T(8,128)(2,1)} %gather_normed.1) | copy-start | bytes 12582916
  210.4 22.2 %slice-start.2 = ((s8[8388608]{0:T(1024)(128)(4,1)}), s8[4194304]{0:T(1024)(128)(4,1)S(1)}, s32[]{:S(2)}) async-start(s8[8388608]{0:T(1024)(128)(4,1)} %bitcast.150), calls=%async_computation.2 | async-start | bytes 8388608
  220.0 6.3 %copy-start.63 = (bf16[1024,2048]{1,0:T(8,128)(2,1)S(1)}, bf16[1024,2048]{1,0:T(8,128)(2,1)}, u32[]{:S(2)}) copy-start(bf16[1024,2048]{1,0:T(8,128)(2,1)} %get-tuple-element.36) | copy-start | bytes 12582916
  220.0 6.3 %copy-start.66 = (f32[1024,1024]{1,0:T(8,128)S(1)}, f32[1024,1024]{1,0:T(8,128)}, u32[]{:S(2)}) copy-start(f32[1024,1024]{1,0:T(8,128)} %fusion.11) | copy-start | bytes 12582916
  220.0 12.7 %slice-start.3 = ((s8[8388608]{0:T(1024)(128)(4,1)}), s8[4194304]{0:T(1024)(128)(4,1)S(1)}, s32[]{:S(2)}) async-start(s8[8388608]{0:T(1024)(128)(4,1)} %bitcast.150), calls=%async_computation.3 | async-start | bytes 8388608
  286.5 3.4 copy-start.2
  286.5 3.4 copy-start.23
  286.5 3.4 copy-start.53
  289.9 1.5 copy-start.5
  289.9 26.5 %copy-start.56 = (f32[128]{0:T(128)}, f32[128]{0:T(128)S(1)}, u32[]{:S(2)}) copy-start(f32[128]{0:T(128)S(1)} %negate_multiply_fusion.1) | copy-start | bytes 1540
  290.0 26.5 %copy-start.21 = (bf16[1024,2,128]{0,2,1:T(8,128)(2,1)S(1)}, bf16[1024,2,128]{0,2,1:T(8,128)(2,1)}, u32[]{:S(2)}) copy-start(bf16[1024,2,128]{0,2,1:T(8,128)(2,1)} %copy-done.20) | copy-start | bytes 1572868
  316.5 8.6 %slice-start = ((s8[8388608]{0:T(1024)(128)(4,1)}), s8[4194304]{0:T(1024)(128)(4,1)S(1)}, s32[]{:S(2)}) async-start(s8[8388608]{0:T(1024)(128)(4,1)} %bitcast.113), calls=%async_computation | async-start | bytes 8388608
  321.1 4.0 slice-start.1
  321.1 4.0 copy-start.25
  321.1 4.0 copy-start.43
  325.1 1.7 copy-start.65
  326.8 2.7 copy-start.18
  326.8 2.7 copy-start.19
  329.5 1.4 copy-start.16
  329.5 1.4 copy-start.17
  334.5 3.2 copy-start.11
  340.0 5.4 copy-start.26
  340.0 5.4 copy-start.62
  345.4 5.1 copy-start.47
  345.4 5.1 copy-start.49
  345.5 5.1 copy-start.36
  345.5 5.1 copy-start.38
  345.5 5.1 copy-start.40
  345.5 5.2 copy-start.45
  345.5 5.5 copy-start.8
  345.5 6.9 %copy-start.27 = (bf16[2048,1024]{1,0:T(8,128)(2,1)S(1)}, bf16[2048,1024]{1,0:T(8,128)(2,1)}, u32[]{:S(2)}) copy-start(bf16[2048,1024]{1,0:T(8,128)(2,1)} %get-tuple-element.34) | copy-start | bytes 12582916
  486.3 6.0 %copy-start.32 = (f32[16,256]{1,0:T(8,128)S(1)}, f32[16,256]{1,0:T(8,128)}, u32[]{:S(2)}) copy-start(f32[16,256]{1,0:T(8,128)} %get-tuple-element.46.refs_1_) | copy-start | bytes 49156
  486.3 8.2 %copy-start.1 = (f32[2048,256]{1,0:T(8,128)S(1)}, f32[2048,256]{1,0:T(8,128)}, u32[]{:S(2)}) copy-start(f32[2048,256]{1,0:T(8,128)} %param.26) | copy-start | bytes 6291460
  486.3 8.2 %copy-start.30 = (f32[1,2048]{1,0:T(1,128)S(1)}, f32[1,2048]{1,0:T(1,128)}, u32[]{:S(2)}) copy-start(f32[1,2048]{1,0:T(1,128)} %copy-done.29) | copy-start | bytes 24580
  486.3 8.2 %copy-start.42 = (f32[128]{0:T(128)S(1)}, f32[128]{0:T(128)}, u32[]{:S(2)}) copy-start(f32[128]{0:T(128)} %copy-done.41) | copy-start | bytes 1540
  488.3 8.0 %copy-start.61 = (f32[128]{0:T(128)S(1)}, f32[128]{0:T(128)}, u32[]{:S(2)}) copy-start(f32[128]{0:T(128)} %copy-done.60) | copy-start | bytes 1540
  488.3 9.0 %copy-start.51 = (f32[128]{0:T(128)S(1)}, f32[128]{0:T(128)}, u32[]{:S(2)}) copy-start(f32[128]{0:T(128)} %copy-done.50) | copy-start | bytes 1540
  490.3 7.5 %copy-start.58 = (f32[4]{0:T(128)S(1)}, f32[4]{0:T(128)}, u32[]{:S(2)}) copy-start(f32[4]{0:T(128)} %get-tuple-element.99) | copy-start | bytes 52
  532.3 6.6 %copy-start.28 = (f32[56,128]{1,0:T(8,128)S(1)}, f32[56,128]{1,0:T(8,128)}, u32[]{:S(2)}) copy-start(f32[56,128]{1,0:T(8,128)} %get-tuple-element.47) | copy-start | bytes 86020
  532.3 6.7 %copy-start.31 = (f32[2,2048]{1,0:T(2,128)S(1)}, f32[2,2048]{1,0:T(2,128)}, u32[]{:S(2)}) copy-start(f32[2,2048]{1,0:T(2,128)} %param.23) | copy-start | bytes 49156
  532.3 6.7 %copy-start.33 = (f32[2,2048]{1,0:T(2,128)S(1)}, f32[2,2048]{1,0:T(2,128)}, u32[]{:S(2)}) copy-start(f32[2,2048]{1,0:T(2,128)} %param.24) | copy-start | bytes 49156
  532.3 6.7 %copy-start.34 = (f32[2,2048]{1,0:T(2,128)S(1)}, f32[2,2048]{1,0:T(2,128)}, u32[]{:S(2)}) copy-start(f32[2,2048]{1,0:T(2,128)} %param.25) | copy-start | bytes 49156
  539.7 9.1 %copy-start.4 = (f32[128,2048]{1,0:T(8,128)S(1)}, f32[128,2048]{1,0:T(8,128)}, u32[]{:S(2)}) copy-start(f32[128,2048]{1,0:T(8,128)} %copy-done.3) | copy-start | bytes 3145732
  539.7 9.1 %copy-start.6 = (f32[128,2048]{1,0:T(8,128)S(1)}, f32[128,2048]{1,0:T(8,128)}, u32[]{:S(2)}) copy-start(f32[128,2048]{1,0:T(8,128)} %copy-done.5) | copy-start | bytes 3145732
  539.7 9.1 %copy-start.57 = (f32[128]{0:T(128)S(1)}, f32[128]{0:T(128)}, u32[]{:S(2)}) copy-start(f32[128]{0:T(128)} %copy-done.56) | copy-start | bytes 1540
  (7 other events, 6.9 us)

commit v2 on v1

--- a/solution.py
+++ b/solution.py
@@ -63,6 +63,17 @@
     if not isinstance(start, int):
         start = pl.multiple_of(start, ROWS)
     return pl.ds(start, size)
+
+
+def lanes(start, size):
+    if not isinstance(start, int):
+        start = pl.multiple_of(start, 128)
+    return pl.ds(start, size)
+
+
+def step(*parts):
+    for part in parts:
+        next(part, None)
 
 
 class Net:
@@ -150,28 +161,32 @@
     def block(dy, lo=0, size=rows):
         return out.at[span((wrap(y + dy) * 2 + c) * rows + lo, size)]
 
-    mine = net.keep(own, block(0))
     up = net.put(own, block(0), moved(dy=1))
     down = net.put(own, block(0), moved(dy=-1))
     across = [net.put(own, block(0), moved(dc=1))]
-    yield
+    mine = net.keep(own, block(0))
+    yield None
+    mine.wait()
+    across[0].wait_recv()
+    yield 0
     up.wait_recv()
     on = net.put(block(-1, 0, half), block(-1, 0, half), moved(dy=1))
     across.append(net.put(block(-1), block(-1), moved(dc=1)))
-    yield
+    yield None
     down.wait_recv()
     back = net.put(block(1, half, half), block(1, half, half), moved(dy=-1))
     across.append(net.put(block(1), block(1), moved(dc=1)))
-    yield
+    across[1].wait_recv()
+    yield 3
+    across[2].wait_recv()
+    yield 1
     on.wait_recv()
     across.append(net.put(block(2, 0, half), block(2, 0, half), moved(dc=1)))
-    yield
     back.wait_recv()
     across.append(net.put(block(2, half, half), block(2, half, half), moved(dc=1)))
-    yield
-    mine.wait()
-    for copy in across:
-        copy.wait_recv()
+    across[3].wait_recv()
+    across[4].wait_recv()
+    yield 2
 
 
 GATHER_COPIES = 10
@@ -266,6 +281,70 @@
     done.wait()
 
 
+def pairs_scratch(rows, cols):
+    return [
+        pltpu.VMEM((SIDE, 2 * rows, cols), BF),
+        pltpu.VMEM((SIDE, rows, cols), BF),
+        pltpu.VMEM((2, rows // 2, cols), BF),
+        pltpu.VMEM((2, rows, cols), BF),
+        pltpu.VMEM((3, rows, cols), BF),
+        pltpu.VMEM((rows, cols), F32),
+    ]
+
+
+PAIR_ORDER = (2, 1, 3, 0)
+
+
+def reduce_pairs(net, out, scr):
+    parts, other, through, landed, ready, total = scr
+    x, z, y, c = here()
+    rows = total.shape[0]
+    half = rows // 2
+    first, last = pl.ds(0, half), pl.ds(half, half)
+
+    def cross(dy):
+        return net.put(parts.at[dy, span((1 - c) * rows, rows)], other.at[dy], moved(dc=1))
+
+    def pair(dy, lo, size):
+        mine = parts[dy, span(c * rows + lo, size), :].astype(F32)
+        return mine + other[dy, pl.ds(lo, size), :].astype(F32)
+
+    cross_two = cross(2)
+    yield
+    cross_one = cross(1)
+    cross_two.wait_recv()
+    ready[0] = pair(2, 0, rows).astype(BF)
+    via_up = net.put(ready.at[0, first], through.at[0], moved(dy=1))
+    via_down = net.put(ready.at[0, last], through.at[1], moved(dy=-1))
+    yield
+    cross_three = cross(3)
+    cross_one.wait_recv()
+    ready[1, last, :] = pair(1, half, half).astype(BF)
+    up_late = net.put(ready.at[1, last], landed.at[0, last], moved(dy=1))
+    yield
+    cross_own = cross(0)
+    cross_three.wait_recv()
+    ready[2, first, :] = pair(3, 0, half).astype(BF)
+    down_first = net.put(ready.at[2, first], landed.at[1, first], moved(dy=-1))
+    yield
+    via_up.wait_recv()
+    ready[1, first, :] = (pair(1, 0, half) + through[0].astype(F32)).astype(BF)
+    up_first = net.put(ready.at[1, first], landed.at[0, first], moved(dy=1))
+    via_down.wait_recv()
+    ready[2, last, :] = (pair(3, half, half) + through[1].astype(F32)).astype(BF)
+    down_late = net.put(ready.at[2, last], landed.at[1, last], moved(dy=-1))
+    yield
+    cross_own.wait_recv()
+    total[...] = pair(0, 0, rows)
+    yield
+    for copy in (up_late, down_first, up_first, down_late):
+        copy.wait_recv()
+    total[...] += landed[0].astype(F32) + landed[1].astype(F32)
+    done = net.keep(total, out)
+    yield
+    done.wait()
+
+
 def reduce_call(parts, cid, name):
     n = len(parts)
     shapes = [(p.shape[0] // NARROW, p.shape[1]) for p in parts]
@@ -292,7 +371,7 @@
 def spread_narrow(net, src, slab):
     w = lax.axis_index("wide")
     n = lax.axis_index("narrow")
-    base = w * TOK + n * ROWS
+    base = n * ROWS if slab.shape[0] == TOK else w * TOK + n * ROWS
     mine = net.keep(src.at[n], slab.at[span(base, ROWS)])
     copies = []
     for p in NARROW_ALL:
@@ -307,7 +386,7 @@
 SPREAD_COPIES = 7
 
 
-def gather_wide(net, slab, lead):
+def gather_wide(net, slab, lead, stage=None):
     x, z, y, c = here()
     rows = TOK // 2
     half = rows // 2
@@ -323,11 +402,13 @@
     def then_to(d):
         return moved(dz=d) if lead == "x" else moved(dx=d)
 
-    def both(src, to):
-        return net.put(src, src, to(1)), net.put(src, src, to(-1))
-
-    fore, aft = both(block(0, 0), lead_to)
-    second = {0: both(block(0, 0), then_to)}
+    def both(src, to, dst=None):
+        dst = src if dst is None else dst
+        return net.put(src, dst, to(1)), net.put(src, dst, to(-1))
+
+    mine = block(0, 0) if stage is None else stage.at[pl.ds(low, rows)]
+    fore, aft = both(mine, lead_to, block(0, 0))
+    second = {0: both(mine, then_to, block(0, 0))}
     yield
     fore.wait_recv()
     on = net.put(block(-1, 0, 0, half), block(-1, 0, 0, half), lead_to(1))
@@ -345,6 +426,7 @@
         b.wait_recv()
         last.append(net.put(block(a, 1, half, half), block(a, 1, half, half), then_to(-1)))
 
+    kept = None if stage is None else net.keep(mine, block(0, 0))
     relay(0)
     yield
     on.wait_recv()
@@ -356,6 +438,8 @@
     yield
     relay(2)
     yield
+    if kept is not None:
+        kept.wait()
     for copy in last:
         copy.wait_recv()
 
@@ -376,6 +460,8 @@
 
         def weights(i):
             yield from spread_narrow(net, ins[k + i], outs[k + i])
+            if i:
+                return
             a = gather_wide(net, outs[k + i], "x")
             b = gather_wide(net, outs[k + i], "z")
             live = [a, b]
@@ -395,7 +481,8 @@
         )
 
     shapes = [jax.ShapeDtypeStruct((NARROW * o.shape[0], o.shape[1]), o.dtype) for o in owns] + [
-        jax.ShapeDtypeStruct((D, s.shape[2]), s.dtype) for s in sources
+        jax.ShapeDtypeStruct((TOK if i else D, s.shape[2]), s.dtype)
+        for i, s in enumerate(sources)
     ]
     return comm_call(
         body,
@@ -406,6 +493,232 @@
         k * GATHER_COPIES + m * (SPREAD_COPIES + 2 * WIDE_COPIES),
         k + m,
         "first_gather",
+    )
+
+
+def turn(values, cosine, sine):
+    return values * cosine + pltpu.roll(values, HEAD_DIM // 2, 1) * sine
+
+
+def allowed_keys(first_row, rows, first_length):
+    query = first_row + lax.broadcasted_iota(jnp.int32, (rows, 1), 0)
+    key = lax.broadcasted_iota(jnp.int32, (rows, GROUP), 1)
+    start = jnp.where(query >= first_length, first_length, 0)
+    return (key <= query) & (key >= start)
+
+
+def branch_mask(marks, lane):
+    n = lax.axis_index("narrow").astype(F32)
+    return (n < 2.0 * (marks[:, lane : lane + 1].astype(F32) + 1.0)).astype(F32)
+
+
+def attention_forward(normed, slab, turns, first_length, marks, d_ffn_own, stage, cid):
+    pair_rows = 2 * TOK
+    head_part = D // NARROW
+
+    def body(net, ins, outs, scr):
+        normed, slab, turns, first_length, marks, d_ffn_own, stage = ins
+        attn_sum, q_out, k_out, v_out, p_out, a_out, d_ffn, slab_b = outs
+        xv, wv, tv, lv, mv, qv, kv, vv, pv, av = scr[:10]
+        x, z, y, c = here()
+        loads = [net.keep(a, b) for a, b in zip(ins[:5], scr[:5])]
+        greet(NEAR_Y + NEAR_XZ)
+        moves = [
+            gather_wide(net, slab_b, "x", stage),
+            gather_wide(net, slab_b, "z", stage),
+            gather_narrow(net, d_ffn_own, d_ffn),
+        ]
+        step(*moves)
+        for load in loads:
+            load.wait()
+
+        @pl.loop(0, SIDE)
+        def _(i):
+            r = span(i * pair_rows, pair_rows)
+            proj = jnp.dot(xv[r, :], wv[:, : 3 * head_part], preferred_element_type=F32)
+            cosine, sine = tv[0, r, :], tv[1, r, :]
+            for h in range(2):
+                at = pl.ds(h * HEAD_DIM, HEAD_DIM)
+                a = h * HEAD_DIM
+                qv[r, at] = turn(proj[:, a : a + HEAD_DIM], cosine, sine).astype(BF)
+                a += head_part
+                kv[r, at] = turn(proj[:, a : a + HEAD_DIM], cosine, sine).astype(BF)
+            vv[r, :] = proj[:, 2 * head_part :].astype(BF)
+
+        stores = [net.keep(qv, q_out), net.keep(kv, k_out), net.keep(vv, v_out)]
+        total = reduce_pairs(net, attn_sum, scr[10:])
+        length = lv[0:1, 0:1]
+        for dy in PAIR_ORDER:
+            first = wrap(y + dy) * pair_rows
+            r = span(first, pair_rows)
+            allowed = allowed_keys(first, pair_rows, length)
+            heads = []
+            for h in range(2):
+                at = pl.ds(h * HEAD_DIM, HEAD_DIM)
+                scores = lax.dot_general(
+                    qv[r, at], kv[:, at], CONTRACT_COLS, preferred_element_type=F32
+                )
+                scores = jnp.where(allowed, scores * HEAD_DIM ** (-0.5), -1e30)
+                expo = jnp.exp(scores - jnp.max(scores, axis=-1, keepdims=True))
+                probs = expo * (1.0 / jnp.sum(expo, axis=-1, keepdims=True))
+                pv[h, r, :] = probs.astype(BF)
+                heads.append(jnp.dot(pv[h, r, :], vv[:, at], preferred_element_type=F32))
+            mask = branch_mask(mv[r, :], 0)
+            av[r, :] = (jnp.concatenate(heads, axis=1) * mask).astype(BF)
+            scr[10][dy] = lax.dot_general(
+                av[r, :], wv[:, 3 * head_part :], CONTRACT_COLS, preferred_element_type=F32
+            ).astype(BF)
+            step(total, *moves)
+        stores += [net.keep(pv, p_out), net.keep(av, a_out)]
+        take_turns(total, *moves)
+        for store in stores:
+            store.wait()
+
+    low = jax.ShapeDtypeStruct((GROUP, head_part), BF)
+    return comm_call(
+        body,
+        [normed, slab, turns, first_length, marks, d_ffn_own, stage],
+        [
+            jax.ShapeDtypeStruct((TOK, D), F32),
+            low,
+            low,
+            low,
+            jax.ShapeDtypeStruct((2, GROUP, GROUP), BF),
+            low,
+            jax.ShapeDtypeStruct((GROUP, D), BF),
+            jax.ShapeDtypeStruct((D, stage.shape[1]), BF),
+        ],
+        [
+            pltpu.VMEM((GROUP, D), BF),
+            pltpu.VMEM(slab.shape, BF),
+            pltpu.VMEM(turns.shape, F32),
+            pltpu.VMEM(first_length.shape, jnp.int32),
+            pltpu.VMEM(marks.shape, BF),
+            pltpu.VMEM((GROUP, head_part), BF),
+            pltpu.VMEM((GROUP, head_part), BF),
+            pltpu.VMEM((GROUP, head_part), BF),
+            pltpu.VMEM((2, GROUP, GROUP), BF),
+            pltpu.VMEM((GROUP, head_part), BF),
+        ]
+        + pairs_scratch(TOK, D),
+        cid,
+        REDUCE_COPIES + 2 * WIDE_COPIES + GATHER_COPIES,
+        5 + 5 + 4,
+        "attention_forward",
+    )
+
+
+def feed_forward(normed_own, d_ffn, slab, marks, cid):
+    pair_rows = 2 * TOK
+    units = FF // NARROW
+    strip = 256
+
+    def body(net, ins, outs, scr):
+        own, d_ffn, slab, marks = ins
+        norm_sum, ffn_part, g_up, g_down = outs
+        xv, dv, w_up, w_down, mv, act, du, da, gu, gd, yv = scr[:11]
+        x, z, y, c = here()
+        loads = [
+            net.keep(d_ffn, dv),
+            net.keep(slab.at[:, pl.ds(units, units)], w_down),
+            net.keep(slab.at[:, pl.ds(0, units)], w_up),
+            net.keep(marks, mv),
+        ]
+        greet(NEAR_Y)
+        gather = gather_narrow(net, own, xv)
+        next(gather)
+        loads[0].wait()
+        loads[1].wait()
+
+        @pl.loop(0, SIDE)
+        def _(i):
+            r = span(i * pair_rows, pair_rows)
+            da[r, :] = jnp.dot(dv[r, :], w_down[...], preferred_element_type=F32)
+
+        loads[2].wait()
+        loads[3].wait()
+        for dy in gather:
+            if dy is not None:
+                r = span(wrap(y + dy) * pair_rows, pair_rows)
+                up = jnp.dot(xv[r, :], w_up[...], preferred_element_type=F32)
+                positive = jnp.maximum(up, 0.0)
+                masked = positive * branch_mask(mv[r, :], 64)
+                act[r, :] = (positive * masked).astype(BF)
+                du[r, :] = (da[r, :] * (2.0 * masked)).astype(BF)
+
+        total = reduce_pairs(net, norm_sum, scr[11:])
+        for dy in PAIR_ORDER:
+            r = span(wrap(y + dy) * pair_rows, pair_rows)
+            scr[11][dy] = lax.dot_general(
+                du[r, :], w_up[...], CONTRACT_COLS, preferred_element_type=F32
+            ).astype(BF)
+            next(total)
+
+        def gradient(left, right, to, start, stop):
+            @pl.loop(start, stop)
+            def _(i):
+                at = lanes(i * strip, strip)
+                to[span(i * strip, strip), :] = lax.dot_general(
+                    left[:, at], right[...], CONTRACT_ROWS, preferred_element_type=F32
+                ).astype(BF)
+
+        gradient(dv, act, gd, 0, 4)
+        next(total)
+        gradient(dv, act, gd, 4, 8)
+        stores = [net.keep(gd, g_down)]
+        step(total)
+        gradient(xv, du, gu, 0, 8)
+        stores.append(net.keep(gu, g_up))
+        step(total)
+
+        @pl.loop(0, SIDE)
+        def _(i):
+            r = span(i * pair_rows, pair_rows)
+            yv[r, :] = lax.dot_general(
+                act[r, :], w_down[...], CONTRACT_COLS, preferred_element_type=F32
+            ).astype(BF)
+
+        stores.append(net.keep(yv, ffn_part))
+        take_turns(total)
+        for store in stores:
+            store.wait()
+
+    wide = pltpu.VMEM((GROUP, D), BF)
+    tall = pltpu.VMEM((D, units), BF)
+    square = pltpu.VMEM((GROUP, units), BF)
+    return comm_call(
+        body,
+        [normed_own, d_ffn, slab, marks],
+        [
+            jax.ShapeDtypeStruct((TOK, D), F32),
+            jax.ShapeDtypeStruct((GROUP, D), BF),
+            jax.ShapeDtypeStruct((D, units), BF),
+            jax.ShapeDtypeStruct((D, units), BF),
+        ],
+        [wide, wide, tall, tall, pltpu.VMEM(marks.shape, BF), square, square]
+        + [pltpu.VMEM((GROUP, units), F32), tall, tall, wide]
+        + pairs_scratch(TOK, D),
+        cid,
+        GATHER_COPIES + REDUCE_COPIES,
+        4 + 1 + 1 + 3,
+        "feed_forward",
+    )
+
+
+def gather_and_reduce(own, part, cid):
+    def body(net, ins, outs, scr):
+        greet(NEAR_Y)
+        take_turns(gather_narrow(net, ins[0], outs[0]), reduce_narrow(net, ins[1], outs[1], scr))
+
+    return comm_call(
+        body,
+        [own, part],
+        [jax.ShapeDtypeStruct((GROUP, D), BF), jax.ShapeDtypeStruct((TOK, D), F32)],
+        reduce_scratch(TOK, D),
+        cid,
+        GATHER_COPIES + REDUCE_COPIES,
+        1 + REDUCE_LOCALS,
+        "gather_and_reduce",
     )
 
 
@@ -715,7 +1028,6 @@
     rank_number = lax.axis_index("narrow")
     own_heads = HEADS // NARROW
     head_part = D // NARROW
-    unit_part = FF // NARROW
 
     low = block_master.astype(BF)
     source_a = jnp.concatenate([cut(low, i * D, D, NARROW) for i in range(4)], axis=2)
@@ -735,70 +1047,55 @@
     d_ffn_own = (upstream * gate_ffn[:, None]).astype(BF)
     marks = jnp.where(jnp.arange(128)[None, :] < 64, picks[:, 0:1], picks[:, 1:2]).astype(BF)
 
-    normed_low, d_ffn_low, group_marks, slab_a, slab_b = first_gather(
-        [normed_own, d_ffn_own, marks], [source_a, source_b], 0
+    normed_low, group_marks, slab_a, stage_b = first_gather(
+        [normed_own, marks], [source_a, source_b], 0
     )
     w_qkv, w_out = slab_a[:, : 3 * head_part], slab_a[:, 3 * head_part :]
-    w_up, w_down = slab_b[:, :unit_part], slab_b[:, unit_part:]
     picks_attn = group_marks[:, 0:1].astype(jnp.int32)
-    picks_ffn = group_marks[:, 64:65].astype(jnp.int32)
 
     key_index = jnp.arange(GROUP, dtype=jnp.int32)
-    key_segment, key_position = segment_info(lengths[0], key_index)
-    allowed = (key_segment[:, None] == key_segment[None, :]) & (
-        key_index[None, :] <= key_index[:, None]
-    )
-    projected = jnp.dot(normed_low, w_qkv, preferred_element_type=F32)
-    query_raw = projected[:, :head_part].reshape(GROUP, own_heads, HEAD_DIM)
-    key_raw = projected[:, head_part : 2 * head_part].reshape(GROUP, own_heads, HEAD_DIM)
-    rotated, rotate_back = jax.vjp(lambda values: rotate(values, key_position), query_raw)
-    query_low = rotated.astype(BF)
-    key_low = rotate(key_raw, key_position).astype(BF)
-    value_low = projected[:, 2 * head_part :].reshape(GROUP, own_heads, HEAD_DIM).astype(BF)
-    scores = (
-        jnp.einsum("qhd,khd->hqk", query_low, key_low, preferred_element_type=F32) * score_scale
-    )
-    scores = jnp.where(allowed[None], scores, -1e30)
-    top_score = jnp.max(scores, axis=-1, keepdims=True)
-    expo = jnp.exp(scores - top_score)
-    probs = expo / jnp.sum(expo, axis=-1, keepdims=True)
-    probs_low = probs.astype(BF)
-    attended = jnp.einsum("hqk,khd->qhd", probs_low, value_low, preferred_element_type=F32)
+    _, key_position = segment_info(lengths[0], key_index)
+    half_dim = HEAD_DIM // 2
+    frequency = 10000.0 ** (-jnp.arange(half_dim, dtype=F32) / half_dim)
+    angles = key_position.astype(F32)[:, None] * frequency[None, :]
+    cosine, sine = jnp.cos(angles), jnp.sin(angles)
+    turns = jnp.stack(
+        [
+            jnp.concatenate([cosine, cosine], axis=1),
+            jnp.concatenate([-sine, sine], axis=1),
+        ]
+    )
+    first_length = jnp.broadcast_to(lengths[:, 0:1], (8, 128))
+    attn_out, query_flat, key_flat, value_flat, probs_low, mixed_low, d_ffn_low, slab_b = (
+        attention_forward(
+            normed_low, slab_a, turns, first_length, group_marks, d_ffn_own, stage_b, 1
+        )
+    )
+    query_low = query_flat.reshape(GROUP, own_heads, HEAD_DIM)
+    key_low = key_flat.reshape(GROUP, own_heads, HEAD_DIM)
+    value_low = value_flat.reshape(GROUP, own_heads, HEAD_DIM)
+    probs = probs_low.astype(F32)
     head_number = rank_number * own_heads + jnp.arange(own_heads, dtype=jnp.int32)
     head_mask = (head_number[None, :] < HEADS * (picks_attn + 1) // LEVELS).astype(F32)
-    mixed_low = (attended * head_mask[:, :, None]).reshape(GROUP, head_part).astype(BF)
-    attn_part = lax.dot_general(mixed_low, w_out, CONTRACT_COLS, preferred_element_type=F32)
-    (attn_out,) = reduce_call([attn_part.astype(BF)], 1, "sum_attention")
 
     after_attn = inputs + gate_attn[:, None] * attn_out
     norm_two, norm_two_back = jax.vjp(layer_norm, after_attn, gains[1])
-    normed_two_low = gather_call(norm_two.astype(BF), 2, "gather_normed")
-
-    up_proj = jnp.dot(normed_two_low, w_up, preferred_element_type=F32)
-    unit_number = rank_number * unit_part + jnp.arange(unit_part, dtype=jnp.int32)
-    unit_mask = (unit_number[None, :] < FF * (picks_ffn + 1) // LEVELS).astype(F32)
-    positive = jnp.maximum(up_proj, 0.0)
-    activity_low = (positive * positive * unit_mask).astype(BF)
-    ffn_part = lax.dot_general(activity_low, w_down, CONTRACT_COLS, preferred_element_type=F32)
-    d_activity = jnp.dot(d_ffn_low, w_down, preferred_element_type=F32)
-    d_up_low = (d_activity * unit_mask * 2.0 * positive).astype(BF)
-    d_norm_part = lax.dot_general(d_up_low, w_up, CONTRACT_COLS, preferred_element_type=F32)
-    grad_down = lax.dot_general(
-        d_ffn_low, activity_low, CONTRACT_ROWS, preferred_element_type=F32
-    ).astype(BF)
-    grad_up = lax.dot_general(
-        normed_two_low, d_up_low, CONTRACT_ROWS, preferred_element_type=F32
-    ).astype(BF)
-    d_norm_two, ffn_out = reduce_call(
-        [d_norm_part.astype(BF), ffn_part.astype(BF)], 3, "sum_ffn"
-    )
-
-    result = (after_attn + gate_ffn[:, None] * ffn_out).astype(BF)
-    d_gate_ffn = jnp.sum(upstream * ffn_out, axis=1)
+
+    d_norm_two, ffn_part, grad_up, grad_down = feed_forward(
+        norm_two.astype(BF), d_ffn_low, slab_b, group_marks, 2
+    )
     d_after, d_gain_two = norm_two_back(d_norm_two)
     d_after = d_after + upstream
     d_gate_attn = jnp.sum(d_after * attn_out, axis=1)
-    d_attn_low = gather_call((d_after * gate_attn[:, None]).astype(BF), 4, "gather_dattn")
+    d_attn_low, ffn_out = gather_and_reduce(
+        (d_after * gate_attn[:, None]).astype(BF), ffn_part, 3
+    )
+
+    result = (after_attn + gate_ffn[:, None] * ffn_out).astype(BF)
+    d_gate_ffn = jnp.sum(upstream * ffn_out, axis=1)
+    _, rotate_back = jax.vjp(
+        lambda values: rotate(values, key_position), jnp.zeros((GROUP, own_heads, HEAD_DIM), F32)
+    )
 
     grad_out = lax.dot_general(
         d_attn_low, mixed_low, CONTRACT_ROWS, preferred_element_type=F32

time: 557 us -> 464 us (0.83)
  matrix products: 104 us -> 26.3 us
  Pallas kernels: 360 us -> 353 us
    dot_general x9 -> x0, matrix products: 60 us -> none  [the longest x1 10 us: on_device(): up_proj = jnp.dot(normed_two_low, w_up, preferred_element_type=F32)]
    sub x1 -> x0, matrix products: 8.83 us -> none  [on_device(): expo = jnp.exp(scores - top_score)]
    pallas_call x8 -> x7, Pallas kernels: 360 us -> 353 us  [comm_call(): pl.pallas_call(kernel, out_shape=outs, in_specs=[pl.BlockSpec(memory_spac...]
    unnamed x152 -> x70, local copies, waits for them, and re-layouts: 11.5 us -> 5.41 us
where the time goes in v2:
time: 464 us; the launch traced here: 458 us
  Pallas kernels  353 us (76%)
  other arithmetic  49 us (11%)
  matrix products  26.3 us (6%)
  local copies, waits for them, and re-layouts  23.4 us (5%)
  between operations  5.99 us (1%)
    pallas_call x7, Pallas kernels, comm_call(): pl.pallas_call(kernel, out_shape=outs, in_specs=[pl.BlockSpec(memory_spac...  353 us

profile of v2, /device:TPU:1, one launch (start us, length us, event | category | flops | bytes accessed | tf_op | source)
XLA Modules:
  0.0 457.9 jit_solution(3421269081945528971)
XLA Ops:
  0.7 1.0 reduce-window.4
  2.3 1.2 convert_reduce_fusion
  3.5 1.3 fusion.18
  4.9 0.8 slice_bitcast_fusion.4
  5.8 1.2 broadcast_in_dim.116.refs_3_
  7.1 0.8 fusion.82
  7.9 0.7 select_convert_fusion.refs_1_
  8.6 1.5 fusion.16.refs_0_
  11.1 0.9 fusion.20.refs_5_
  12.2 0.7 pad_maximum_fusion.5.refs_2_
  13.0 0.8 pad_maximum_fusion.4.refs_3_
  13.8 2.9 multiply_cosine_fusion
  17.0 2.4 maximum_bitcast_fusion
  19.3 0.9 copy.125
  20.2 2.2 pad_maximum_fusion.1.refs_2_
  22.4 51.5 %first_gather.1 = (bf16[1024,2048]{1,0:T(8,128)(2,1)}, bf16[1024,128]{1,0:T(8,128)(2,1)}, bf16[2048,1024]{1,0:T(8,128)(2,1)}, bf16[128,2048]{1,0:T(8,128)(2,1)}) custom-call(bf16[128,2048]{1,0:T(8,128)(2,1)} %copy-done.5, bf16[128,128]{1,0:T(8,128)(2,1)} %select_convert_fusion.refs_1_, bf16[8,16,1024]{2,1,0:T(8,128)(2,1)} %pad_maximum_fusion.5.refs_2_, ...), custom_call_target="tpu_custom_call" | custom-call | tf_op jit(solution)/shard_map/first_gather/pallas_call | solution.py:138
  74.0 1.4 fusion.25
  75.5 46.9 %attention_forward.1 = (f32[128,2048]{1,0:T(8,128)}, bf16[1024,256]{1,0:T(8,128)(2,1)}, bf16[1024,256]{1,0:T(8,128)(2,1)}, bf16[1024,256]{1,0:T(8,128)(2,1)}, bf...) custom-call(bf16[1024,2048]{1,0:T(8,128)(2,1)} %get-tuple-element.44, ...), custom_call_target="tpu_custom_call" | custom-call | tf_op jit(solution)/shard_map/attention_forward/pallas_call | solution.py:138
  122.4 2.1 copy.140
  124.5 2.0 copy.141
  126.5 1.5 fusion.79
  128.3 1.0 multiply_convert_fusion.2.refs_0_
  129.3 56.5 %feed_forward.1 = (f32[128,2048]{1,0:T(8,128)}, bf16[1024,2048]{1,0:T(8,128)(2,1)}, bf16[2048,1024]{1,0:T(8,128)(2,1)}, bf16[2048,1024]{1,0:T(8,128)(2,1)}) custom-call(bf16[128,2048]{1,0:T(8,128)(2,1)} %multiply_convert_fusion.2.refs_0_, bf16[1024,2048]{1,0:T(8,128)(2,1)} %get-tuple-element.49.refs_1_, bf16[2048,2048]{1,0:T(8,128)(2,1)} %get-tuple-element.50.refs_2_, ...), custom_call_target="tpu_custom_call" | custom-call | tf_op jit(solution)/shard_map/feed_forward/pallas_call | solution.py:138
  185.9 1.7 multiply_reduce_fusion
  188.6 1.1 multiply_convert_fusion.1.refs_0_
  189.6 43.4 %gather_and_reduce.1 = (bf16[1024,2048]{1,0:T(8,128)(2,1)}, f32[128,2048]{1,0:T(8,128)}) custom-call(bf16[128,2048]{1,0:T(8,128)(2,1)} %multiply_convert_fusion.1.refs_0_, bf16[1024,2048]{1,0:T(8,128)(2,1)} %get-tuple-element.52.refs_1_), custom_call_target="tpu_custom_call" | custom-call | tf_op jit(solution)/shard_map/gather_and_reduce/pallas_call | solution.py:138
  233.1 2.5 fusion.21
  236.0 0.9 fusion.38
  236.8 1.0 reshape.326
  237.9 1.4 fusion.84.refs_1_
  239.3 4.8 %convolution_convert_fusion.2.refs_1_ = bf16[2048,256]{1,0:T(8,128)(2,1)} fusion(bf16[1024,2048]{1,0:T(8,128)(2,1)} %get-tuple-element.56, bf16[1024,256]{1,0:T(8,128)(2,1)} %get-tuple-element.60), kind=kOutput, calls=%fused_computation.8 | convolution fusion | flops 1074266112 | bytes 5767168 | tf_op jit(solution)/shard_map/dot_general | solution.py:1100
  244.4 1.3 fusion.22
  245.7 0.9 copy-done
  246.5 0.8 convolution_convert_fusion.4
  247.6 1.8 fusion
  249.4 1.3 fusion.1
  250.7 0.8 fusion.12
  251.7 1.5 fusion.13
  253.7 1.7 copy-done.14
  255.4 5.4 %convolution_convert_fusion.1.refs_0_ = bf16[2048,768]{1,0:T(8,128)(2,1)} fusion(bf16[1024,2048]{1,0:T(8,128)(2,1)S(1)} %copy-done.14, bf16[1024,256]{0,1:T(8,128)(2,1)S(1)} %bitcast.125, bf16[1024,256]{0,1:T(8,128)(2,1)S(1)} %bitcast.123, bf16[1024,256]{0,1:T(8,128)(2,1)S(1)} %bitcast.121), kind=kOutput, calls=%fused_computation.5 | convolution fusion | flops 3227516928 | bytes 8912896 | tf_op jit(solution)/shard_map/dot_general | solution.py:1120
  260.8 5.1 %convolution_convert_fusion.refs_0_ = bf16[1024,2048]{1,0:T(8,128)(2,1)} fusion(bf16[2048,1024]{1,0:T(8,128)(2,1)S(1)} %copy-done.13, bf16[1024,256]{0,1:T(8,128)(2,1)S(1)} %bitcast.126, bf16[1024,256]{0,1:T(8,128)(2,1)S(1)} %bitcast.124, bf16[1024,256]{0,1:T(8,128)(2,1)S(1)} %bitcast.122), kind=kOutput, calls=%fused_computation.4 | convolution fusion | flops 3228041216 | bytes 8912896 | tf_op jit(solution)/shard_map/dot_general | solution.py:1123
  265.9 29.6 %sum_dnormed.1 = (f32[128,2048]{1,0:T(8,128)}, f32[256,256]{1,0:T(8,128)}) custom-call(bf16[1024,2048]{1,0:T(8,128)(2,1)} %convolution_convert_fusion.refs_0_, bf16[2048,256]{1,0:T(8,128)(2,1)} %fusion.84.refs_1_), custom_call_target="tpu_custom_call" | custom-call | tf_op jit(solution)/shard_map/sum_dnormed/pallas_call | solution.py:138
  295.5 1.9 fusion.19
  298.1 1.5 add_add_fusion.2
  299.5 0.7 convert_element_type.110.refs_4_
  300.2 99.2 %reduce_grads.1 = (bf16[8,16,768]{2,1,0:T(8,128)(2,1)}, bf16[8,16,256]{2,1,0:T(8,128)(2,1)}, bf16[8,16,1024]{2,1,0:T(8,128)(2,1)}, bf16[8,16,1024]{2,1,0:T(8,128)(2,1)}, f32[16,256]{1,0:T(8,128)}) custom-call(bf16[2048,768]{1,0:T(8,128)(2,1)} %convolution_convert_fusion.1.refs_0_, bf16[2048,256]{1,0:T(8,128)(2,1)} %convolution_convert_fusion.2.refs_1_, ...), custom_call_target="tpu_custom_call" | custom-call | tf_op jit(solution)/shard_map/reduce_grads/pallas_call | solution.py:138
  399.4 1.3 multiply_reduce_fusion.5
  400.8 0.8 copy.152
  401.6 0.9 slice_bitcast_fusion
  402.6 1.0 copy.153
  403.6 1.0 copy.154
  404.7 1.0 fusion.6
  407.0 0.7 concatenate.28
  407.7 26.1 %last_sums.1 = (f32[56,128]{1,0:T(8,128)}, f32[2048,256]{1,0:T(8,128)}) custom-call(f32[56,128]{1,0:T(8,128)} %bitcast.145, f32[16,256]{1,0:T(8,128)} %get-tuple-element.68.refs_1_), custom_call_target="tpu_custom_call" | custom-call | tf_op jit(solution)/shard_map/last_sums/pallas_call | solution.py:138
  433.8 1.3 multiply_reduce_fusion.6
  435.1 1.3 multiply_reduce_fusion.4
  436.5 1.3 slice.109
  439.8 0.7 slice_multiply_fusion.1
  440.5 0.7 slice_multiply_fusion
  441.2 0.7 multiply_subtract_fusion.2
  442.7 2.6 slice.97
  445.3 1.2 slice.108
  446.6 6.7 %multiply_subtract_fusion = (f32[2048,256]{1,0:T(8,128)}, f32[2048,256]{1,0:T(8,128)}, f32[2048,256]{1,0:T(8,128)}) fusion(f32[2048,256]{1,0:T(8,128)S(1)} %copy-done.2, f32[2048,256]{1,0:T(8,128)} %get-tuple-element.70, f32[]{:T(128)S(6)} %min.3, f32[2048,256]{1,0:T(8,128)} %param.27, f32[2048,256]{1,0:T(8,128)} %param.28), kind=kLoop, calls=%fused_computation.13 | loop fusion | flops 8388608 | bytes 14680068 | tf_op jit(solution)/shard_map/sub | solution.py:996
  453.3 3.2 fusion.75
  (119 shorter events, 6.8 us)
Async XLA Ops:
  0.7 9.4 %copy-start.2 = (f32[2048,256]{1,0:T(8,128)S(1)}, f32[2048,256]{1,0:T(8,128)}, u32[]{:S(2)}) copy-start(f32[2048,256]{1,0:T(8,128)} %param.26) | copy-start | bytes 6291460
  3.5 6.9 %copy-start.28 = (f32[256,8]{0,1:T(8,128)S(1)}, f32[256,8]{0,1:T(8,128)}, u32[]{:S(2)}) copy-start(f32[256,8]{0,1:T(8,128)} %param.29) | copy-start | bytes 24580
  8.6 2.5 copy-start.7
  10.1 2.0 copy-start.5
  10.1 2.0 copy-start.10
  10.4 0.7 copy-start.23
  122.4 4.2 copy-start.1
  185.8 1.7 copy-start.16
  187.5 1.0 copy-start.8
  188.0 45.1 %copy-start.3 = (f32[128,2048]{1,0:T(8,128)}, f32[128,2048]{1,0:T(8,128)S(1)}, u32[]{:S(2)}) copy-start(f32[128,2048]{1,0:T(8,128)S(1)} %get-tuple-element.135) | copy-start | bytes 3145732
  189.6 43.4 %copy-start.15 = (f32[128,2048]{1,0:T(8,128)S(1)}, f32[128,2048]{1,0:T(8,128)}, u32[]{:S(2)}) copy-start(f32[128,2048]{1,0:T(8,128)} %get-tuple-element.48) | copy-start | bytes 3145732
  233.0 2.7 copy-start.24
  233.0 4.8 %copy-start.6 = (bf16[128,2048]{1,0:T(8,128)(2,1)S(1)}, bf16[128,2048]{1,0:T(8,128)(2,1)}, u32[]{:S(2)}) copy-start(bf16[128,2048]{1,0:T(8,128)(2,1)} %copy-done.5) | copy-start | bytes 1572868
  239.3 4.8 %copy-start.13 = (bf16[2048,1024]{1,0:T(8,128)(2,1)S(1)}, bf16[2048,1024]{1,0:T(8,128)(2,1)}, u32[]{:S(2)}) copy-start(bf16[2048,1024]{1,0:T(8,128)(2,1)} %get-tuple-element.45.refs_1_) | copy-start | bytes 12582916
  239.3 5.0 %copy-start.31 = (bf16[1024,2048]{1,0:T(8,128)(2,1)S(1)}, bf16[1024,2048]{1,0:T(8,128)(2,1)}, u32[]{:S(2)}) copy-start(bf16[1024,2048]{1,0:T(8,128)(2,1)} %get-tuple-element.56) | copy-start | bytes 12582916
  244.4 2.2 copy-start
  246.5 1.0 copy-start.21
  249.4 1.3 copy-start.12
  250.7 1.0 copy-start.17
  251.7 1.5 copy-start.20
  253.2 2.2 copy-start.14
  295.5 2.5 copy-start.4
  295.5 2.5 copy-start.9
  298.0 1.5 copy-start.22
  402.5 38.7 %copy-start.25 = (f32[2,2048]{1,0:T(2,128)S(1)}, f32[2,2048]{1,0:T(2,128)}, u32[]{:S(2)}) copy-start(f32[2,2048]{1,0:T(2,128)} %param.23) | copy-start | bytes 49156
  402.5 38.7 %copy-start.26 = (f32[2,2048]{1,0:T(2,128)S(1)}, f32[2,2048]{1,0:T(2,128)}, u32[]{:S(2)}) copy-start(f32[2,2048]{1,0:T(2,128)} %param.24) | copy-start | bytes 49156
  402.6 38.7 %copy-start.27 = (f32[2,2048]{1,0:T(2,128)S(1)}, f32[2,2048]{1,0:T(2,128)}, u32[]{:S(2)}) copy-start(f32[2,2048]{1,0:T(2,128)} %param.25) | copy-start | bytes 49156
  402.6 39.5 %copy-start.29 = (f32[256,8]{0,1:T(8,128)S(1)}, f32[256,8]{0,1:T(8,128)}, u32[]{:S(2)}) copy-start(f32[256,8]{0,1:T(8,128)} %param.30) | copy-start | bytes 24580
  402.6 39.5 %copy-start.30 = (f32[256,8]{0,1:T(8,128)S(1)}, f32[256,8]{0,1:T(8,128)}, u32[]{:S(2)}) copy-start(f32[256,8]{0,1:T(8,128)} %param.31) | copy-start | bytes 24580
  446.6 6.7 %copy-start.11 = (f32[16,24576]{1,0:T(8,128)S(1)}, f32[16,24576]{1,0:T(8,128)}, u32[]{:S(2)}) copy-start(f32[16,24576]{1,0:T(8,128)} %param.20) | copy-start | bytes 4718596
  446.6 6.7 %copy-start.18 = (f32[16,24576]{1,0:T(8,128)S(1)}, f32[16,24576]{1,0:T(8,128)}, u32[]{:S(2)}) copy-start(f32[16,24576]{1,0:T(8,128)} %param.21) | copy-start | bytes 4718596
  446.6 6.7 %copy-start.19 = (f32[16,24576]{1,0:T(8,128)S(1)}, f32[16,24576]{1,0:T(8,128)}, u32[]{:S(2)}) copy-start(f32[16,24576]{1,0:T(8,128)} %param.22) | copy-start | bytes 4718596

commit v3 on v2

--- a/solution.py
+++ b/solution.py
@@ -80,7 +80,7 @@
     def __init__(self, send, recv, local):
         self.send, self.recv, self.local = send, recv, local
         self.used, self.used_local = 0, 0
-        self.sent, self.kept = [], []
+        self.sent = []
 
     def put(self, src, dst, target):
         i = self.used
@@ -104,6 +104,12 @@
         copy.start()
         return copy
 
+    def sent_by(self, *copies):
+        for copy in copies:
+            copy.wait_send()
+        done = [id(copy) for copy in copies]
+        self.sent = [copy for copy in self.sent if id(copy) not in done]
+
     def finish(self):
         for copy in self.sent:
             copy.wait_send()
@@ -147,7 +153,7 @@
             pltpu.SemaphoreType.DMA((max(locals_, 1),)),
         ],
         compiler_params=pltpu.CompilerParams(
-            collective_id=cid, has_side_effects=True, vmem_limit_bytes=56 * 2**20
+            collective_id=cid, has_side_effects=True, vmem_limit_bytes=62 * 2**20
         ),
         name=name,
     )(*ins)
@@ -187,6 +193,7 @@
     across[3].wait_recv()
     across[4].wait_recv()
     yield 2
+    net.sent_by(up, down, on, back, *across)
 
 
 GATHER_COPIES = 10
@@ -458,26 +465,13 @@
     def body(net, ins, outs, scr):
         greet(NARROW_ALL + NEAR_XZ)
 
-        def weights(i):
-            yield from spread_narrow(net, ins[k + i], outs[k + i])
-            if i:
-                return
-            a = gather_wide(net, outs[k + i], "x")
-            b = gather_wide(net, outs[k + i], "z")
-            live = [a, b]
-            while live:
-                for g in list(live):
-                    try:
-                        next(g)
-                    except StopIteration:
-                        live.remove(g)
-                yield
-
+        for _ in spread_narrow(net, ins[k], outs[k]):
+            pass
         take_turns(
-            weights(0),
-            gather_narrow(net, ins[0], outs[0]),
-            *[weights(i) for i in range(1, m)],
-            *[gather_narrow(net, ins[i], outs[i]) for i in range(1, k)],
+            gather_wide(net, outs[k], "x"),
+            gather_wide(net, outs[k], "z"),
+            *[gather_narrow(net, ins[i], outs[i]) for i in range(k)],
+            *[spread_narrow(net, ins[k + i], outs[k + i]) for i in range(1, m)],
         )
 
     shapes = [jax.ShapeDtypeStruct((NARROW * o.shape[0], o.shape[1]), o.dtype) for o in owns] + [
@@ -561,8 +555,9 @@
                 scores = jnp.where(allowed, scores * HEAD_DIM ** (-0.5), -1e30)
                 expo = jnp.exp(scores - jnp.max(scores, axis=-1, keepdims=True))
                 probs = expo * (1.0 / jnp.sum(expo, axis=-1, keepdims=True))
-                pv[h, r, :] = probs.astype(BF)
-                heads.append(jnp.dot(pv[h, r, :], vv[:, at], preferred_element_type=F32))
+                low = probs.astype(BF)
+                pv[wrap(y + dy), :, pl.ds(h * GROUP, GROUP)] = low
+                heads.append(jnp.dot(low, vv[:, at], preferred_element_type=F32))
             mask = branch_mask(mv[r, :], 0)
             av[r, :] = (jnp.concatenate(heads, axis=1) * mask).astype(BF)
             scr[10][dy] = lax.dot_general(
@@ -583,7 +578,7 @@
             low,
             low,
             low,
-            jax.ShapeDtypeStruct((2, GROUP, GROUP), BF),
+            jax.ShapeDtypeStruct((SIDE, pair_rows, 2 * GROUP), BF),
             low,
             jax.ShapeDtypeStruct((GROUP, D), BF),
             jax.ShapeDtypeStruct((D, stage.shape[1]), BF),
@@ -597,7 +592,7 @@
             pltpu.VMEM((GROUP, head_part), BF),
             pltpu.VMEM((GROUP, head_part), BF),
             pltpu.VMEM((GROUP, head_part), BF),
-            pltpu.VMEM((2, GROUP, GROUP), BF),
+            pltpu.VMEM((SIDE, pair_rows, 2 * GROUP), BF),
             pltpu.VMEM((GROUP, head_part), BF),
         ]
         + pairs_scratch(TOK, D),
@@ -705,161 +700,298 @@
     )
 
 
-def gather_and_reduce(own, part, cid):
+def wide_scratch(cols):
+    part, half = TOK // 2, TOK // 4
+    return [
+        pltpu.VMEM((2, 2, SIDE, half, cols), BF),
+        pltpu.VMEM((2, 2, SIDE, part, cols), BF),
+        pltpu.VMEM((2, 2, SIDE, half, cols), BF),
+        pltpu.VMEM((2, SIDE, part, cols), BF),
+        pltpu.VMEM((2, 2, half, cols), BF),
+        pltpu.VMEM((2, 2, part, cols), BF),
+        pltpu.VMEM((2, 2, half, cols), BF),
+        pltpu.VMEM((TOK, cols), BF),
+    ]
+
+
+REDUCE_WIDE_COPIES = 24
+REDUCE_WIDE_LOCALS = 6
+
+
+def reduce_wide(net, grad, scr, lead):
+    via, landed, ready, sums, via_two, landed_two, ready_two, total = scr
+    x, z, y, c = here()
+    part, half = TOK // 2, TOK // 4
+    k = 0 if lead == "x" else 1
+    low = k * part
+    blocks = grad.reshape(SIDE, SIDE, TOK, grad.shape[1])
+    first, last = pl.ds(0, half), pl.ds(half, half)
+
+    def line(d, lo, size):
+        rows = pl.ds(low + lo, size)
+        if lead == "x":
+            return (wrap(x + d), slice(None), rows, slice(None))
+        return (slice(None), wrap(z + d), rows, slice(None))
+
+    def lead_to(d):
+        return moved(dx=d) if lead == "x" else moved(dz=d)
+
+    def then_to(d):
+        return moved(dz=d) if lead == "x" else moved(dx=d)
+
+    via_up = net.put(blocks.at[line(2, 0, half)], via.at[k, 0], lead_to(1))
+    via_down = net.put(blocks.at[line(2, half, half)], via.at[k, 1], lead_to(-1))
+    up_late = net.put(blocks.at[line(1, half, half)], landed.at[k, 0, :, last], lead_to(1))
+    down_first = net.put(blocks.at[line(3, 0, half)], landed.at[k, 1, :, first], lead_to(-1))
+    loads = [
+        net.keep(blocks.at[line(1, 0, half)], ready.at[k, 0]),
+        net.keep(blocks.at[line(3, half, half)], ready.at[k, 1]),
+        net.keep(blocks.at[line(0, 0, part)], sums.at[k]),
+    ]
+    yield
+    for load in loads:
+        load.wait()
+    via_up.wait_recv()
+
+    @pl.loop(0, SIDE)
+    def _(i):
+        ready[k, 0, i] = (ready[k, 0, i].astype(F32) + via[k, 0, i].astype(F32)).astype(BF)
+
+    up_first = net.put(ready.at[k, 0], landed.at[k, 0, :, first], lead_to(1))
+    via_down.wait_recv()
+
+    @pl.loop(0, SIDE)
+    def _(i):
+        ready[k, 1, i] = (ready[k, 1, i].astype(F32) + via[k, 1, i].astype(F32)).astype(BF)
+
+    down_late = net.put(ready.at[k, 1], landed.at[k, 1, :, last], lead_to(-1))
+    yield
+    for copy in (up_late, down_first, up_first, down_late):
+        copy.wait_recv()
+
+    @pl.loop(0, SIDE)
+    def _(i):
+        both = landed[k, 0, i].astype(F32) + landed[k, 1, i].astype(F32)
+        sums[k, i] = (sums[k, i].astype(F32) + both).astype(BF)
+
+    me = z if lead == "x" else x
+
+    def block(d, rows):
+        return sums.at[k, wrap(me + d), rows]
+
+    via_up = net.put(block(2, first), via_two.at[k, 0], then_to(1))
+    via_down = net.put(block(2, last), via_two.at[k, 1], then_to(-1))
+    up_late = net.put(block(1, last), landed_two.at[k, 0, last], then_to(1))
+    down_first = net.put(block(3, first), landed_two.at[k, 1, first], then_to(-1))
+    yield
+    via_up.wait_recv()
+    ready_two[k, 0] = (block(1, first)[...].astype(F32) + via_two[k, 0].astype(F32)).astype(BF)
+    up_first = net.put(ready_two.at[k, 0], landed_two.at[k, 0, first], then_to(1))
+    via_down.wait_recv()
+    ready_two[k, 1] = (block(3, last)[...].astype(F32) + via_two[k, 1].astype(F32)).astype(BF)
+    down_late = net.put(ready_two.at[k, 1], landed_two.at[k, 1, last], then_to(-1))
+    yield
+    for copy in (up_late, down_first, up_first, down_late):
+        copy.wait_recv()
+    both = landed_two[k, 0].astype(F32) + landed_two[k, 1].astype(F32)
+    total[pl.ds(low, part), :] = (sums[k, me].astype(F32) + both).astype(BF)
+
+
+def return_narrow(net, total, out, pieces):
+    n = lax.axis_index("narrow")
+    copies, mine = [], []
+    for start, width, to in pieces:
+        spot = out.at[:, lanes(to + n * width, width)]
+        columns = pl.ds(start, width)
+        for p in NARROW_ALL:
+            target = moved(**p)
+            copies.append(net.put(total.at[span(target[1] * ROWS, ROWS), columns], spot, target))
+        mine.append(net.keep(total.at[span(n * ROWS, ROWS), columns], spot))
+    yield
+    for copy in mine:
+        copy.wait()
+    for copy in copies:
+        copy.wait_recv()
+
+
+def wide_then_narrow(net, grad, out, scr, pieces):
+    a, b = reduce_wide(net, grad, scr, "x"), reduce_wide(net, grad, scr, "z")
+    while True:
+        more = [next(a, StopIteration), next(b, StopIteration)]
+        if StopIteration in more:
+            break
+        yield
+    yield from return_narrow(net, scr[7], out, pieces)
+
+
+def attention_backward(d_attn_own, ffn_part, g_up, g_down, normed, kept, cid):
+    pair_rows = 2 * TOK
+    head_part = D // NARROW
+    units = FF // NARROW
+    strip = 256
+    scale = HEAD_DIM ** (-0.5)
+    scratch = (
+        [pltpu.VMEM(r.shape, r.dtype) for r in kept]
+        + [
+            pltpu.VMEM((GROUP, D), BF),
+            pltpu.VMEM((GROUP, head_part), F32),
+            pltpu.VMEM((GROUP, head_part), F32),
+            pltpu.VMEM((GROUP, 3 * head_part), BF),
+            pltpu.VMEM((D, 4 * head_part), BF),
+        ]
+        + pairs_scratch(TOK, D)[1:]
+        + reduce_scratch(TOK, D)
+        + wide_scratch(4 * head_part)
+        + wide_scratch(units)
+        + wide_scratch(units)
+    )
+
     def body(net, ins, outs, scr):
-        greet(NEAR_Y)
-        take_turns(gather_narrow(net, ins[0], outs[0]), reduce_narrow(net, ins[1], outs[1], scr))
+        d_attn_own, ffn_part, g_up, g_down, normed = ins[:5]
+        norm_sum, ffn_sum, block = outs
+        wv, tv, mv, qv, kv, vv, pv, av = scr[:8]
+        big, dk, dv, dproj, ga = scr[8:13]
+        pairs, narrow = [pv, *scr[13:18]], scr[18:24]
+        wide_a, wide_up, wide_down = scr[24:32], scr[32:40], scr[40:48]
+        x, z, y, c = here()
+        loads = [net.keep(a, b) for a, b in zip(ins[5:], scr[:8])]
+        greet(NARROW_ALL + NEAR_XZ)
+        gather = gather_narrow(net, d_attn_own, big)
+        next(gather)
+        down = wide_then_narrow(net, g_down, block, wide_down, [(0, units, 4 * D + FF)])
+        up = wide_then_narrow(net, g_up, block, wide_up, [(0, units, 4 * D)])
+        quarter = [(i * head_part, head_part, i * D) for i in range(4)]
+        mixed = wide_then_narrow(net, ga, block, wide_a, quarter)
+        feed = reduce_narrow(net, ffn_part, ffn_sum, narrow)
+        next(down)
+        dk[...] = jnp.zeros_like(dk)
+        dv[...] = jnp.zeros_like(dv)
+        for load in loads:
+            load.wait()
+
+        def one_pair(dy):
+            r = span(wrap(y + dy) * pair_rows, pair_rows)
+            mask = branch_mask(mv[r, :], 0)
+            back = jnp.dot(big[r, :], wv[:, 3 * head_part :], preferred_element_type=F32)
+            back = (back * mask).astype(BF)
+            for h in range(2):
+                at = pl.ds(h * HEAD_DIM, HEAD_DIM)
+                d_out = back[:, h * HEAD_DIM : (h + 1) * HEAD_DIM]
+                d_probs = lax.dot_general(
+                    d_out, vv[:, at], CONTRACT_COLS, preferred_element_type=F32
+                )
+                probs_low = pv[wrap(y + dy), :, pl.ds(h * GROUP, GROUP)]
+                probs = probs_low.astype(F32)
+                weighted = probs * d_probs
+                centre = jnp.sum(weighted, axis=-1, keepdims=True)
+                ds = (weighted - probs * centre).astype(BF)
+                dq = jnp.dot(ds, kv[:, at], preferred_element_type=F32) * scale
+                dproj[r, at] = turn(dq, tv[0, r, :], -tv[1, r, :]).astype(BF)
+                dk[:, at] += lax.dot_general(
+                    ds, qv[r, at], CONTRACT_ROWS, preferred_element_type=F32
+                )
+                dv[:, at] += lax.dot_general(
+                    probs_low, d_out, CONTRACT_ROWS, preferred_element_type=F32
+                )
+
+        for dy in gather:
+            if dy is not None:
+                one_pair(dy)
+                if dy == 0:
+                    step(down, up)
+                if dy == 1:
+                    step(down)
+
+        @pl.loop(0, SIDE)
+        def _(i):
+            r = span(i * pair_rows, pair_rows)
+            cosine, sine = tv[0, r, :], -tv[1, r, :]
+            for h in range(2):
+                at = pl.ds(h * HEAD_DIM, HEAD_DIM)
+                to = pl.ds(head_part + h * HEAD_DIM, HEAD_DIM)
+                dproj[r, to] = turn(dk[r, at] * scale, cosine, sine).astype(BF)
+            dproj[r, pl.ds(2 * head_part, head_part)] = dv[r, :].astype(BF)
+
+        total = reduce_pairs(net, norm_sum, pairs)
+        for dy in PAIR_ORDER:
+            r = span(wrap(y + dy) * pair_rows, pair_rows)
+            pairs[0][dy] = lax.dot_general(
+                dproj[r, :], wv[:, : 3 * head_part], CONTRACT_COLS, preferred_element_type=F32
+            ).astype(BF)
+            next(total)
+
+        @pl.loop(0, D // strip)
+        def _(i):
+            r = span(i * strip, strip)
+            ga[r, pl.ds(3 * head_part, head_part)] = lax.dot_general(
+                big[:, lanes(i * strip, strip)], av[...], CONTRACT_ROWS, preferred_element_type=F32
+            ).astype(BF)
+
+        refill = net.keep(normed, big)
+        step(down, up, feed)
+        refill.wait()
+
+        @pl.loop(0, D // strip)
+        def _(i):
+            r = span(i * strip, strip)
+            ga[r, pl.ds(0, 3 * head_part)] = lax.dot_general(
+                big[:, lanes(i * strip, strip)],
+                dproj[...],
+                CONTRACT_ROWS,
+                preferred_element_type=F32,
+            ).astype(BF)
+
+        take_turns(mixed, total, down, up, feed)
 
     return comm_call(
         body,
-        [own, part],
-        [jax.ShapeDtypeStruct((GROUP, D), BF), jax.ShapeDtypeStruct((TOK, D), F32)],
-        reduce_scratch(TOK, D),
+        [d_attn_own, ffn_part, g_up, g_down, normed] + list(kept),
+        [
+            jax.ShapeDtypeStruct((TOK, D), F32),
+            jax.ShapeDtypeStruct((TOK, D), F32),
+            jax.ShapeDtypeStruct((ROWS, 4 * D + 2 * FF), BF),
+        ],
+        scratch,
         cid,
-        GATHER_COPIES + REDUCE_COPIES,
-        1 + REDUCE_LOCALS,
-        "gather_and_reduce",
-    )
-
-
-def grad_scratch(cols):
-    part = TOK // 2
-    return [
-        pltpu.VMEM((2, SIDE, part, cols), BF),
-        pltpu.VMEM((2, 3, SIDE, part, cols), BF),
-        pltpu.VMEM((2, SIDE, part, cols), BF),
-        pltpu.VMEM((2, 3, part, cols), BF),
-        pltpu.VMEM((TOK, cols), BF),
-    ]
-
-
-GRAD_COPIES = 2 * 6 + 7
-GRAD_LOCALS = 3
-
-
-def reduce_wide(net, grad, out, scr, lead):
-    own, landed, sums, late, total = scr
-    x, z, y, c = here()
-    part = TOK // 2
-    half = 0 if lead == "x" else 1
-    low = half * part
-    blocks = grad.reshape(SIDE, SIDE, TOK, grad.shape[1])
-
-    def line(d):
-        if lead == "x":
-            return blocks.at[wrap(x + d), :, span(low, part), :]
-        return blocks.at[:, wrap(z + d), span(low, part), :]
-
-    def lead_to(d):
-        return moved(dx=d) if lead == "x" else moved(dz=d)
-
-    def then_to(d):
-        return moved(dz=d) if lead == "x" else moved(dx=d)
-
-    mine = net.keep(line(0), own.at[half])
-    copies = [net.put(line(d), landed.at[half, d - 1], lead_to(d)) for d in (2, 1, 3)]
-    yield
-    mine.wait()
-    for copy in copies:
-        copy.wait_recv()
-
-    @pl.loop(0, SIDE)
-    def _(i):
-        s = own[half, i].astype(F32)
-        for d in range(3):
-            s = s + landed[half, d, i].astype(F32)
-        sums[half, i] = s.astype(BF)
-
-    me = z if lead == "x" else x
-    copies = [net.put(sums.at[half, wrap(me + d)], late.at[half, d - 1], then_to(d)) for d in (2, 1, 3)]
-    yield
-    for copy in copies:
-        copy.wait_recv()
-    s = sums[half, me].astype(F32)
-    for d in range(3):
-        s = s + late[half, d].astype(F32)
-    total[span(low, part), :] = s.astype(BF)
-
-
-def return_narrow(net, total, out):
-    n = lax.axis_index("narrow")
-
-    def rows(i):
-        return total.at[span(i * ROWS, ROWS)]
-
-    mine = net.keep(rows(n), out.at[n])
-    copies = []
-    for p in NARROW_ALL:
-        target = moved(**p)
-        copies.append(net.put(rows(target[1]), out.at[n], target))
-    yield
-    mine.wait()
-    for copy in copies:
-        copy.wait_recv()
-
-
-def reduce_grads(grads, small, cid):
-    m = len(grads)
-    scratch = [s for g in grads for s in grad_scratch(g.shape[1])]
-    scratch += [pltpu.VMEM((WIDE, ROWS, RH), BF), pltpu.VMEM((ROWS, RH), F32)]
-
+        GATHER_COPIES + 2 * REDUCE_COPIES + 3 * REDUCE_WIDE_COPIES + 6 * 7,
+        8 + 1 + 1 + 1 + REDUCE_LOCALS + 3 * REDUCE_WIDE_LOCALS + 6,
+        "attention_backward",
+    )
+
+
+def small_wide(part, cid):
     def body(net, ins, outs, scr):
-        greet(NARROW_ALL + WIDE_ALL)
+        landed, total = scr
+        greet(WIDE_ALL)
         w = lax.axis_index("wide")
 
-        def one(i):
-            s = scr[5 * i : 5 * i + 5]
-            a = reduce_wide(net, ins[i], outs[i], s, "x")
-            b = reduce_wide(net, ins[i], outs[i], s, "z")
-            live = [a, b]
-            while live:
-                for g in list(live):
-                    try:
-                        next(g)
-                    except StopIteration:
-                        live.remove(g)
-                if live:
-                    yield
-            yield from return_narrow(net, s[4], outs[i])
-
-        def little():
-            landed, total = scr[5 * m :]
-
-            def rows(i):
-                return ins[m].at[span(i * ROWS, ROWS)]
-
-            mine = net.keep(rows(w), landed.at[w])
-            copies = []
-            for p in WIDE_ALL:
-                target = moved(**p)
-                copies.append(net.put(rows(target[0]), landed.at[w], target))
-            yield
-            yield
-            mine.wait()
-            for copy in copies:
-                copy.wait_recv()
-            s = landed[0].astype(F32)
-            for i in range(1, WIDE):
-                s = s + landed[i].astype(F32)
-            total[...] = s
-            done = net.keep(total, outs[m])
-            yield
-            done.wait()
-
-        take_turns(*[one(i) for i in range(m)], little())
-
-    shapes = [jax.ShapeDtypeStruct((NARROW, ROWS, g.shape[1]), BF) for g in grads]
-    shapes.append(jax.ShapeDtypeStruct((ROWS, RH), F32))
+        def rows(i):
+            return ins[0].at[span(i * ROWS, ROWS)]
+
+        mine = net.keep(rows(w), landed.at[w])
+        copies = []
+        for p in WIDE_ALL:
+            target = moved(**p)
+            copies.append(net.put(rows(target[0]), landed.at[w], target))
+        mine.wait()
+        for copy in copies:
+            copy.wait_recv()
+        s = landed[0].astype(F32)
+        for i in range(1, WIDE):
+            s = s + landed[i].astype(F32)
+        total[...] = s
+        net.keep(total, outs[0]).wait()
+
     return comm_call(
         body,
-        list(grads) + [small],
-        shapes,
-        scratch,
+        [part],
+        [jax.ShapeDtypeStruct((ROWS, RH), F32)],
+        [pltpu.VMEM((WIDE, ROWS, RH), BF), pltpu.VMEM((ROWS, RH), F32)],
         cid,
-        m * GRAD_COPIES + 15,
-        m * GRAD_LOCALS + 2,
-        "reduce_grads",
-    )
+        15,
+        2,
+        "small_wide",
+    )[0]
 
 
 def last_sums(vector, shard, cid):
@@ -947,23 +1079,6 @@
     return centered * lax.rsqrt(spread + NORM_EPS) * gain_row
 
 
-def rotate(values, position):
-    halfway = values.shape[-1] // 2
-    frequency = 10000.0 ** (-jnp.arange(halfway, dtype=jnp.float32) / halfway)
-    angles = position.astype(jnp.float32)[:, None] * frequency[None, :]
-    cosine = jnp.cos(angles)[:, None, :]
-    sine_part = jnp.sin(angles)[:, None, :]
-    first_part = values[..., :halfway]
-    second_part = values[..., halfway:]
-    return jnp.concatenate(
-        [
-            first_part * cosine - second_part * sine_part,
-            first_part * sine_part + second_part * cosine,
-        ],
-        axis=-1,
-    )
-
-
 def segment_info(seg_lengths, token_index):
     seg_ends = jnp.cumsum(seg_lengths)
     segment = jnp.sum((token_index[:, None] >= seg_ends[None, :]).astype(jnp.int32), axis=1)
@@ -1000,10 +1115,6 @@
 def cut(rows, start, width, pieces):
     part = rows[:, start : start + width].reshape(rows.shape[0], pieces, width // pieces)
     return part.transpose(1, 0, 2)
-
-
-def joined(part):
-    return part.transpose(1, 0, 2).reshape(ROWS, -1)
 
 
 def on_device(
@@ -1024,11 +1135,6 @@
     router_out_first,
     router_out_second,
 ):
-    score_scale = HEAD_DIM ** (-0.5)
-    rank_number = lax.axis_index("narrow")
-    own_heads = HEADS // NARROW
-    head_part = D // NARROW
-
     low = block_master.astype(BF)
     source_a = jnp.concatenate([cut(low, i * D, D, NARROW) for i in range(4)], axis=2)
     source_b = jnp.concatenate([cut(low, 4 * D + i * FF, FF, NARROW) for i in range(2)], axis=2)
@@ -1050,8 +1156,6 @@
     normed_low, group_marks, slab_a, stage_b = first_gather(
         [normed_own, marks], [source_a, source_b], 0
     )
-    w_qkv, w_out = slab_a[:, : 3 * head_part], slab_a[:, 3 * head_part :]
-    picks_attn = group_marks[:, 0:1].astype(jnp.int32)
 
     key_index = jnp.arange(GROUP, dtype=jnp.int32)
     _, key_position = segment_info(lengths[0], key_index)
@@ -1066,17 +1170,11 @@
         ]
     )
     first_length = jnp.broadcast_to(lengths[:, 0:1], (8, 128))
-    attn_out, query_flat, key_flat, value_flat, probs_low, mixed_low, d_ffn_low, slab_b = (
+    attn_out, query_low, key_low, value_low, probs_low, mixed_low, d_ffn_low, slab_b = (
         attention_forward(
             normed_low, slab_a, turns, first_length, group_marks, d_ffn_own, stage_b, 1
         )
     )
-    query_low = query_flat.reshape(GROUP, own_heads, HEAD_DIM)
-    key_low = key_flat.reshape(GROUP, own_heads, HEAD_DIM)
-    value_low = value_flat.reshape(GROUP, own_heads, HEAD_DIM)
-    probs = probs_low.astype(F32)
-    head_number = rank_number * own_heads + jnp.arange(own_heads, dtype=jnp.int32)
-    head_mask = (head_number[None, :] < HEADS * (picks_attn + 1) // LEVELS).astype(F32)
 
     after_attn = inputs + gate_attn[:, None] * attn_out
     norm_two, norm_two_back = jax.vjp(layer_norm, after_attn, gains[1])
@@ -1087,55 +1185,24 @@
     d_after, d_gain_two = norm_two_back(d_norm_two)
     d_after = d_after + upstream
     d_gate_attn = jnp.sum(d_after * attn_out, axis=1)
-    d_attn_low, ffn_out = gather_and_reduce(
-        (d_after * gate_attn[:, None]).astype(BF), ffn_part, 3
+    d_normed, ffn_out, block_low = attention_backward(
+        (d_after * gate_attn[:, None]).astype(BF),
+        ffn_part,
+        grad_up,
+        grad_down,
+        normed_low,
+        [slab_a, turns, group_marks, query_low, key_low, value_low, probs_low, mixed_low],
+        3,
     )
 
     result = (after_attn + gate_ffn[:, None] * ffn_out).astype(BF)
     d_gate_ffn = jnp.sum(upstream * ffn_out, axis=1)
-    _, rotate_back = jax.vjp(
-        lambda values: rotate(values, key_position), jnp.zeros((GROUP, own_heads, HEAD_DIM), F32)
-    )
-
-    grad_out = lax.dot_general(
-        d_attn_low, mixed_low, CONTRACT_ROWS, preferred_element_type=F32
-    ).astype(BF)
-    d_mixed = jnp.dot(d_attn_low, w_out, preferred_element_type=F32)
-    d_attended = (d_mixed.reshape(GROUP, own_heads, HEAD_DIM) * head_mask[:, :, None]).astype(BF)
-    d_probs = jnp.einsum("qhd,khd->hqk", d_attended, value_low, preferred_element_type=F32)
-    centre = jnp.sum(probs * d_probs, axis=-1, keepdims=True)
-    d_scores = (probs * (d_probs - centre)).astype(BF)
-    d_query = (
-        jnp.einsum("hqk,khd->qhd", d_scores, key_low, preferred_element_type=F32) * score_scale
-    )
-    d_key = (
-        jnp.einsum("hqk,qhd->khd", d_scores, query_low, preferred_element_type=F32) * score_scale
-    )
-    d_value = jnp.einsum("hqk,qhd->khd", probs_low, d_attended, preferred_element_type=F32)
-    d_query_raw = rotate_back(d_query)[0].reshape(GROUP, head_part)
-    d_key_raw = rotate_back(d_key)[0].reshape(GROUP, head_part)
-    d_proj_low = jnp.concatenate(
-        [d_query_raw, d_key_raw, d_value.reshape(GROUP, head_part)], axis=1
-    ).astype(BF)
-    grad_qkv = lax.dot_general(
-        normed_low, d_proj_low, CONTRACT_ROWS, preferred_element_type=F32
-    ).astype(BF)
-    d_normed_part = lax.dot_general(d_proj_low, w_qkv, CONTRACT_COLS, preferred_element_type=F32)
     d_normed_router, grad_router_in, grad_router_out = router_back((d_gate_attn, d_gate_ffn))
-    d_normed, router_in_part = reduce_call(
-        [d_normed_part.astype(BF), grad_router_in.astype(BF)], 5, "sum_dnormed"
-    )
+    (router_in_part,) = reduce_call([grad_router_in.astype(BF)], 5, "sum_router")
+    router_in_shard = small_wide(router_in_part.astype(BF), 6)
     d_inputs, d_gain_one = norm_one_back(d_normed + d_normed_router)
     d_inputs = d_inputs + d_after
-
-    sum_qkv, sum_out, sum_up, sum_down, router_in_shard = reduce_grads(
-        [grad_qkv, grad_out, grad_up, grad_down], router_in_part.astype(BF), 6
-    )
-    block_grad = jnp.concatenate(
-        [joined(sum_qkv[:, :, i * head_part : (i + 1) * head_part]) for i in range(3)]
-        + [joined(sum_out), joined(sum_up), joined(sum_down)],
-        axis=1,
-    ).astype(F32)
+    block_grad = block_low.astype(F32)
 
     levels = jnp.arange(LEVELS, dtype=jnp.int32)
     counts_local = jnp.concatenate(

time: 464 us -> 353 us (0.76)
  Pallas kernels: 353 us -> 284 us
  matrix products: 26.3 us -> 4.82 us
  local copies, waits for them, and re-layouts: 23.4 us -> 7.97 us
    pallas_call x7, Pallas kernels: 353 us -> 284 us  [comm_call(): pl.pallas_call(kernel, out_shape=outs, in_specs=[pl.BlockSpec(memory_spac...]
    dot_general x8 -> x0, matrix products: 21.3 us -> none  [the longest x1 5.37 us: on_device(): lax.dot_general(normed_low, d_proj_low, CONTRACT_ROWS, preferred_element_...]
    reshape x8 -> x0, local copies, waits for them, and re-layouts: 6.94 us -> none  [the longest x6 2.8 us: joined(): return part.transpose(1, 0, 2).reshape(ROWS, -1)]
where the time goes in v3:
time: 353 us; the launch traced here: 348 us
  Pallas kernels  284 us (80%)
  other arithmetic  45.5 us (13%)
  local copies, waits for them, and re-layouts  7.97 us (2%)
  between operations  5.79 us (2%)
  matrix products  4.82 us (1%)
    pallas_call x7, Pallas kernels, comm_call(): pl.pallas_call(kernel, out_shape=outs, in_specs=[pl.BlockSpec(memory_spac...  284 us
    sub x3, other arithmetic, adamw(): weight - step_rate * (first_hat / (jnp.sqrt(second_hat) + 1e-08) + 0.1 *...  8.54 us

profile of v3, /device:TPU:1, one launch (start us, length us, event | category | flops | bytes accessed | tf_op | source)
XLA Modules:
  0.0 348.0 jit_solution(3752911669524535023)
XLA Ops:
  0.7 0.0 copy-start.1
  0.7 1.3 convert_reduce_fusion
  2.0 1.3 fusion.13
  3.4 0.8 fusion.66
  4.2 0.0 copy-start.18
  4.2 0.0 copy-start.6
  4.2 1.5 fusion.11.refs_0_
  5.7 0.0 copy-start.4
  5.7 0.3 fusion.67
  6.0 0.2 fusion.25
  6.3 0.1 fusion.38
  6.4 0.9 fusion.15.refs_5_
  7.4 0.1 convert_element_type.61
  7.5 0.7 pad_maximum_fusion.2.refs_2_
  8.3 0.8 pad_maximum_fusion.1.refs_3_
  9.2 0.7 select_convert_fusion.refs_1_
  9.9 46.2 %first_gather.1 = (bf16[1024,2048]{1,0:T(8,128)(2,1)}, bf16[1024,128]{1,0:T(8,128)(2,1)}, bf16[2048,1024]{1,0:T(8,128)(2,1)}, bf16[128,2048]{1,0:T(8,128)(2,1)}) custom-call(bf16[128,2048]{1,0:T(8,128)(2,1)} %copy-done.4, bf16[128,128]{1,0:T(8,128)(2,1)} %select_convert_fusion.refs_1_, bf16[8,16,1024]{2,1,0:T(8,128)(2,1)} %pad_maximum_fusion.2.refs_2_, ...), custom_call_target="tpu_custom_call" | custom-call | tf_op jit(solution)/shard_map/first_gather/pallas_call | solution.py:144
  56.1 0.2 reduce-window.4
  56.3 0.1 fusion.28
  56.4 0.1 fusion.29
  56.5 1.9 multiply_cosine_fusion
  58.4 0.3 maximum_bitcast_fusion
  58.8 1.0 pad_maximum_fusion.refs_2_.refs_6_
  59.8 0.6 broadcast_in_dim.109.refs_3_
  60.4 49.4 %attention_forward.1 = (f32[128,2048]{1,0:T(8,128)}, bf16[1024,256]{1,0:T(8,128)(2,1)}, bf16[1024,256]{1,0:T(8,128)(2,1)}, bf16[1024,256]{1,0:T(8,128)(2,1)}, bf...) custom-call(bf16[1024,2048]{1,0:T(8,128)(2,1)} %get-tuple-element.38, ...), custom_call_target="tpu_custom_call" | custom-call | tf_op jit(solution)/shard_map/attention_forward/pallas_call | solution.py:144
  109.9 1.5 fusion.63
  111.4 0.3 multiply_reduce_fusion.3
  111.7 1.0 multiply_convert_fusion.1.refs_0_
  112.7 56.5 %feed_forward.1 = (f32[128,2048]{1,0:T(8,128)}, bf16[1024,2048]{1,0:T(8,128)(2,1)}, bf16[2048,1024]{1,0:T(8,128)(2,1)}, bf16[2048,1024]{1,0:T(8,128)(2,1)}) custom-call(bf16[128,2048]{1,0:T(8,128)(2,1)} %multiply_convert_fusion.1.refs_0_, bf16[1024,2048]{1,0:T(8,128)(2,1)} %get-tuple-element.43.refs_1_, bf16[2048,2048]{1,0:T(8,128)(2,1)} %get-tuple-element.44.refs_2_, ...), custom_call_target="tpu_custom_call" | custom-call | tf_op jit(solution)/shard_map/feed_forward/pallas_call | solution.py:144
  169.2 1.7 multiply_reduce_fusion
  170.9 0.4 fusion.62
  171.4 1.0 copy-done.2
  172.3 1.1 multiply_convert_fusion.refs_0_
  173.4 85.7 %attention_backward.1 = (f32[128,2048]{1,0:T(8,128)}, f32[128,2048]{1,0:T(8,128)}, bf16[16,24576]{1,0:T(8,128)(2,1)}) custom-call(bf16[128,2048]{1,0:T(8,128)(2,1)} %multiply_convert_fusion.refs_0_, bf16[1024,2048]{1,0:T(8,128)(2,1)} %get-tuple-element.46.refs_1_, bf16[2048,1024]{1,0:T(8,128)(2,1)} %get-tuple-element.47.refs_2_, ...), custom_call_target="tpu_custom_call" | custom-call | tf_op jit(solution)/shard_map/attention_backward/pallas_call | solution.py:144
  259.1 0.0 copy-start.5
  259.1 3.3 fusion.16
  262.4 0.1 fusion.35
  262.6 0.2 fusion.23
  262.8 1.4 fusion.68.refs_0_
  264.3 10.3 %sum_router.1 = f32[256,256]{1,0:T(8,128)} custom-call(bf16[2048,256]{1,0:T(8,128)(2,1)} %fusion.68.refs_0_), custom_call_target="tpu_custom_call" | custom-call | tf_op jit(solution)/shard_map/sum_router/pallas_call | solution.py:144
  274.6 1.6 convert_element_type.73.refs_0_
  276.2 8.2 %small_wide.1.refs_1_ = f32[16,256]{1,0:T(8,128)} custom-call(bf16[256,256]{1,0:T(8,128)(2,1)} %convert_element_type.73.refs_0_), custom_call_target="tpu_custom_call" | custom-call | tf_op jit(solution)/shard_map/small_wide/pallas_call | solution.py:144
  284.4 1.3 multiply_reduce_fusion.5
  285.7 1.0 fusion.3
  288.0 0.2 fusion.24
  288.2 0.1 reshape.195
  288.4 0.0 copy-start.17
  288.4 2.5 fusion.14
  290.9 0.5 fusion.12
  291.4 0.7 concatenate.19
  292.1 27.6 %last_sums.1 = (f32[56,128]{1,0:T(8,128)}, f32[2048,256]{1,0:T(8,128)}) custom-call(f32[56,128]{1,0:T(8,128)} %bitcast.76, f32[16,256]{1,0:T(8,128)} %small_wide.1.refs_1_), custom_call_target="tpu_custom_call" | custom-call | tf_op jit(solution)/shard_map/last_sums/pallas_call | solution.py:144
  319.7 1.3 slice.85
  320.9 1.3 multiply_reduce_fusion.4
  323.5 1.3 multiply_reduce_fusion.6
  325.6 0.7 slice_multiply_fusion.1
  326.3 0.1 mul.571
  326.4 0.1 copy.83
  326.4 0.6 multiply_subtract_fusion.3
  327.1 7.2 %multiply_subtract_fusion = (f32[2048,256]{1,0:T(8,128)}, f32[2048,256]{1,0:T(8,128)}, f32[2048,256]{1,0:T(8,128)}) fusion(f32[2048,256]{1,0:T(8,128)} %param.26, f32[2048,256]{1,0:T(8,128)} %get-tuple-element.58, f32[]{:T(128)S(6)} %min.3, f32[2048,256]{1,0:T(8,128)} %param.27, f32[2048,256]{1,0:T(8,128)} %param.28), kind=kLoop, calls=%fused_computation.5 | loop fusion | flops 8388608 | bytes 14680068 | tf_op jit(solution)/shard_map/sub | solution.py:1111
  334.4 0.7 multiply_subtract_fusion.2
  335.1 5.9 %fusion.59 = (bf16[16,24576]{1,0:T(8,128)(2,1)}, f32[16,24576]{1,0:T(8,128)}, f32[16,24576]{1,0:T(8,128)}, f32[16,24576]{1,0:T(8,128)}) fusion(f32[16,24576]{1,0:T(8,128)} %param.20, f32[]{:T(128)S(6)} %min.3, bf16[16,24576]{1,0:T(8,128)(2,1)} %get-tuple-element.56, f32[16,24576]{1,0:T(8,128)} %param.21, f32[16,24576]{1,0:T(8,128)} %param.22), kind=kLoop, calls=%fused_computation.146 | loop fusion | flops 7077888 | bytes 11010052 | tf_op jit(solution)/shard_map/convert_element_type | solution.py:1256
  341.0 1.9 slice.73
  342.9 1.2 slice.84
  344.1 2.5 add_add_fusion.2
  (63 shorter events, 0.4 us)
Async XLA Ops:
  0.7 5.0 %copy-start.1 = (f32[2048,256]{1,0:T(8,128)S(1)}, f32[2048,256]{1,0:T(8,128)}, u32[]{:S(2)}) copy-start(f32[2048,256]{1,0:T(8,128)} %param.26) | copy-start | bytes 6291460
  2.0 4.0 %copy-start.15 = (f32[256,8]{0,1:T(8,128)S(1)}, f32[256,8]{0,1:T(8,128)}, u32[]{:S(2)}) copy-start(f32[256,8]{0,1:T(8,128)} %param.29) | copy-start | bytes 24580
  4.2 2.1 copy-start.18
  4.2 2.2 copy-start.6
  5.7 1.7 copy-start.4
  5.7 1.7 copy-start.8
  8.2 47.9 %copy-start.19 = (s32[1,2]{1,0:T(1,128)S(1)}, s32[1,2]{1,0:T(1,128)}, u32[]{:S(2)}) copy-start(s32[1,2]{1,0:T(1,128)} %param.17) | copy-start | bytes 28
  60.4 49.4 %copy-start = (bf16[128,2048]{1,0:T(8,128)(2,1)S(1)}, bf16[128,2048]{1,0:T(8,128)(2,1)}, u32[]{:S(2)}) copy-start(bf16[128,2048]{1,0:T(8,128)(2,1)} %param.16) | copy-start | bytes 1572868
  169.2 1.7 copy-start.9
  170.9 1.4 copy-start.7
  171.4 1.0 copy-start.2
  259.1 3.7 %copy-start.5 = (bf16[128,2048]{1,0:T(8,128)(2,1)S(1)}, bf16[128,2048]{1,0:T(8,128)(2,1)}, u32[]{:S(2)}) copy-start(bf16[128,2048]{1,0:T(8,128)(2,1)} %copy-done.4) | copy-start | bytes 1572868
  262.6 23.2 %copy-start.10 = (bf16[16,24576]{1,0:T(8,128)(2,1)S(1)}, bf16[16,24576]{1,0:T(8,128)(2,1)}, u32[]{:S(2)}) copy-start(bf16[16,24576]{1,0:T(8,128)(2,1)} %get-tuple-element.56) | copy-start | bytes 2359300
  288.4 38.1 %copy-start.16 = (f32[256,8]{0,1:T(8,128)S(1)}, f32[256,8]{0,1:T(8,128)}, u32[]{:S(2)}) copy-start(f32[256,8]{0,1:T(8,128)} %param.30) | copy-start | bytes 24580
  288.4 38.1 %copy-start.17 = (f32[256,8]{0,1:T(8,128)S(1)}, f32[256,8]{0,1:T(8,128)}, u32[]{:S(2)}) copy-start(f32[256,8]{0,1:T(8,128)} %param.31) | copy-start | bytes 24580
  327.1 7.2 %copy-start.11 = (f32[56,128]{1,0:T(8,128)S(1)}, f32[56,128]{1,0:T(8,128)}, u32[]{:S(2)}) copy-start(f32[56,128]{1,0:T(8,128)} %get-tuple-element.57) | copy-start | bytes 86020
  327.1 7.3 %copy-start.12 = (f32[2,2048]{1,0:T(2,128)S(1)}, f32[2,2048]{1,0:T(2,128)}, u32[]{:S(2)}) copy-start(f32[2,2048]{1,0:T(2,128)} %param.23) | copy-start | bytes 49156
  327.1 7.3 %copy-start.13 = (f32[2,2048]{1,0:T(2,128)S(1)}, f32[2,2048]{1,0:T(2,128)}, u32[]{:S(2)}) copy-start(f32[2,2048]{1,0:T(2,128)} %param.24) | copy-start | bytes 49156
  327.1 7.3 %copy-start.14 = (f32[2,2048]{1,0:T(2,128)S(1)}, f32[2,2048]{1,0:T(2,128)}, u32[]{:S(2)}) copy-start(f32[2,2048]{1,0:T(2,128)} %param.25) | copy-start | bytes 49156
  335.1 9.0 %copy-start.3 = (f32[128,2048]{1,0:T(8,128)S(1)}, f32[128,2048]{1,0:T(8,128)}, u32[]{:S(2)}) copy-start(f32[128,2048]{1,0:T(8,128)} %copy-done.2) | copy-start | bytes 3145732

commit v4 on v3

v4 whole, which is shorter than its diff:
```python
import functools

import jax
import jax.numpy as jnp
from jax import lax
from jax.experimental import pallas as pl
from jax.experimental.pallas import tpu as pltpu
from jax.sharding import PartitionSpec as P

D = 2048
HEADS = 16
HEAD_DIM = 128
FF = 8192
RH = 256
LEVELS = 4
STEP = 10
TOK = 128
GROUP = 1024
SIDE = 4
WIDE = 16
NARROW = 8
ROWS = 16

NORM_EPS = 1e-05
CLIP_NORM = 1.0
CONTRACT_COLS = (((1,), (1,)), ((), ()))
CONTRACT_ROWS = (((0,), (0,)), ((), ()))
MESH = pl.DeviceIdType.MESH
BF = jnp.bfloat16
F32 = jnp.float32


FORWARD_PLAN = (
    "sa", "gm", "sb", "sa", "wa", "gx", "wa", "gx", "gm", "gm", "wa", "wa", "sb", "gm", "gx",
    "wa", "gg", "gm", "wa", "wb", "gx", "gx", "gx", "gm", "wa", "Q", "wb", "gg", "T2", "T1",
    "gg", "wb", "total", "gg", "T3", "total", "wb", "T0", "gg", "total", "wb", "gx", "total",
    "gm", "total", "wb", "total", "wb", "gg", "total", "wa", "gg",
)
FEED_PLAN = (
    "gather", "gather", "DA", "U0", "gather", "gather", "U3", "gather", "U1", "gather", "U2",
    "N2", "GD", "total", "N1", "wide", "N3", "total", "N0", "DS", "total", "YF", "total",
    "wide", "GU", "total", "gather", "DT", "total", "wide", "total",
)
BACKWARD_PLAN = (
    "gather", "up", "gates", "gather", "up", "LD", "gather", "down", "feed", "feed", "P0",
    "gather", "P3", "gates", "P1", "feed", "up", "gather", "down", "gather", "P2", "feed", "up",
    "RT", "gates", "GO", "GQ", "up", "gather", "gates", "mixed", "down", "N2", "feed", "N0",
    "total", "N3", "down", "N1", "feed", "up", "up", "mixed", "gates", "total", "total",
    "total", "gates", "total", "down", "mixed", "mixed", "mixed", "gates", "total", "gates",
    "total", "mixed",
)


def here():
    w = lax.axis_index("wide")
    n = lax.axis_index("narrow")
    return lax.div(w, SIDE), lax.rem(w, SIDE), lax.div(n, 2), lax.rem(n, 2)


def wrap(i):
    return lax.rem(i + 2 * SIDE, SIDE)


def moved(dx=0, dz=0, dy=0, dc=0):
    x, z, y, c = here()
    return (wrap(x + dx) * SIDE + wrap(z + dz), wrap(y + dy) * 2 + lax.rem(c + dc, 2))


NEAR_Y = [dict(dy=1), dict(dy=-1), dict(dc=1)]
NARROW_ALL = [dict(dy=a, dc=b) for a in range(SIDE) for b in range(2) if a or b]
NEAR_XZ = [dict(dx=1), dict(dx=-1), dict(dz=1), dict(dz=-1)]
LINES_XZ = [dict(dx=a) for a in (1, 2, 3)] + [dict(dz=a) for a in (1, 2, 3)]
WIDE_ALL = [dict(dx=a, dz=b) for a in range(SIDE) for b in range(SIDE) if a or b]


def greet(partners):
    barrier = pltpu.get_barrier_semaphore()
    for p in partners:
        pl.semaphore_signal(barrier, inc=1, device_id=moved(**p), device_id_type=MESH)
    pl.semaphore_wait(barrier, len(partners))


def span(start, size):
    if not isinstance(start, int):
        start = pl.multiple_of(start, ROWS)
    return pl.ds(start, size)


def lanes(start, size):
    if not isinstance(start, int):
        start = pl.multiple_of(start, 128)
    return pl.ds(start, size)


def step(*parts):
    for part in parts:
        next(part, None)


class Net:
    def __init__(self, send, recv, local):
        self.send, self.recv, self.local = send, recv, local
        self.used, self.used_local = 0, 0
        self.sent = []

    def put(self, src, dst, target):
        i = self.used
        self.used += 1
        copy = pltpu.make_async_remote_copy(
            src_ref=src,
            dst_ref=dst,
            send_sem=self.send.at[i],
            recv_sem=self.recv.at[i],
            device_id=target,
            device_id_type=MESH,
        )
        copy.start()
        self.sent.append(copy)
        return copy

    def keep(self, src, dst):
        i = self.used_local
        self.used_local += 1
        copy = pltpu.make_async_copy(src, dst, self.local.at[i])
        copy.start()
        return copy

    def sent_by(self, *copies):
        for copy in copies:
            copy.wait_send()
        done = [id(copy) for copy in copies]
        self.sent = [copy for copy in self.sent if id(copy) not in done]

    def finish(self):
        for copy in self.sent:
            copy.wait_send()


def take_turns(*parts):
    live = list(parts)
    while live:
        still = []
        for part in live:
            try:
                next(part)
                still.append(part)
            except StopIteration:
                pass
        live = still


def follow(plan, works, moves):
    for name in plan:
        if name in works:
            works[name]()
        else:
            next(moves[name], None)
    take_turns(*moves.values())


def comm_call(body, ins, outs, scratch, cid, copies, locals_, name, flops=0):
    n_in, n_out, n_scr = len(ins), len(outs), len(scratch)

    def kernel(*refs):
        in_refs = refs[:n_in]
        out_refs = refs[n_in : n_in + n_out]
        scr = refs[n_in + n_out : n_in + n_out + n_scr]
        send, recv, local = refs[n_in + n_out + n_scr :]
        net = Net(send, recv, local)
        body(net, in_refs, out_refs, scr)
        net.finish()
        assert net.used <= copies and net.used_local <= locals_, (net.used, net.used_local)

    return pl.pallas_call(
        kernel,
        out_shape=outs,
        in_specs=[pl.BlockSpec(memory_space=pl.ANY)] * n_in,
        out_specs=[pl.BlockSpec(memory_space=pl.ANY)] * n_out,
        scratch_shapes=list(scratch)
        + [
            pltpu.SemaphoreType.DMA((copies,)),
            pltpu.SemaphoreType.DMA((copies,)),
            pltpu.SemaphoreType.DMA((max(locals_, 1),)),
        ],
        compiler_params=pltpu.CompilerParams(
            collective_id=cid, has_side_effects=True, vmem_limit_bytes=63 * 2**20
        ),
        name=name,
    )(*ins)


def gather_narrow(net, own, out):
    x, z, y, c = here()
    rows = own.shape[0]
    half = rows // 2

    def block(dy, lo=0, size=rows):
        return out.at[span((wrap(y + dy) * 2 + c) * rows + lo, size)]

    first, last = own.at[pl.ds(0, half)], own.at[pl.ds(half, half)]
    up = net.put(first, block(0, 0, half), moved(dy=1))
    down = net.put(last, block(0, half, half), moved(dy=-1))
    up_late = net.put(last, block(0, half, half), moved(dy=1))
    down_late = net.put(first, block(0, 0, half), moved(dy=-1))
    across = [net.put(own, block(0), moved(dc=1))]
    mine = net.keep(own, block(0))
    yield
    mine.wait()
    across[0].wait_recv()
    yield
    up.wait_recv()
    on = net.put(block(-1, 0, half), block(-1, 0, half), moved(dy=1))
    down.wait_recv()
    back = net.put(block(1, half, half), block(1, half, half), moved(dy=-1))
    yield
    up_late.wait_recv()
    across.append(net.put(block(-1), block(-1), moved(dc=1)))
    down_late.wait_recv()
    across.append(net.put(block(1), block(1), moved(dc=1)))
    across[1].wait_recv()
    across[2].wait_recv()
    yield
    on.wait_recv()
    across.append(net.put(block(2, 0, half), block(2, 0, half), moved(dc=1)))
    back.wait_recv()
    across.append(net.put(block(2, half, half), block(2, half, half), moved(dc=1)))
    yield
    across[3].wait_recv()
    across[4].wait_recv()
    yield
    net.sent_by(up, down, up_late, down_late, on, back, *across)


GATHER_COPIES = 12


def gather_small(net, own, out):
    c = here()[3]
    y = here()[2]
    rows = own.shape[0]

    def block(dy):
        return out.at[span((wrap(y + dy) * 2 + c) * rows, rows)]

    along = [net.put(own, block(0), moved(dy=d)) for d in (2, 1, 3)]
    across = [net.put(own, block(0), moved(dc=1))]
    mine = net.keep(own, block(0))
    yield
    for copy, d in zip(along, (2, 1, 3)):
        copy.wait_recv()
        across.append(net.put(block(-d), block(-d), moved(dc=1)))
    yield
    mine.wait()
    for copy in across:
        copy.wait_recv()


GATHER_SMALL_COPIES = 7


def gather_call(own, cid, name):
    rows, cols = own.shape

    def body(net, ins, outs, scr):
        greet(NEAR_Y)
        take_turns(gather_narrow(net, ins[0], outs[0]))

    return comm_call(
        body,
        [own],
        [jax.ShapeDtypeStruct((NARROW * rows, cols), own.dtype)],
        [],
        cid,
        GATHER_COPIES,
        1,
        name,
    )[0]


def reduce_scratch(rows, cols):
    return [
        pltpu.VMEM((SIDE, rows, cols), BF),
        pltpu.VMEM((SIDE, rows, cols), BF),
        pltpu.VMEM((2, rows // 2, cols), BF),
        pltpu.VMEM((2, rows, cols), BF),
        pltpu.VMEM((3, rows, cols), BF),
        pltpu.VMEM((rows, cols), F32),
    ]


REDUCE_COPIES = 10
REDUCE_LOCALS = 5


def reduce_narrow(net, part, out, scr):
    own, other, through, landed, ready, total = scr
    x, z, y, c = here()
    rows, cols = out.shape
    half = rows // 2

    def block(dy, core):
        return part.at[span((wrap(y + dy) * 2 + core) * rows, rows)]

    order = (2, 1, 3, 0)
    local, cross = {}, {}
    for dy in order:
        cross[dy] = net.put(block(dy, 1 - c), other.at[dy], moved(dc=1))
        local[dy] = net.keep(block(dy, c), own.at[dy])

    def pair(dy, lo, size):
        s = span(lo, size)
        return own[dy, s, :].astype(F32) + other[dy, s, :].astype(F32)

    yield
    local[2].wait()
    cross[2].wait_recv()
    ready[0] = pair(2, 0, rows).astype(BF)
    first, last = span(0, half), span(half, half)
    via_up = net.put(ready.at[0, first], through.at[0], moved(dy=1))
    via_down = net.put(ready.at[0, last], through.at[1], moved(dy=-1))
    yield
    local[1].wait()
    cross[1].wait_recv()
    ready[1, last, :] = pair(1, half, half).astype(BF)
    up_late = net.put(ready.at[1, last], landed.at[0, last], moved(dy=1))
    local[3].wait()
    cross[3].wait_recv()
    ready[2, first, :] = pair(3, 0, half).astype(BF)
    down_first = net.put(ready.at[2, first], landed.at[1, first], moved(dy=-1))
    yield
    via_up.wait_recv()
    ready[1, first, :] = (pair(1, 0, half) + through[0].astype(F32)).astype(BF)
    up_first = net.put(ready.at[1, first], landed.at[0, first], moved(dy=1))
    via_down.wait_recv()
    ready[2, last, :] = (pair(3, half, half) + through[1].astype(F32)).astype(BF)
    down_late = net.put(ready.at[2, last], landed.at[1, last], moved(dy=-1))
    yield
    local[0].wait()
    cross[0].wait_recv()
    total[...] = pair(0, 0, rows)
    yield
    for copy in (up_late, down_first, up_first, down_late):
        copy.wait_recv()
    total[...] += landed[0].astype(F32) + landed[1].astype(F32)
    done = net.keep(total, out)
    yield
    done.wait()


def pairs_scratch(rows, cols):
    return [
        pltpu.VMEM((SIDE * 2 * rows, cols), BF),
        pltpu.VMEM((SIDE, rows, cols), BF),
        pltpu.VMEM((2, rows // 2, cols), BF),
        pltpu.VMEM((2, rows, cols), BF),
        pltpu.VMEM((3, rows, cols), BF),
        pltpu.VMEM((rows, cols), F32),
    ]


PAIR_ORDER = (2, 1, 3, 0)


class Pairs:
    def __init__(self, net, out, scr):
        self.net, self.out, self.scr = net, out, scr
        self.crossed = {}

    def store(self, dy, value):
        rows = value.shape[0]
        self.scr[0][pl.ds(dy * rows, rows), :] = value.astype(BF)

    def cross(self, dy):
        parts, other = self.scr[:2]
        c = here()[3]
        rows = other.shape[1]
        self.crossed[dy] = self.net.put(
            parts.at[span((2 * dy + 1 - c) * rows, rows)], other.at[dy], moved(dc=1)
        )

    def steps(self):
        net = self.net
        parts, other, through, landed, ready, total = self.scr
        c = here()[3]
        rows = total.shape[0]
        half = rows // 2
        first, last = pl.ds(0, half), pl.ds(half, half)

        def pair(dy, lo, size):
            mine = parts[span((2 * dy + c) * rows + lo, size), :].astype(F32)
            return mine + other[dy, pl.ds(lo, size), :].astype(F32)

        self.crossed[2].wait_recv()
        ready[0] = pair(2, 0, rows).astype(BF)
        via_up = net.put(ready.at[0, first], through.at[0], moved(dy=1))
        via_down = net.put(ready.at[0, last], through.at[1], moved(dy=-1))
        yield
        self.crossed[1].wait_recv()
        ready[1, last, :] = pair(1, half, half).astype(BF)
        up_late = net.put(ready.at[1, last], landed.at[0, last], moved(dy=1))
        yield
        self.crossed[3].wait_recv()
        ready[2, first, :] = pair(3, 0, half).astype(BF)
        down_first = net.put(ready.at[2, first], landed.at[1, first], moved(dy=-1))
        yield
        via_up.wait_recv()
        ready[1, first, :] = (pair(1, 0, half) + through[0].astype(F32)).astype(BF)
        up_first = net.put(ready.at[1, first], landed.at[0, first], moved(dy=1))
        via_down.wait_recv()
        ready[2, last, :] = (pair(3, half, half) + through[1].astype(F32)).astype(BF)
        down_late = net.put(ready.at[2, last], landed.at[1, last], moved(dy=-1))
        yield
        self.crossed[0].wait_recv()
        total[...] = pair(0, 0, rows)
        yield
        for copy in (up_late, down_first, up_first, down_late):
            copy.wait_recv()
        total[...] += landed[0].astype(F32) + landed[1].astype(F32)
        done = net.keep(total, self.out)
        yield
        done.wait()


def spread_narrow(net, src, slab):
    w = lax.axis_index("wide")
    n = lax.axis_index("narrow")
    base = n * ROWS if slab.shape[0] == TOK else w * TOK + n * ROWS
    mine = net.keep(src.at[n], slab.at[span(base, ROWS)])
    copies = []
    for p in NARROW_ALL:
        target = moved(**p)
        copies.append(net.put(src.at[target[1]], slab.at[span(base, ROWS)], target))
    yield
    mine.wait()
    for copy in copies:
        copy.wait_recv()


SPREAD_COPIES = 7


def gather_wide(net, slab, lead, stage=None):
    x, z, y, c = here()
    rows = TOK // 2
    half = rows // 2
    low = 0 if lead == "x" else rows

    def block(a, b, lo=0, size=rows):
        px, pz = (a, b) if lead == "x" else (b, a)
        return slab.at[span((wrap(x + px) * SIDE + wrap(z + pz)) * TOK + low + lo, size)]

    def lead_to(d):
        return moved(dx=d) if lead == "x" else moved(dz=d)

    def then_to(d):
        return moved(dz=d) if lead == "x" else moved(dx=d)

    def both(src, to, dst=None):
        dst = src if dst is None else dst
        return net.put(src, dst, to(1)), net.put(src, dst, to(-1))

    mine = block(0, 0) if stage is None else stage.at[pl.ds(low, rows)]
    fore, aft = both(mine, lead_to, block(0, 0))
    second = {0: both(mine, then_to, block(0, 0))}
    yield
    fore.wait_recv()
    on = net.put(block(-1, 0, 0, half), block(-1, 0, 0, half), lead_to(1))
    second[-1] = both(block(-1, 0), then_to)
    aft.wait_recv()
    back = net.put(block(1, 0, half, half), block(1, 0, half, half), lead_to(-1))
    second[1] = both(block(1, 0), then_to)
    yield
    last = []

    def relay(a):
        f, b = second[a]
        f.wait_recv()
        last.append(net.put(block(a, -1, 0, half), block(a, -1, 0, half), then_to(1)))
        b.wait_recv()
        last.append(net.put(block(a, 1, half, half), block(a, 1, half, half), then_to(-1)))

    kept = None if stage is None else net.keep(mine, block(0, 0))
    relay(0)
    yield
    on.wait_recv()
    back.wait_recv()
    second[2] = both(block(2, 0), then_to)
    yield
    relay(-1)
    relay(1)
    yield
    relay(2)
    yield
    if kept is not None:
        kept.wait()
    for copy in last:
        copy.wait_recv()


WIDE_COPIES = 20


def turn(values, cosine, sine):
    return values * cosine + pltpu.roll(values, HEAD_DIM // 2, 1) * sine


def allowed_keys(first_row, rows, first_length):
    query = first_row + lax.broadcasted_iota(jnp.int32, (rows, 1), 0)
    key = lax.broadcasted_iota(jnp.int32, (rows, GROUP), 1)
    start = jnp.where(query >= first_length, first_length, 0)
    return (key <= query) & (key >= start)


PICK_ATTN, PICK_FFN, GATE_FFN = 0, 32, 64


def branch_mask(marks, lane):
    n = lax.axis_index("narrow").astype(F32)
    return (n < 2.0 * (marks[:, lane : lane + 1] + 1.0)).astype(F32)


def attention_forward(normed_own, source_a, source_b, turns, first_length, marks, upstream, cid):
    pair_rows = 2 * TOK
    head_part = D // NARROW

    def body(net, ins, outs, scr):
        normed_own, source_a, source_b, turns, first_length, marks, upstream = ins
        attn_sum, q_out, k_out, v_out, p_out, a_out, g_out, slab_a, slab_b, normed, marks_out = outs
        xv, wv, tv, lv, mv, qv, kv, vv, pv, av = scr[:10]
        stage = scr[-1]
        x, z, y, c = here()
        loads = [net.keep(turns, tv), net.keep(first_length, lv)]
        greet(NARROW_ALL + NEAR_XZ)
        sums = Pairs(net, attn_sum, scr[10:16])
        stores = []
        moves = dict(
            sa=spread_narrow(net, source_a, wv),
            sb=spread_narrow(net, source_b, stage),
            gx=gather_narrow(net, normed_own, xv),
            gm=gather_narrow(net, marks, mv),
            gg=gather_narrow(net, upstream, g_out),
            wa=side_by_side(*[gather_wide(net, wv, lead) for lead in "xz"]),
            wb=side_by_side(*[gather_wide(net, slab_b, lead, stage) for lead in "xz"]),
            total=sums.steps(),
        )

        def project():
            stores.extend([net.keep(xv, normed), net.keep(wv, slab_a)])
            for load in loads:
                load.wait()

            @pl.loop(0, SIDE)
            def _(i):
                r = span(i * pair_rows, pair_rows)
                proj = jnp.dot(xv[r, :], wv[:, : 3 * head_part], preferred_element_type=F32)
                cosine, sine = tv[0, r, :], tv[1, r, :]
                for h in range(2):
                    at = pl.ds(h * HEAD_DIM, HEAD_DIM)
                    a = h * HEAD_DIM
                    qv[r, at] = turn(proj[:, a : a + HEAD_DIM], cosine, sine).astype(BF)
                    a += head_part
                    kv[r, at] = turn(proj[:, a : a + HEAD_DIM], cosine, sine).astype(BF)
                vv[r, :] = proj[:, 2 * head_part :].astype(BF)

            stores.extend([net.keep(qv, q_out), net.keep(kv, k_out), net.keep(vv, v_out)])

        def attend(dy):
            first = wrap(y + dy) * pair_rows
            r = span(first, pair_rows)
            allowed = allowed_keys(first, pair_rows, lv[0:1, 0:1])
            heads = []
            for h in range(2):
                at = pl.ds(h * HEAD_DIM, HEAD_DIM)
                scores = lax.dot_general(
                    qv[r, at], kv[:, at], CONTRACT_COLS, preferred_element_type=F32
                )
                scores = jnp.where(allowed, scores * HEAD_DIM ** (-0.5), -1e30)
                expo = jnp.exp(scores - jnp.max(scores, axis=-1, keepdims=True))
                probs = expo * (1.0 / jnp.sum(expo, axis=-1, keepdims=True))
                low = probs.astype(BF)
                pv[r, pl.ds(h * GROUP, GROUP)] = low
                heads.append(jnp.dot(low, vv[:, at], preferred_element_type=F32))
            mask = branch_mask(mv[r, :], PICK_ATTN)
            av[r, :] = (jnp.concatenate(heads, axis=1) * mask).astype(BF)
            back = lax.dot_general(
                av[r, :], wv[:, 3 * head_part :], CONTRACT_COLS, preferred_element_type=F32
            )
            sums.store(dy, back)
            sums.cross(dy)

        works = dict(Q=project)
        for dy in PAIR_ORDER:
            works[f"T{dy}"] = functools.partial(attend, dy)
        follow(FORWARD_PLAN, works, moves)
        stores += [net.keep(pv, p_out), net.keep(av, a_out), net.keep(mv, marks_out)]
        for store in stores:
            store.wait()

    low = jax.ShapeDtypeStruct((GROUP, head_part), BF)
    return comm_call(
        body,
        [normed_own, source_a, source_b, turns, first_length, marks, upstream],
        [
            jax.ShapeDtypeStruct((TOK, D), F32),
            low,
            low,
            low,
            jax.ShapeDtypeStruct((GROUP, 2 * GROUP), BF),
            low,
            jax.ShapeDtypeStruct((GROUP, D), BF),
            jax.ShapeDtypeStruct((D, source_a.shape[2]), BF),
            jax.ShapeDtypeStruct((D, source_b.shape[2]), BF),
            jax.ShapeDtypeStruct((GROUP, D), BF),
            jax.ShapeDtypeStruct((GROUP, 128), F32),
        ],
        [
            pltpu.VMEM((GROUP, D), BF),
            pltpu.VMEM((D, source_a.shape[2]), BF),
            pltpu.VMEM(turns.shape, F32),
            pltpu.VMEM(first_length.shape, jnp.int32),
            pltpu.VMEM((GROUP, 128), F32),
            pltpu.VMEM((GROUP, head_part), BF),
            pltpu.VMEM((GROUP, head_part), BF),
            pltpu.VMEM((GROUP, head_part), BF),
            pltpu.VMEM((GROUP, 2 * GROUP), BF),
            pltpu.VMEM((GROUP, head_part), BF),
        ]
        + pairs_scratch(TOK, D)
        + [pltpu.VMEM((TOK, source_b.shape[2]), BF)],
        cid,
        REDUCE_COPIES + 4 * WIDE_COPIES + 3 * GATHER_COPIES + 2 * SPREAD_COPIES,
        2 + 2 + 3 + 2 + 2 + 3 + 1 + 2 + 1,
        "attention_forward",
    )


def first_scratch(cols):
    part, half = TOK // 2, TOK // 4
    return [
        pltpu.VMEM((2, 2, SIDE, half, cols), BF),
        pltpu.VMEM((2, 2, SIDE, part, cols), BF),
        pltpu.VMEM((2, 2, SIDE, half, cols), BF),
        pltpu.VMEM((2, SIDE, part, cols), BF),
    ]


def second_scratch(cols):
    part, half = TOK // 2, TOK // 4
    return [
        pltpu.VMEM((2, 2, half, cols), BF),
        pltpu.VMEM((2, 2, part, cols), BF),
        pltpu.VMEM((2, 2, half, cols), BF),
        pltpu.VMEM((TOK, cols), BF),
    ]


FIRST_COPIES = 12
SECOND_COPIES = 12
FIRST_LOCALS = 6


def lead_moves(lead):
    def lead_to(d):
        return moved(dx=d) if lead == "x" else moved(dz=d)

    def then_to(d):
        return moved(dz=d) if lead == "x" else moved(dx=d)

    return lead_to, then_to


def reduce_first(net, grad, scr, lead):
    via, landed, ready, sums = scr
    x, z, y, c = here()
    part, half = TOK // 2, TOK // 4
    k = 0 if lead == "x" else 1
    low = k * part
    blocks = grad.reshape(SIDE, SIDE, TOK, grad.shape[1])
    first, last = pl.ds(0, half), pl.ds(half, half)
    lead_to, _ = lead_moves(lead)

    def line(d, lo, size):
        rows = pl.ds(low + lo, size)
        if lead == "x":
            return (wrap(x + d), slice(None), rows, slice(None))
        return (slice(None), wrap(z + d), rows, slice(None))

    via_up = net.put(blocks.at[line(2, 0, half)], via.at[k, 0], lead_to(1))
    via_down = net.put(blocks.at[line(2, half, half)], via.at[k, 1], lead_to(-1))
    up_late = net.put(blocks.at[line(1, half, half)], landed.at[k, 0, :, last], lead_to(1))
    down_first = net.put(blocks.at[line(3, 0, half)], landed.at[k, 1, :, first], lead_to(-1))
    loads = [
        net.keep(blocks.at[line(1, 0, half)], ready.at[k, 0]),
        net.keep(blocks.at[line(3, half, half)], ready.at[k, 1]),
        net.keep(blocks.at[line(0, 0, part)], sums.at[k]),
    ]
    yield
    for load in loads:
        load.wait()
    via_up.wait_recv()

    @pl.loop(0, SIDE)
    def _(i):
        ready[k, 0, i] = (ready[k, 0, i].astype(F32) + via[k, 0, i].astype(F32)).astype(BF)

    up_first = net.put(ready.at[k, 0], landed.at[k, 0, :, first], lead_to(1))
    via_down.wait_recv()

    @pl.loop(0, SIDE)
    def _(i):
        ready[k, 1, i] = (ready[k, 1, i].astype(F32) + via[k, 1, i].astype(F32)).astype(BF)

    down_late = net.put(ready.at[k, 1], landed.at[k, 1, :, last], lead_to(-1))
    yield
    for copy in (up_late, down_first, up_first, down_late):
        copy.wait_recv()

    @pl.loop(0, SIDE)
    def _(i):
        both = landed[k, 0, i].astype(F32) + landed[k, 1, i].astype(F32)
        sums[k, i] = (sums[k, i].astype(F32) + both).astype(BF)


def reduce_second(net, sums, scr, lead):
    via, landed, ready, total = scr
    x, z, y, c = here()
    part, half = TOK // 2, TOK // 4
    k = 0 if lead == "x" else 1
    first, last = pl.ds(0, half), pl.ds(half, half)
    _, then_to = lead_moves(lead)
    me = z if lead == "x" else x

    def block(d, rows):
        return sums.at[k, wrap(me + d), rows]

    via_up = net.put(block(2, first), via.at[k, 0], then_to(1))
    via_down = net.put(block(2, last), via.at[k, 1], then_to(-1))
    up_late = net.put(block(1, last), landed.at[k, 0, last], then_to(1))
    down_first = net.put(block(3, first), landed.at[k, 1, first], then_to(-1))
    yield
    via_up.wait_recv()
    ready[k, 0] = (block(1, first)[...].astype(F32) + via[k, 0].astype(F32)).astype(BF)
    up_first = net.put(ready.at[k, 0], landed.at[k, 0, first], then_to(1))
    via_down.wait_recv()
    ready[k, 1] = (block(3, last)[...].astype(F32) + via[k, 1].astype(F32)).astype(BF)
    down_late = net.put(ready.at[k, 1], landed.at[k, 1, last], then_to(-1))
    yield
    for copy in (up_late, down_first, up_first, down_late):
        copy.wait_recv()
    both = landed[k, 0].astype(F32) + landed[k, 1].astype(F32)
    total[pl.ds(k * part, part), :] = (sums[k, me].astype(F32) + both).astype(BF)


def side_by_side(*parts):
    while True:
        if StopIteration in [next(part, StopIteration) for part in parts]:
            break
        yield


def return_narrow(net, total, out, pieces):
    n = lax.axis_index("narrow")
    copies, mine = [], []
    for start, width, to in pieces:
        spot = out.at[:, lanes(to + n * width, width)]
        columns = pl.ds(start, width)
        for p in NARROW_ALL:
            target = moved(**p)
            copies.append(net.put(total.at[span(target[1] * ROWS, ROWS), columns], spot, target))
        mine.append(net.keep(total.at[span(n * ROWS, ROWS), columns], spot))
    yield
    for copy in mine:
        copy.wait()
    for copy in copies:
        copy.wait_recv()


def second_then_narrow(net, sums, out, scr, pieces):
    yield from side_by_side(*[reduce_second(net, sums, scr, lead) for lead in "xz"])
    yield from return_narrow(net, scr[3], out, pieces)


def wide_then_narrow(net, grad, out, scr, pieces):
    yield from side_by_side(*[reduce_first(net, grad, scr[:4], lead) for lead in "xz"])
    yield from second_then_narrow(net, scr[3], out, scr[4:], pieces)


def feed_forward(normed_own, upstream, slab, marks, cid):
    pair_rows = 2 * TOK
    units = FF // NARROW
    strip = 256

    def body(net, ins, outs, scr):
        own, upstream, slab, marks = ins
        norm_sum, ffn_part, g_up, down_sums, gate_out = outs
        xv, dv, w_up, w_down, mv, act, du, da, gu, gd, yv = scr[:11]
        gated, dots, dots_in, dots_sum = scr[17:21]
        n = lax.axis_index("narrow")
        x, z, y, c = here()
        loads = [
            net.keep(upstream, dv),
            net.keep(slab.at[:, pl.ds(units, units)], w_down),
            net.keep(slab.at[:, pl.ds(0, units)], w_up),
            net.keep(marks, mv),
        ]
        greet(NARROW_ALL + NEAR_XZ)
        sums = Pairs(net, norm_sum, scr[11:17])
        ones = jnp.ones((8, units), BF)
        stores, dot_copies = [], []

        def gradient(left, right, to):
            @pl.loop(0, D // strip)
            def _(i):
                at = lanes(i * strip, strip)
                to[span(i * strip, strip), :] = lax.dot_general(
                    left[:, at], right[...], CONTRACT_ROWS, preferred_element_type=F32
                ).astype(BF)

        def down_back():
            loads[0].wait()
            loads[1].wait()

            @pl.loop(0, SIDE)
            def _(i):
                r = span(i * pair_rows, pair_rows)
                da[r, :] = jnp.dot(dv[r, :], w_down[...], preferred_element_type=F32)

            loads[2].wait()
            loads[3].wait()

        def units_of(dy):
            r = span(wrap(y + dy) * pair_rows, pair_rows)
            up = jnp.dot(xv[r, :], w_up[...], preferred_element_type=F32)
            positive = jnp.maximum(up, 0.0)
            masked = positive * branch_mask(mv[r, :], PICK_FFN)
            gate = mv[r, GATE_FFN : GATE_FFN + 1]
            active = positive * masked
            act[r, :] = active.astype(BF)
            gated[r, :] = (active * gate).astype(BF)
            back = da[r, :]
            du[r, :] = (back * (2.0 * gate * masked)).astype(BF)
            dot = lax.dot_general(
                ones, (back * active).astype(BF), CONTRACT_COLS, preferred_element_type=F32
            )
            for core in range(2):
                dots[wrap(y + dy) * 2 + core] = dot[:, core * TOK : (core + 1) * TOK]

        def norm_back(dy):
            r = span(wrap(y + dy) * pair_rows, pair_rows)
            back = lax.dot_general(
                du[r, :], w_up[...], CONTRACT_COLS, preferred_element_type=F32
            )
            sums.store(dy, back)
            sums.cross(dy)

        def send_dots():
            for p in NARROW_ALL:
                target = moved(**p)
                dot_copies.append(net.put(dots.at[target[1]], dots_in.at[n], target))
            dots_in[n] = dots[n]

        def up_gradient():
            gradient(xv, du, gu)
            stores.append(net.keep(gu, g_up))

        def output():
            @pl.loop(0, SIDE)
            def _(i):
                r = span(i * pair_rows, pair_rows)
                yv[r, :] = lax.dot_general(
                    act[r, :], w_down[...], CONTRACT_COLS, preferred_element_type=F32
                ).astype(BF)

            stores.append(net.keep(yv, ffn_part))

        def take_dots():
            for copy in dot_copies:
                copy.wait_recv()
            s = dots_in[0]
            for i in range(1, NARROW):
                s = s + dots_in[i]
            dots_sum[...] = s
            stores.append(net.keep(dots_sum, gate_out))

        works = dict(
            DA=down_back,
            GD=functools.partial(gradient, dv, gated, gd),
            GU=up_gradient,
            YF=output,
            DS=send_dots,
            DT=take_dots,
        )
        for dy in PAIR_ORDER:
            works[f"U{dy}"] = functools.partial(units_of, dy)
            works[f"N{dy}"] = functools.partial(norm_back, dy)
        moves = dict(
            gather=gather_narrow(net, own, xv),
            total=sums.steps(),
            wide=side_by_side(*[reduce_first(net, gd, scr[21:], lead) for lead in "xz"]),
        )
        follow(FEED_PLAN, works, moves)
        stores.append(net.keep(scr[24], down_sums))
        for store in stores:
            store.wait()

    wide = pltpu.VMEM((GROUP, D), BF)
    tall = pltpu.VMEM((D, units), BF)
    square = pltpu.VMEM((GROUP, units), BF)
    return comm_call(
        body,
        [normed_own, upstream, slab, marks],
        [
            jax.ShapeDtypeStruct((TOK, D), F32),
            jax.ShapeDtypeStruct((GROUP, D), BF),
            jax.ShapeDtypeStruct((D, units), BF),
            jax.ShapeDtypeStruct((2, SIDE, TOK // 2, units), BF),
            jax.ShapeDtypeStruct((8, TOK), F32),
        ],
        [wide, wide, tall, tall, pltpu.VMEM(marks.shape, F32), square, square]
        + [pltpu.VMEM((GROUP, units), F32), tall, tall, wide]
        + pairs_scratch(TOK, D)
        + [square]
        + [pltpu.VMEM((NARROW, 8, TOK), F32)] * 2
        + [pltpu.VMEM((8, TOK), F32)]
        + first_scratch(units),
        cid,
        GATHER_COPIES + REDUCE_COPIES + 7 + FIRST_COPIES,
        4 + 1 + 1 + 4 + FIRST_LOCALS,
        "feed_forward",
    )


def attention_backward(d_attn_own, ffn_part, g_up, down_sums, normed, hidden_own, kept, cid):
    table_rows = D // NARROW
    pair_rows = 2 * TOK
    head_part = D // NARROW
    units = FF // NARROW
    strip = 256
    scale = HEAD_DIM ** (-0.5)
    scratch = (
        [pltpu.VMEM(r.shape, r.dtype) for r in kept]
        + [
            pltpu.VMEM((GROUP, D), BF),
            pltpu.VMEM((GROUP, head_part), F32),
            pltpu.VMEM((GROUP, head_part), F32),
            pltpu.VMEM((GROUP, 3 * head_part), BF),
            pltpu.VMEM((D, 4 * head_part), BF),
        ]
        + pairs_scratch(TOK, D)[1:]
        + reduce_scratch(TOK, D)
        + first_scratch(4 * head_part)
        + second_scratch(4 * head_part)
        + first_scratch(units)
        + second_scratch(units)
        + [pltpu.VMEM(down_sums.shape, BF)]
        + second_scratch(units)
        + [
            pltpu.VMEM((GROUP, table_rows), BF),
            pltpu.VMEM((GROUP, RH), BF),
            pltpu.VMEM((table_rows, RH), BF),
            pltpu.VMEM((WIDE, ROWS, RH), BF),
            pltpu.VMEM((ROWS, RH), BF),
            pltpu.VMEM((table_rows, RH), BF),
        ]
    )

    def body(net, ins, outs, scr):
        d_attn_own, ffn_part, g_up, down_sums, normed, hidden_own = ins[:6]
        norm_sum, ffn_sum, block, table = outs
        wv, tv, mv, qv, kv, vv, pv, av = scr[:8]
        big, dk, dv, dproj, ga = scr[8:13]
        pairs, narrow = [big, *scr[13:18]], scr[18:24]
        wide_a, wide_up, wide_down = scr[24:32], scr[32:40], scr[40:45]
        columns, hidden, part, landed, shard, mine = scr[45:51]
        n = lax.axis_index("narrow")
        x, z, y, c = here()
        first_load = net.keep(down_sums, wide_down[0])
        loads = [net.keep(a, b) for a, b in zip(ins[6:], scr[:8])]
        loads.append(net.keep(normed.at[:, lanes(n * table_rows, table_rows)], columns))
        greet(NARROW_ALL + WIDE_ALL)
        sums = Pairs(net, norm_sum, pairs)
        quarter = [(i * head_part, head_part, i * D) for i in range(4)]

        def router():
            yield from gather_small(net, hidden_own, hidden)
            w = lax.axis_index("wide")
            part[...] = lax.dot_general(
                columns[...], hidden[...], CONTRACT_ROWS, preferred_element_type=F32
            ).astype(BF)
            copies = []
            for p in WIDE_ALL:
                target = moved(**p)
                rows = part.at[span(target[0] * ROWS, ROWS)]
                copies.append(net.put(rows, landed.at[w], target))
            kept = net.keep(part.at[span(w * ROWS, ROWS)], landed.at[w])
            yield
            kept.wait()
            for copy in copies:
                copy.wait_recv()
            s = landed[0].astype(F32)
            for i in range(1, WIDE):
                s = s + landed[i].astype(F32)
            shard[...] = s.astype(BF)
            spot = mine.at[span(w * ROWS, ROWS)]
            copies = [net.put(shard, spot, moved(**p)) for p in WIDE_ALL]
            kept = net.keep(shard, spot)
            yield
            kept.wait()
            for copy in copies:
                copy.wait_recv()
            yield from gather_small(net, mine, table)

        moves = dict(
            gather=gather_narrow(net, d_attn_own, big),
            down=second_then_narrow(
                net, wide_down[0], block, wide_down[1:], [(0, units, 4 * D + FF)]
            ),
            up=wide_then_narrow(net, g_up, block, wide_up, [(0, units, 4 * D)]),
            mixed=wide_then_narrow(net, ga, block, wide_a, quarter),
            feed=reduce_narrow(net, ffn_part, ffn_sum, narrow),
            gates=router(),
            total=sums.steps(),
        )

        def wait_loads():
            first_load.wait()
            for load in loads:
                load.wait()
            dk[...] = jnp.zeros_like(dk)
            dv[...] = jnp.zeros_like(dv)

        def one_pair(dy):
            r = span(wrap(y + dy) * pair_rows, pair_rows)
            mask = branch_mask(mv[r, :], PICK_ATTN)
            back = jnp.dot(big[r, :], wv[:, 3 * head_part :], preferred_element_type=F32)
            back = (back * mask).astype(BF)
            for h in range(2):
                at = pl.ds(h * HEAD_DIM, HEAD_DIM)
                d_out = back[:, h * HEAD_DIM : (h + 1) * HEAD_DIM]
                d_probs = lax.dot_general(
                    d_out, vv[:, at], CONTRACT_COLS, preferred_element_type=F32
                )
                probs_low = pv[r, pl.ds(h * GROUP, GROUP)]
                probs = probs_low.astype(F32)
                weighted = probs * d_probs
                centre = jnp.sum(weighted, axis=-1, keepdims=True)
                ds = (weighted - probs * centre).astype(BF)
                dq = jnp.dot(ds, kv[:, at], preferred_element_type=F32) * scale
                dproj[r, at] = turn(dq, tv[0, r, :], -tv[1, r, :]).astype(BF)
                dk[:, at] += lax.dot_general(
                    ds, qv[r, at], CONTRACT_ROWS, preferred_element_type=F32
                )
                dv[:, at] += lax.dot_general(
                    probs_low, d_out, CONTRACT_ROWS, preferred_element_type=F32
                )

        refill = []

        def turn_back():
            refill.append(net.keep(normed, pv))

            @pl.loop(0, SIDE)
            def _(i):
                r = span(i * pair_rows, pair_rows)
                cosine, sine = tv[0, r, :], -tv[1, r, :]
                for h in range(2):
                    at = pl.ds(h * HEAD_DIM, HEAD_DIM)
                    to = pl.ds(head_part + h * HEAD_DIM, HEAD_DIM)
                    dproj[r, to] = turn(dk[r, at] * scale, cosine, sine).astype(BF)
                dproj[r, pl.ds(2 * head_part, head_part)] = dv[r, :].astype(BF)

        def gradient(left, right, start, width):
            @pl.loop(0, D // strip)
            def _(i):
                ga[span(i * strip, strip), pl.ds(start, width)] = lax.dot_general(
                    left[:, lanes(i * strip, strip)],
                    right[...],
                    CONTRACT_ROWS,
                    preferred_element_type=F32,
                ).astype(BF)

        def mixed_gradient():
            refill[0].wait()
            gradient(pv, dproj, 0, 3 * head_part)

        def norm_back(dy):
            r = span(wrap(y + dy) * pair_rows, pair_rows)
            back = lax.dot_general(
                dproj[r, :], wv[:, : 3 * head_part], CONTRACT_COLS, preferred_element_type=F32
            )
            sums.store(dy, back)
            sums.cross(dy)

        works = dict(
            LD=wait_loads,
            RT=turn_back,
            GO=functools.partial(gradient, big, av, 3 * head_part, head_part),
            GQ=mixed_gradient,
        )
        for dy in PAIR_ORDER:
            works[f"P{dy}"] = functools.partial(one_pair, dy)
            works[f"N{dy}"] = functools.partial(norm_back, dy)
        follow(BACKWARD_PLAN, works, moves)

    return comm_call(
        body,
        [d_attn_own, ffn_part, g_up, down_sums, normed, hidden_own] + list(kept),
        [
            jax.ShapeDtypeStruct((TOK, D), F32),
            jax.ShapeDtypeStruct((TOK, D), F32),
            jax.ShapeDtypeStruct((ROWS, 4 * D + 2 * FF), BF),
            jax.ShapeDtypeStruct((D, RH), BF),
        ],
        scratch,
        cid,
        GATHER_COPIES
        + 2 * REDUCE_COPIES
        + 2 * FIRST_COPIES
        + 3 * SECOND_COPIES
        + 6 * 7
        + 2 * (15 + GATHER_SMALL_COPIES),
        10 + 1 + 1 + 1 + REDUCE_LOCALS + 2 * FIRST_LOCALS + 6 + 4,
        "attention_backward",
    )


VECTOR_ROWS = 64
GAIN_ROWS = 2 * D // 128
SMALL_ROWS = GAIN_ROWS + RH * 2 * LEVELS // 128
SQUARE_ROWS = 8


def last_sums(vector, block, table, cid):
    def squares_of(ref, rows, cols):
        s = jnp.zeros((SQUARE_ROWS, 128), F32)
        for i in range(ref.shape[0] // rows):
            for j in range(ref.shape[1] // cols):
                piece = ref[i * rows : (i + 1) * rows, j * cols : (j + 1) * cols].astype(F32)
                piece = piece * piece
                for a in range(rows // SQUARE_ROWS):
                    for b in range(cols // 128):
                        s = s + piece[a * 8 : a * 8 + 8, b * 128 : b * 128 + 128]
        return s

    def body(net, ins, outs, scr):
        vec, block, table = ins
        vec_out, norm_out = outs
        own, first, second, total, held, full, norm = scr
        w = lax.axis_index("wide")
        n = lax.axis_index("narrow")
        loads = [net.keep(block, held), net.keep(vec, own), net.keep(table, full)]
        greet(NARROW_ALL + WIDE_ALL)
        loads[0].wait()
        squares = squares_of(held, ROWS, 2048)
        loads[1].wait()
        own[pl.ds(VECTOR_ROWS - SQUARE_ROWS, SQUARE_ROWS), :] = squares
        copies = [net.put(own, first.at[n], moved(**p)) for p in NARROW_ALL]
        mine = net.keep(own, first.at[n])
        loads[2].wait()
        squares = squares_of(full, 128, RH)
        mine.wait()
        for copy in copies:
            copy.wait_recv()
        s = first[0]
        for i in range(1, NARROW):
            s = s + first[i]
        total[0] = s
        copies = [net.put(total.at[0], second.at[w], moved(**p)) for p in WIDE_ALL]
        mine = net.keep(total.at[0], second.at[w])
        mine.wait()
        for copy in copies:
            copy.wait_recv()
        s = second[0]
        for i in range(1, WIDE):
            s = s + second[i]
        total[1] = s
        stores = [net.keep(total.at[1], vec_out)]
        small = s[:SMALL_ROWS]
        sum_all = jnp.sum(small * small) + jnp.sum(s[VECTOR_ROWS - SQUARE_ROWS :] + squares)
        norm[...] = jnp.sqrt(jnp.full((8, 128), sum_all, F32))
        stores.append(net.keep(norm, norm_out))
        for store in stores:
            store.wait()

    rows = VECTOR_ROWS
    return comm_call(
        body,
        [vector, block, table],
        [jax.ShapeDtypeStruct((rows, 128), F32), jax.ShapeDtypeStruct((8, 128), F32)],
        [
            pltpu.VMEM((rows, 128), F32),
            pltpu.VMEM((NARROW, rows, 128), F32),
            pltpu.VMEM((WIDE, rows, 128), F32),
            pltpu.VMEM((2, rows, 128), F32),
            pltpu.VMEM(block.shape, BF),
            pltpu.VMEM(table.shape, BF),
            pltpu.VMEM((8, 128), F32),
        ],
        cid,
        7 + 15,
        7,
        "last_sums",
    )


def adamw_step(master, moment_one, moment_two, grad, norm, tile):
    one_scale = 0.02 / (1.0 - 0.9**STEP)
    two_scale = 1.0 / (1.0 - 0.95**STEP)

    def kernel(w, m, v, g, n, new_w, new_m, new_v, *copy):
        clip = jnp.minimum(1.0, CLIP_NORM / n[0:1, 0:1])
        gradient = g[...].astype(F32) * clip
        one = 0.9 * m[...] + 0.1 * gradient
        two = 0.95 * v[...] + 0.05 * (gradient * gradient)
        new_m[...] = one
        new_v[...] = two
        root = jnp.sqrt(two * two_scale) + 1e-08
        updated = w[...] * (1.0 - 0.02 * 0.1) - (one * one_scale) / root
        new_w[...] = updated
        for ref in copy:
            ref[...] = updated.astype(BF)

    rows, cols = master.shape
    across = cols // tile[1]
    part = pl.BlockSpec(tile, lambda i: (i // across, i % across))
    shape = jax.ShapeDtypeStruct(master.shape, F32)
    low = jax.ShapeDtypeStruct(master.shape, BF)
    outs = [shape, shape, shape] + ([low] if rows == ROWS else [])
    return pl.pallas_call(
        kernel,
        grid=(rows * cols // (tile[0] * tile[1]),),
        out_shape=outs,
        in_specs=[part] * 4 + [pl.BlockSpec((8, 128), lambda i: (0, 0))],
        out_specs=[part] * len(outs),
        name="adamw_step",
    )(master, moment_one, moment_two, grad, norm)


def layer_norm(values, gain_row):
    average = jnp.mean(values, axis=-1, keepdims=True)
    centered = values - average
    spread = jnp.mean(centered * centered, axis=-1, keepdims=True)
    return centered * lax.rsqrt(spread + NORM_EPS) * gain_row


def segment_info(seg_lengths, token_index):
    seg_ends = jnp.cumsum(seg_lengths)
    segment = jnp.sum((token_index[:, None] >= seg_ends[None, :]).astype(jnp.int32), axis=1)
    starts = seg_ends - seg_lengths
    owners = segment[:, None] == jnp.arange(seg_lengths.shape[0], dtype=jnp.int32)[None, :]
    start_of = jnp.sum(jnp.where(owners, starts[None, :], 0), axis=1)
    return (segment, token_index - start_of)


def router_gates(logits, picks):
    levels = jnp.arange(LEVELS, dtype=jnp.int32)
    chosen_attn = (picks[:, 0:1] == levels[None, :]).astype(jnp.float32)
    chosen_ffn = (picks[:, 1:2] == levels[None, :]).astype(jnp.float32)
    gate_attn = float(LEVELS) * jnp.sum(
        jax.nn.softmax(logits[:, :LEVELS], axis=-1) * chosen_attn, axis=-1
    )
    gate_ffn = float(LEVELS) * jnp.sum(
        jax.nn.softmax(logits[:, LEVELS:], axis=-1) * chosen_ffn, axis=-1
    )
    return (gate_attn, gate_ffn)


def adamw(weight, moment_one, moment_two, gradient, step_rate):
    moment_one = 0.9 * moment_one + 0.1 * gradient
    moment_two = 0.95 * moment_two + 0.05 * gradient * gradient
    first_hat = moment_one / (1.0 - 0.9**STEP)
    second_hat = moment_two / (1.0 - 0.95**STEP)
    updated = weight - step_rate * (first_hat / (jnp.sqrt(second_hat) + 1e-08) + 0.1 * weight)
    return (updated, moment_one, moment_two)


def cut(rows, start, width, pieces):
    part = rows[:, start : start + width].reshape(rows.shape[0], pieces, width // pieces)
    return part.transpose(1, 0, 2)


def on_device(
    tokens,
    lengths,
    picks,
    cotangent,
    block_master,
    block_first,
    block_second,
    gains,
    gains_first,
    gains_second,
    router_in,
    router_in_first,
    router_in_second,
    router_out,
    router_out_first,
    router_out_second,
):
    low = block_master.astype(BF)
    source_a = jnp.concatenate([cut(low, i * D, D, NARROW) for i in range(4)], axis=2)
    source_b = jnp.concatenate([cut(low, 4 * D + i * FF, FF, NARROW) for i in range(2)], axis=2)
    inputs = tokens.astype(F32)
    norm_one, norm_one_back = jax.vjp(layer_norm, inputs, gains[0])
    normed_own = norm_one.astype(BF)
    hidden, hidden_back = jax.vjp(jax.nn.gelu, jnp.dot(normed_own.astype(F32), router_in))
    (gate_attn, gate_ffn), gates_back = jax.vjp(
        lambda logits: router_gates(logits, picks), jnp.dot(hidden, router_out)
    )
    upstream = cotangent.astype(F32)
    lane = jnp.arange(128)[None, :]
    marks = jnp.where(
        lane < PICK_FFN,
        picks[:, 0:1].astype(F32),
        jnp.where(lane < GATE_FFN, picks[:, 1:2].astype(F32), gate_ffn[:, None]),
    )

    key_index = jnp.arange(GROUP, dtype=jnp.int32)
    _, key_position = segment_info(lengths[0], key_index)
    half_dim = HEAD_DIM // 2
    frequency = 10000.0 ** (-jnp.arange(half_dim, dtype=F32) / half_dim)
    angles = key_position.astype(F32)[:, None] * frequency[None, :]
    cosine, sine = jnp.cos(angles), jnp.sin(angles)
    turns = jnp.stack(
        [
            jnp.concatenate([cosine, cosine], axis=1),
            jnp.concatenate([-sine, sine], axis=1),
        ]
    )
    first_length = jnp.broadcast_to(lengths[:, 0:1], (8, 128))
    (
        attn_out,
        query_low,
        key_low,
        value_low,
        probs_low,
        mixed_low,
        group_upstream,
        slab_a,
        slab_b,
        normed_low,
        group_marks,
    ) = attention_forward(
        normed_own, source_a, source_b, turns, first_length, marks, cotangent, 1
    )

    after_attn = inputs + gate_attn[:, None] * attn_out
    norm_two, norm_two_back = jax.vjp(layer_norm, after_attn, gains[1])

    d_norm_two, ffn_part, grad_up, down_sums, gate_rows = feed_forward(
        norm_two.astype(BF), group_upstream, slab_b, group_marks, 2
    )
    d_gate_ffn = gate_rows[0]
    d_after, d_gain_two = norm_two_back(d_norm_two)
    d_after = d_after + upstream
    d_gate_attn = jnp.sum(d_after * attn_out, axis=1)
    (d_logits,) = gates_back((d_gate_attn, d_gate_ffn))
    (d_hidden,) = hidden_back(lax.dot_general(d_logits, router_out, CONTRACT_COLS))
    d_normed, ffn_out, block_low, router_in_grad = attention_backward(
        (d_after * gate_attn[:, None]).astype(BF),
        ffn_part,
        grad_up,
        down_sums,
        normed_low,
        d_hidden.astype(BF),
        [slab_a, turns, group_marks, query_low, key_low, value_low, probs_low, mixed_low],
        3,
    )

    result = (after_attn + gate_ffn[:, None] * ffn_out).astype(BF)
    grad_router_out = lax.dot_general(hidden, d_logits, CONTRACT_ROWS)
    d_normed_router = lax.dot_general(d_hidden, router_in, CONTRACT_COLS)
    d_inputs, d_gain_one = norm_one_back(d_normed + d_normed_router)
    d_inputs = d_inputs + d_after

    levels = jnp.arange(LEVELS, dtype=jnp.int32)
    counts_local = [
        jnp.sum((picks[:, b : b + 1] == levels[None, :]).astype(F32), axis=0) for b in range(2)
    ]
    rest = jnp.zeros(((VECTOR_ROWS - SMALL_ROWS) * 128 - 2 * LEVELS,), F32)
    vector = jnp.concatenate(
        [d_gain_one, d_gain_two, grad_router_out.ravel(), *counts_local, rest]
    ).reshape(VECTOR_ROWS, 128)
    vector, norm = last_sums(vector, block_low, router_in_grad, 7)
    gain_grad = vector[:GAIN_ROWS].reshape(2, D)
    router_out_grad = vector[GAIN_ROWS:SMALL_ROWS].reshape(RH, 2 * LEVELS)
    counts = vector[SMALL_ROWS, : 2 * LEVELS].reshape(2, LEVELS)
    grad_norm = norm[0, 0]
    clip_factor = jnp.minimum(1.0, CLIP_NORM / grad_norm)
    new_block, new_block_first, new_block_second, block_copy = adamw_step(
        block_master, block_first, block_second, block_low, norm, (ROWS, 4096)
    )
    new_gains, new_gains_first, new_gains_second = adamw(
        gains, gains_first, gains_second, gain_grad * clip_factor, 0.6
    )
    new_router_in, new_router_in_first, new_router_in_second = adamw_step(
        router_in, router_in_first, router_in_second, router_in_grad, norm, (256, RH)
    )
    new_router_out, new_router_out_first, new_router_out_second = adamw(
        router_out, router_out_first, router_out_second, router_out_grad * clip_factor, 0.02
    )
    return (
        result,
        d_inputs,
        counts,
        grad_norm,
        new_block,
        new_block_first,
        new_block_second,
        block_copy,
        new_gains,
        new_gains_first,
        new_gains_second,
        new_router_in,
        new_router_in_first,
        new_router_in_second,
        new_router_out,
        new_router_out_first,
        new_router_out_second,
    )


def solution(mesh):
    both = P(("wide", "narrow"), None)
    return jax.shard_map(
        on_device,
        mesh=mesh,
        in_specs=(both, P("wide", None)) + (both,) * 5 + (P(),) * 9,
        out_specs=(both, both, P(), P()) + (both,) * 4 + (P(),) * 9,
        check_vma=False,
    )
```

time: 353 us -> 295 us (0.84)
  Pallas kernels: 284 us -> 254 us
  other arithmetic: 45.5 us -> 23.8 us
  between operations: 5.79 us -> 1.99 us
    pallas_call x7 -> x4, Pallas kernels: 284 us -> 238 us  [comm_call(): pl.pallas_call(kernel, out_shape=outs, in_specs=[pl.BlockSpec(memory_spac...]
    pallas_call x0 -> x2, Pallas kernels: none -> 15.3 us  [adamw_step(): pl.pallas_call(kernel, grid=(rows * cols // (tile[0] * tile[1]),), out_sh...]
    convert_element_type x5 -> x1, other arithmetic: 10.3 us -> 0.95 us  [on_device(): result = (after_attn + gate_ffn[:, None] * ffn_out).astype(BF)]
    sub x3 -> x2, other arithmetic: 8.54 us -> 1.31 us  [adamw(): weight - step_rate * (first_hat / (jnp.sqrt(second_hat) + 1e-08) + 0.1 *...]
    reduce_sum x5 -> x1, other arithmetic: 8.22 us -> 1.09 us  [on_device(): d_gate_attn = jnp.sum(d_after * attn_out, axis=1)]
where the time goes in v4:
time: 295 us; the launch traced here: 291 us
  Pallas kernels  254 us (86%)
  other arithmetic  23.8 us (8%)
  local copies, waits for them, and re-layouts  7.22 us (2%)
  matrix products  4.01 us (1%)
    pallas_call x4, Pallas kernels, comm_call(): pl.pallas_call(kernel, out_shape=outs, in_specs=[pl.BlockSpec(memory_spac...  238 us
    pallas_call x2, Pallas kernels, adamw_step(): pl.pallas_call(kernel, grid=(rows * cols // (tile[0] * tile[1]),), out_sh...  15.3 us

profile of v4, /device:TPU:1, one launch (start us, length us, event | category | flops | bytes accessed | tf_op | source)
XLA Modules:
  0.0 290.7 jit_solution(12709604769366110749)
XLA Ops:
  0.7 0.0 copy-start.4
  0.7 1.3 convert_reduce_fusion
  2.0 1.3 fusion.8
  3.4 0.8 fusion.55
  4.2 0.0 copy-start.23
  4.2 0.0 copy-start.9
  4.2 1.5 fusion.6.refs_0_
  5.7 0.0 copy-done.4
  5.8 0.0 copy-start.10
  5.8 0.3 fusion.56
  6.1 0.0 copy-done.20
  6.1 0.2 fusion.18
  6.3 0.1 fusion.31
  6.5 0.7 select_select_fusion.refs_5_
  7.2 0.1 convert_element_type.51
  7.4 0.7 pad_maximum_fusion.2.refs_1_
  8.1 0.0 copy-done.24
  8.1 0.2 reduce-window.4
  8.3 0.1 fusion.21
  8.4 0.1 fusion.22
  8.5 1.9 multiply_cosine_fusion
  10.4 0.3 maximum_bitcast_fusion
  10.8 1.0 pad_maximum_fusion.refs_3_.refs_7_
  11.9 0.0 copy-start.3
  11.9 0.8 pad_maximum_fusion.1.refs_2_
  12.7 0.6 broadcast_in_dim.120.refs_4_
  13.4 84.5 %attention_forward.1 = (f32[128,2048]{1,0:T(8,128)}, bf16[1024,256]{1,0:T(8,128)(2,1)}, bf16[1024,256]{1,0:T(8,128)(2,1)}, bf16[1024,256]{1,0:T(8,128)(2,1)}, bf...) custom-call(bf16[128,2048]{1,0:T(8,128)(2,1)} %copy-done.10, ...), custom_call_target="tpu_custom_call" | custom-call | tf_op jit(solution)/shard_map/attention_forward/pallas_call | solution.py:174
  97.9 1.5 fusion.52
  99.4 0.3 multiply_reduce_fusion.3
  99.7 0.7 copy-done
  100.4 1.0 multiply_convert_fusion.1.refs_0_
  101.4 56.2 %feed_forward.1 = (f32[128,2048]{1,0:T(8,128)}, bf16[1024,2048]{1,0:T(8,128)(2,1)}, bf16[2048,1024]{1,0:T(8,128)(2,1)}, bf16[2,4,64,1024]{3,2,1,0:T(8,128)(2,1)}, f32[8,128]{1,0:T(8,128)}) custom-call(bf16[128,2048]{1,0:T(8,128)(2,1)} %multiply_convert_fusion.1.refs_0_, bf16[1024,2048]{1,0:T(8,128)(2,1)} %get-tuple-element.47.refs_1_, ...), custom_call_target="tpu_custom_call" | custom-call | tf_op jit(solution)/shard_map/feed_forward/pallas_call | solution.py:174
  157.6 2.1 multiply_reduce_fusion
  159.7 0.0 copy-done.13
  159.7 0.4 fusion.51
  160.2 1.0 copy-done.5
  161.2 1.1 multiply_reduce_fusion.1
  162.3 0.7 multiply_bitcast_fusion
  163.0 0.1 fusion.28
  163.1 0.2 fusion.17
  163.4 0.1 reshape.192
  163.5 0.9 fusion.16.refs_5_
  164.4 78.3 %attention_backward.1 = (f32[128,2048]{1,0:T(8,128)}, f32[128,2048]{1,0:T(8,128)}, bf16[16,24576]{1,0:T(8,128)(2,1)}, bf16[2048,256]{1,0:T(8,128)(2,1)}) custom-call(bf16[128,2048]{1,0:T(8,128)(2,1)} %get-tuple-element.134.refs_0_, bf16[1024,2048]{1,0:T(8,128)(2,1)} %get-tuple-element.51.refs_1_, bf16[2048,1024]{1,0:T(8,128)(2,1)} %get-tuple-element.52.refs_2_, ...), custom_call_target="tpu_custom_call" | custom-call | tf_op jit(solution)/shard_map/attention_backward/pallas_call | solution.py:174
  242.7 2.4 fusion.9
  245.2 0.0 copy-start.7
  245.2 0.0 copy-start.21
  245.2 0.0 copy-start.22
  245.2 0.9 copy-done.7
  246.1 0.5 fusion.7
  246.7 0.7 concatenate.19
  247.4 19.4 %last_sums.1 = (f32[64,128]{1,0:T(8,128)}, f32[8,128]{1,0:T(8,128)}) custom-call(f32[64,128]{1,0:T(8,128)} %bitcast.77, bf16[16,24576]{1,0:T(8,128)(2,1)} %get-tuple-element.64.refs_1_.g, bf16[2048,256]{1,0:T(8,128)(2,1)} %get-tuple-element.65.refs_2_.g), custom_call_target="tpu_custom_call" | custom-call | tf_op jit(solution)/shard_map/last_sums/pallas_call | solution.py:174
  266.7 1.2 slice.73
  268.6 0.7 slice_multiply_fusion.1
  269.3 0.1 mul.442
  269.4 0.1 copy.83
  269.5 0.0 copy-done.21
  269.5 0.6 multiply_subtract_fusion.1
  270.1 8.4 %adamw_step.3 = (f32[2048,256]{1,0:T(8,128)}, f32[2048,256]{1,0:T(8,128)}, f32[2048,256]{1,0:T(8,128)}) custom-call(f32[2048,256]{1,0:T(8,128)} %w.3, f32[2048,256]{1,0:T(8,128)} %m.3, f32[2048,256]{1,0:T(8,128)} %v.3, bf16[2048,256]{1,0:T(8,128)(2,1)} %get-tuple-element.65.refs_2_.g, f32[8,128]{1,0:T(8,128)} %get-tuple-element.67.n), custom_call_target="tpu_custom_call" | custom-call | tf_op jit(solution)/shard_map/adamw_step/pallas_call | solution.py:1229
  278.6 0.7 multiply_subtract_fusion
  279.3 6.9 %adamw_step.2 = (f32[16,24576]{1,0:T(8,128)}, f32[16,24576]{1,0:T(8,128)}, f32[16,24576]{1,0:T(8,128)}, bf16[16,24576]{1,0:T(8,128)(2,1)}) custom-call(f32[16,24576]{1,0:T(8,128)} %w.2, f32[16,24576]{1,0:T(8,128)} %m.2, f32[16,24576]{1,0:T(8,128)} %v.2, bf16[16,24576]{1,0:T(8,128)(2,1)} %get-tuple-element.64.refs_1_.g, f32[8,128]{1,0:T(8,128)} %get-tuple-element.67.n), custom_call_target="tpu_custom_call" | custom-call | tf_op jit(solution)/shard_map/adamw_step/pallas_call | solution.py:1229
  286.2 0.6 reshape_squeeze.3
  286.9 0.0 copy-done.8
  286.9 2.7 add_add_fusion.2
  289.6 1.0 add_convert_fusion
  (63 shorter events, 0.4 us)
Async XLA Ops:
  0.7 5.1 %copy-start.4 = (f32[2048,256]{1,0:T(8,128)S(1)}, f32[2048,256]{1,0:T(8,128)}, u32[]{:S(2)}) copy-start(f32[2048,256]{1,0:T(8,128)} %w.3) | copy-start | bytes 6291460
  2.0 4.1 %copy-start.20 = (f32[256,8]{0,1:T(8,128)S(1)}, f32[256,8]{0,1:T(8,128)}, u32[]{:S(2)}) copy-start(f32[256,8]{0,1:T(8,128)} %param.29) | copy-start | bytes 24580
  4.2 2.1 copy-start.23
  4.2 3.0 %copy-start.9 = (f32[16,24576]{1,0:T(8,128)S(1)}, f32[16,24576]{1,0:T(8,128)}, u32[]{:S(2)}) copy-start(f32[16,24576]{1,0:T(8,128)} %w.2) | copy-start | bytes 4718596
  5.8 1.6 copy-start.10
  6.3 1.9 copy-start.24
  11.9 86.0 %copy-start.3 = (bf16[128,2048]{1,0:T(8,128)(2,1)S(1)}, bf16[128,2048]{1,0:T(8,128)(2,1)}, u32[]{:S(2)}) copy-start(bf16[128,2048]{1,0:T(8,128)(2,1)} %param.16) | copy-start | bytes 1572868
  99.4 1.0 copy-start
  157.6 2.1 copy-start.1
  157.6 2.2 copy-start.13
  159.7 1.5 copy-start.11
  159.7 1.5 copy-start.12
  160.1 1.1 copy-start.5
  164.3 78.4 %copy-start.15 = (bf16[128,256]{1,0:T(8,128)(2,1)S(1)}, bf16[128,256]{1,0:T(8,128)(2,1)}, u32[]{:S(2)}) copy-start(bf16[128,256]{1,0:T(8,128)(2,1)} %fusion.16.refs_5_) | copy-start | bytes 196612
  245.2 1.0 copy-start.7
  245.2 24.3 %copy-start.21 = (f32[256,8]{0,1:T(8,128)S(1)}, f32[256,8]{0,1:T(8,128)}, u32[]{:S(2)}) copy-start(f32[256,8]{0,1:T(8,128)} %param.30) | copy-start | bytes 24580
  245.2 24.3 %copy-start.22 = (f32[256,8]{0,1:T(8,128)S(1)}, f32[256,8]{0,1:T(8,128)}, u32[]{:S(2)}) copy-start(f32[256,8]{0,1:T(8,128)} %param.31) | copy-start | bytes 24580
  270.1 8.4 %copy-start.17 = (f32[64,128]{1,0:T(8,128)S(1)}, f32[64,128]{1,0:T(8,128)}, u32[]{:S(2)}) copy-start(f32[64,128]{1,0:T(8,128)} %get-tuple-element.66) | copy-start | bytes 98308
  270.1 8.5 %copy-start.16 = (f32[2,2048]{1,0:T(2,128)S(1)}, f32[2,2048]{1,0:T(2,128)}, u32[]{:S(2)}) copy-start(f32[2,2048]{1,0:T(2,128)} %param.23) | copy-start | bytes 49156
  270.1 8.5 %copy-start.18 = (f32[2,2048]{1,0:T(2,128)S(1)}, f32[2,2048]{1,0:T(2,128)}, u32[]{:S(2)}) copy-start(f32[2,2048]{1,0:T(2,128)} %param.24) | copy-start | bytes 49156
  270.1 8.5 %copy-start.19 = (f32[2,2048]{1,0:T(2,128)S(1)}, f32[2,2048]{1,0:T(2,128)}, u32[]{:S(2)}) copy-start(f32[2,2048]{1,0:T(2,128)} %param.25) | copy-start | bytes 49156
  279.3 7.6 %copy-start.6 = (f32[128,2048]{1,0:T(8,128)S(1)}, f32[128,2048]{1,0:T(8,128)}, u32[]{:S(2)}) copy-start(f32[128,2048]{1,0:T(8,128)} %copy-done.5) | copy-start | bytes 3145732
  279.3 7.6 %copy-start.8 = (f32[128,2048]{1,0:T(8,128)S(1)}, f32[128,2048]{1,0:T(8,128)}, u32[]{:S(2)}) copy-start(f32[128,2048]{1,0:T(8,128)} %copy-done.7) | copy-start | bytes 3145732
  286.9 2.7 copy-start.2
  286.9 2.7 copy-start.14
